TPU v7x, 512 devices: a whole 4x8x8 slice. The times are simulated.
512 devices in a mesh: lon: 16 (over x_lo, z), lat: 16 (over y, core), dp: 2 (over x_hi).
Axes of the slice: x: 4 (x_hi: 2, x_lo: 2; x = x_hi * 2 + x_lo), y: 8, z: 8, core: 2. Of those that a mesh axis runs over, the one named last changes fastest.
Arguments:
- output_first: bfloat16 [2, 4, 96, 192, 192], P('dp', None, 'lat', 'lon'), may hold values from -6 to 6
- output_second: bfloat16 [2, 4, 96, 192, 192], P('dp', None, 'lat', 'lon')
- cotangent_first: bfloat16 [2, 4, 96, 192, 192], P('dp', None, 'lat', 'lon'), may hold values from -6 to 6
- cotangent_second: bfloat16 [2, 4, 96, 192, 192], P('dp', None, 'lat', 'lon'), may hold values from -6 to 6
- norm_gain: float32 [192], replicated, may hold values from 0.5 to 1.5
- w_qkv: bfloat16 [192, 576], replicated, may hold values from -0.4375 to 0.4375
- w_proj: bfloat16 [192, 192], replicated, may hold values from -0.4375 to 0.4375
- earth_bias: float32 [2, 16, 6, 3312], P(None, 'lat'), may hold values from -4 to 300
- shifts: int32 [2], replicated, may hold values from 1 to 6, as said below
- region: int32 [96, 192], replicated, may hold values from 0 to 1, as said below
Outputs:
- input_first: bfloat16 [2, 4, 96, 192, 192], P('dp', None, 'lat', 'lon')
- grad_second: bfloat16 [2, 4, 96, 192, 192], P('dp', None, 'lat', 'lon')
- bias_grad: float32 [2, 16, 6, 3312], P(None, 'lat')
Inputs may be any that keep to these rules, and one draw needn't show every extreme that they name: shifts[0] is the latitude offset, from 1 to 5; shifts[1] is the longitude offset and equals 6. region is 1 on the framed rows r >= 96 - shifts[0], whose cells came round from the other edge of the latitude range, and 0 on all other rows; it does not vary with longitude.
All inputs are finite; a program needn't handle non-finite values.
Results may differ from a plain program's by a relative error of at most 0.012.
Values may be sent and summed in bfloat16 or wider, within the bound.
No kernel may reach another device: no remote copies, remote signals or barrier semaphores. Data moves between devices by JAX's collectives and lax.ppermute only.
A program may use at most 128 MiB of HBM per device.

v0:
```python
import jax
import jax.numpy as jnp
from jax import lax
from jax.sharding import PartitionSpec as P

HEADS = 6
WZ = 2
WL = 6
WC = 12
WT = 144
POS = 3312


norm_eps = 1e-05
mask_fill = -1e30


def from_behind(x, axis, by):
    peers = lax.axis_size(axis)
    return lax.ppermute(x, axis, [(i, (i + by) % peers) for i in range(peers)])


def layer_norm(values):
    as_float = values.astype(jnp.float32)
    centered = as_float - jnp.mean(as_float, axis=-1, keepdims=True)
    inverse = lax.rsqrt(jnp.mean(centered * centered, axis=-1, keepdims=True) + norm_eps)
    return (centered * inverse, inverse)


def norm_backward(normed, inverse, norm_gain, upstream):
    scaled = upstream * norm_gain
    return inverse * (
        scaled
        - jnp.mean(scaled, axis=-1, keepdims=True)
        - normed * jnp.mean(scaled * normed, axis=-1, keepdims=True)
    )


def offset_table(span_width):
    starts = jnp.arange(span_width)[:, None]
    finish = jnp.arange(span_width)[None, :]
    offsets = (finish - starts + span_width - 1).reshape(span_width * span_width)
    return (offsets[:, None] == jnp.arange(2 * span_width - 1)[None, :]).astype(jnp.float32)


def expand_bias(bias_table):
    leading = bias_table.shape[:-1]
    ndim_lead = len(leading)
    combos = bias_table.reshape(leading + (WZ * WZ * WL * WL, 2 * WC - 1))
    spread = jnp.einsum(
        "...pd,qd->...pq", combos, offset_table(WC), precision=lax.Precision.HIGHEST
    )
    spread = spread.reshape(leading + (WZ, WZ, WL, WL, WC, WC))
    axis_order = tuple(range(ndim_lead)) + tuple(
        (ndim_lead + position for position in (0, 2, 4, 1, 3, 5))
    )
    return spread.transpose(axis_order).reshape(leading + (WT, WT))


def compress_bias(score_grad):
    leading = score_grad.shape[:-2]
    ndim_lead = len(leading)
    unpacked = score_grad.reshape(leading + (WZ, WL, WC, WZ, WL, WC))
    axis_order = tuple(range(ndim_lead)) + tuple(
        (ndim_lead + position for position in (0, 3, 1, 4, 2, 5))
    )
    paired = unpacked.transpose(axis_order).reshape(leading + (WZ * WZ * WL * WL, WC * WC))
    folded = jnp.einsum(
        "...pq,qd->...pd", paired, offset_table(WC), precision=lax.Precision.HIGHEST
    )
    return folded.reshape(leading + (POS,))


def to_groups(volume):
    samples, levels, lat_size, lon_size, features = volume.shape
    unpacked = volume.reshape(
        samples, levels // WZ, WZ, lat_size // WL, WL, lon_size // WC, WC, features
    )
    grouped = unpacked.transpose(0, 3, 1, 5, 2, 4, 6, 7)
    return grouped.reshape(
        samples * (lat_size // WL) * (levels // WZ) * (lon_size // WC), WT, features
    )


def from_groups(grouped, shape_out):
    samples, levels, lat_size, lon_size, features = shape_out
    unpacked = grouped.reshape(
        samples, lat_size // WL, levels // WZ, lon_size // WC, WZ, WL, WC, features
    )
    return unpacked.transpose(0, 2, 4, 1, 5, 3, 6, 7).reshape(shape_out)


def region_windows(id_block):
    lat_size, lon_size = id_block.shape
    unpacked = id_block.reshape(lat_size // WL, WL, lon_size // WC, WC).transpose(0, 2, 1, 3)
    spread = jnp.broadcast_to(unpacked[:, :, None], (lat_size // WL, lon_size // WC, WZ, WL, WC))
    return spread.reshape(lat_size // WL, lon_size // WC, WT)


def into_frame(volume, lat_shift, lon_shift):
    lon_rim = from_behind(volume, "lon", -1)
    widened = jnp.concatenate((volume, lon_rim), axis=3)
    lat_rim = from_behind(widened, "lat", -1)
    extended = jnp.concatenate((widened, lat_rim), axis=2)
    return lax.dynamic_slice(extended, (0, 0, lat_shift, lon_shift, 0), volume.shape)


def leave_frame(volume, lat_shift, lon_shift, move_lon, move_lat):
    lon_rim = move_lon(volume)
    widened = jnp.concatenate((lon_rim, volume), axis=3)
    lat_rim = move_lat(widened)
    extended = jnp.concatenate((lat_rim, widened), axis=2)
    return lax.dynamic_slice(extended, (0, 0, WL - lat_shift, WC - lon_shift, 0), volume.shape)


def attend(win_input, win_upstream, w_qkv, bias_full, allowed):
    win_count = win_input.shape[0]
    head_dim = win_input.shape[2] // HEADS
    score_scale = head_dim ** (-0.5)
    packed = jnp.einsum("ntc,cf->ntf", win_input, w_qkv, preferred_element_type=jnp.float32).astype(
        jnp.bfloat16
    )
    packed = packed.reshape(win_count, WT, 3, HEADS, head_dim)
    queries = packed[:, :, 0]
    key_rows = packed[:, :, 1]
    value_rows = packed[:, :, 2]
    scores = (
        jnp.einsum("nihd,njhd->nhij", queries, key_rows, preferred_element_type=jnp.float32)
        * score_scale
        + bias_full
    )
    scores = jnp.where(allowed[:, None], scores, mask_fill)
    largest = jnp.max(scores, axis=-1, keepdims=True)
    exponent = jnp.exp(scores - largest)
    weights = exponent / jnp.sum(exponent, axis=-1, keepdims=True)
    weights_low = weights.astype(jnp.bfloat16)
    attended = jnp.einsum(
        "nhij,njhd->nihd", weights_low, value_rows, preferred_element_type=jnp.float32
    ).astype(jnp.bfloat16)
    upstream = win_upstream.reshape(win_count, WT, HEADS, head_dim)
    grad_weights = jnp.einsum(
        "nihd,njhd->nhij", upstream, value_rows, preferred_element_type=jnp.float32
    )
    row_dot = jnp.einsum("nihd,nihd->nhi", upstream, attended, preferred_element_type=jnp.float32)
    grad_scores = weights * (grad_weights - row_dot[..., None])
    grad_low = grad_scores.astype(jnp.bfloat16)
    grad_query = (
        jnp.einsum("nhij,njhd->nihd", grad_low, key_rows, preferred_element_type=jnp.float32)
        * score_scale
    )
    grad_key = (
        jnp.einsum("nhij,nihd->njhd", grad_low, queries, preferred_element_type=jnp.float32)
        * score_scale
    )
    grad_value = jnp.einsum(
        "nhij,nihd->njhd", weights_low, upstream, preferred_element_type=jnp.float32
    )
    coeffs = jnp.stack((grad_query, grad_key, grad_value), axis=2).astype(jnp.bfloat16)
    coeffs = coeffs.reshape(win_count, WT, 3 * HEADS * head_dim)
    return (attended.reshape(win_count, WT, HEADS * head_dim), coeffs, grad_scores)


def local(
    output_first,
    output_second,
    cotangent_first,
    cotangent_second,
    norm_gain,
    w_qkv,
    w_proj,
    earth_bias,
    shifts,
    region,
):
    normed, inverse = layer_norm(output_second)
    hidden = (normed * norm_gain).astype(jnp.bfloat16)
    volume_shape = hidden.shape
    upstream = jnp.einsum(
        "szabf,cf->szabc", cotangent_first, w_proj, preferred_element_type=jnp.float32
    ).astype(jnp.bfloat16)
    lat_shift = shifts[0]
    lon_shift = shifts[1]
    framed_hidden = into_frame(hidden, lat_shift, lon_shift)
    framed_up = into_frame(upstream, lat_shift, lon_shift)
    lat_rows = volume_shape[2]
    lon_cols = volume_shape[3]
    lat_wins = lat_rows // WL
    lon_wins = lon_cols // WC
    level_wins = volume_shape[1] // WZ
    id_block = lax.dynamic_slice(
        region,
        (lax.axis_index("lat") * lat_rows, lax.axis_index("lon") * lon_cols),
        (lat_rows, lon_cols),
    )
    region_ids = region_windows(id_block)
    allowed_local = region_ids[..., :, None] == region_ids[..., None, :]
    allowed = jnp.broadcast_to(
        allowed_local[:, None], (lat_wins, level_wins, lon_wins, WT, WT)
    ).reshape(-1, WT, WT)
    bias_local = expand_bias(earth_bias).transpose(1, 0, 2, 3, 4)
    bias_full = bias_local[:, :, None]
    bias_full = bias_full.reshape(-1, HEADS, WT, WT)
    attended, coeffs, grad_scores = attend(
        to_groups(framed_hidden), to_groups(framed_up), w_qkv, bias_full, allowed
    )
    attended_home = leave_frame(
        from_groups(attended, volume_shape),
        lat_shift,
        lon_shift,
        lambda section: from_behind(section, "lon", 1),
        lambda section: from_behind(section, "lat", 1),
    )
    mixed_out = jnp.einsum(
        "szabc,cf->szabf", attended_home, w_proj, preferred_element_type=jnp.float32
    )
    input_first = (output_first.astype(jnp.float32) - mixed_out).astype(jnp.bfloat16)
    coeff_shape = volume_shape[:4] + (coeffs.shape[-1],)
    coeff_home = leave_frame(
        from_groups(coeffs, coeff_shape),
        lat_shift,
        lon_shift,
        lambda section: from_behind(section, "lon", 1),
        lambda section: from_behind(section, "lat", 1),
    )
    grad_low_home = jnp.einsum(
        "szabf,cf->szabc", coeff_home, w_qkv, preferred_element_type=jnp.float32
    ).astype(jnp.bfloat16)
    feature_grad = lax.optimization_barrier(grad_low_home).astype(jnp.float32)
    grad_second = (
        cotangent_second.astype(jnp.float32)
        + norm_backward(normed, inverse, norm_gain, feature_grad)
    ).astype(jnp.bfloat16)
    bias_parts = (
        grad_scores.reshape(lat_wins, level_wins, lon_wins, HEADS, WT, WT)
        .sum(axis=2)
        .transpose(1, 0, 2, 3, 4)
    )
    bias_grad = lax.psum(compress_bias(bias_parts), ("lon", "dp"))
    return (input_first, grad_second, bias_grad)


def solution(mesh):
    return jax.shard_map(
        local,
        mesh=mesh,
        in_specs=(
            P("dp", None, "lat", "lon", None),
            P("dp", None, "lat", "lon", None),
            P("dp", None, "lat", "lon", None),
            P("dp", None, "lat", "lon", None),
            P(),
            P(),
            P(),
            P(None, "lat", None, None),
            P(),
            P(),
        ),
        out_specs=(
            P("dp", None, "lat", "lon", None),
            P("dp", None, "lat", "lon", None),
            P(None, "lat", None, None),
        ),
        check_vma=False,
    )
```

profile of v0, /device:TPU:8, one launch (start us, length us, event | category | flops | bytes accessed | tf_op | source)
XLA Modules:
  0.0 312.3 jit_solution(1830501027580533090)
XLA Ops:
  7.2 1.3 fusion.7
  8.5 11.9 %collective-permute-start.4 = (bf16[1,4,6,12,192]{4,3,2,1,0:T(8,128)(2,1)S(1)}, bf16[1,4,6,12,192]{4,3,2,1,0:T(8,128)(2,1)S(1)}, u32[]{:S(2)}, u32[]{:S(2)}) collective-permute-start(bf16[1,4,6,12,192]{4,3,2,1,0:T(8,128)(2,1)S(1)} %fusion.7), channel_id=1, source_target_pairs={{0,480},{32,0},{64,32},{96,64},{128,96},{160,128},{192,160},{224,1... | collective-permute-start | bytes 331784 | tf_op jit(solution)/shard_map/ppermute | solution.py:20
  20.4 1.0 convert_reduce_fusion
  21.4 1.1 fusion.29
  22.6 1.1 fusion.23
  23.7 2.5 collective-permute-start
  26.2 1.3 reduce.5
  27.5 0.7 reshape.206
  28.2 8.9 %convolution_bitcast_fusion = f32[2,1,6,2,6,12,2,6,12]{8,7,4,6,3,2,0,5,1:T(8,128)} fusion(f32[2,6,2,2,6,6,23,1]{6,5,4,3,2,1,0,7:T(8,128)S(1)} %reshape.206, s32[12,12]{1,0:T(8,128)S(1)} %subtract_add_fusion), kind=kOutput, calls=%fused_computation.1 | convolution fusion | flops 68680944 | bytes 1154880 | tf_op jit(solution)/shard_map/...pd,qd->...pq/dot_general | solution.py:50
  37.1 20.7 %copy.73 = f32[2,1,6,2,6,12,2,6,12]{5,4,3,8,7,6,2,0,1:T(8,128)} copy(f32[2,1,6,2,6,12,2,6,12]{8,7,4,6,3,2,0,5,1:T(8,128)} %convolution_bitcast_fusion) | data formatting | bytes 1990656 | tf_op jit(solution)/shard_map/reshape;broadcast_in_dim;transpose;reshape | solution.py:202
  57.8 10.3 %reshape.215 = f32[2,6,144,144]{2,3,1,0:T(8,128)} reshape(f32[2,1,6,2,6,12,2,6,12]{5,4,3,8,7,6,2,0,1:T(8,128)} %copy.73) | data formatting | bytes 1990656 | tf_op jit(solution)/shard_map/reshape;broadcast_in_dim;transpose;reshape | solution.py:202
  68.0 0.6 fusion.56
  69.9 0.8 dynamic_slice.16
  73.7 0.6 collective-permute-start.1
  74.3 3.5 %collective-permute-done.5 = bf16[1,4,6,24,192]{4,3,2,1,0:T(8,128)(2,1)S(1)} collective-permute-done((bf16[1,4,6,24,192]{4,3,2,1,0:T(8,128)(2,1)S(1)}, bf16[1,4,6,24,192]{4,3,2,1,0:T(8,128)(2,1)S(1)}, u32[]{:S(2)}, u32[]{:S(2)}) %collective-permute-start.5) | collective-permute-done | bytes 221216 | tf_op jit(solution)/shard_map/ppermute | solution.py:20
  77.8 3.2 %collective-permute-done.1 = bf16[1,4,6,24,192]{4,3,2,1,0:T(8,128)(2,1)S(1)} collective-permute-done((bf16[1,4,6,24,192]{4,3,2,1,0:T(8,128)(2,1)S(1)}, bf16[1,4,6,24,192]{4,3,2,1,0:T(8,128)(2,1)S(1)}, u32[]{:S(2)}, u32[]{:S(2)}) %collective-permute-start.1) | collective-permute-done | bytes 221216 | tf_op jit(solution)/shard_map/ppermute | solution.py:20
  80.9 0.6 fusion.34
  81.5 0.3 reshape_reshape_transpose_reshape.3
  81.8 1.0 copy.43
  83.3 1.1 copy.31
  84.4 2.5 fusion.57
  87.1 1.5 convolution_convert_fusion.4
  88.7 1.1 fusion.5
  89.7 0.4 copy.65
  90.3 2.2 subtract_multiply_fusion
  92.5 0.4 fusion.8
  93.6 1.9 copy.49
  95.4 2.4 convert_element_type.73
  97.8 3.6 %collective-permute-start.6 = (bf16[1,4,6,12,576]{4,3,2,1,0:T(8,128)(2,1)S(1)}, bf16[1,4,6,12,576]{4,3,2,1,0:T(8,128)(2,1)}, u32[]{:S(2)}, u32[]{:S(2)}) collective-permute-start(bf16[1,4,6,12,576]{4,3,2,1,0:T(8,128)(2,1)S(1)} %convert_element_type.73), channel_id=1, source_target_pairs={{0,32},{32,64},{64,96},{96,128},{128,160},{160,192},{192,224},{224... | collective-permute-start | bytes 995336 | tf_op jit(solution)/shard_map/ppermute | solution.py:20
  101.4 0.3 copy.40
  101.7 0.4 reshape_transpose_reshape_reshape.4
  102.1 1.9 collective-permute-start.2
  104.1 2.0 copy.50
  106.1 10.1 %reshape_transpose.3 = f32[2,1,6,2,6,12,2,6,12]{8,7,6,5,4,3,2,0,1:T(8,128)} reshape(f32[2,6,144,144]{3,2,1,0:T(8,128)} %copy.50) | data formatting | bytes 1990656 | tf_op jit(solution)/shard_map/reshape;transpose | solution.py:63
  116.2 14.1 %copy.74 = f32[2,1,6,2,2,6,6,12,12]{8,7,6,5,4,3,0,2,1:T(8,128)} copy(f32[2,1,6,2,2,6,6,12,12]{8,6,4,7,5,3,2,0,1:T(8,128)} %bitcast.109) | data formatting | bytes 1990656 | tf_op jit(solution)/shard_map/reshape.32
  130.3 9.3 %reshape.216 = f32[2,6,144,144]{3,2,0,1:T(8,128)S(1)} reshape(f32[2,1,6,2,2,6,6,12,12]{8,7,6,5,4,3,0,2,1:T(8,128)} %copy.74) | data formatting | bytes 1990656 | tf_op jit(solution)/shard_map/reshape.32
  139.6 0.8 pad_maximum_fusion.3
  140.4 1.6 collective-permute-start.3
  142.0 2.1 pad_maximum_fusion
  144.2 1.0 fusion.49
  145.2 1.2 reshape.203
  149.0 148.9 %all-reduce.2.cloned.1.call-done = f32[2,1,6,3312]{3,0,2,1:T(2,128)} async-done(((f32[2,1,6,3312]{3,0,2,1:T(2,128)}), f32[2,1,6,3312]{3,0,2,1:T(2,128)}) %all-reduce.2.cloned.1.call-update) | async-done | bytes 158992 | tf_op jit(solution)/shard_map/psum | solution.py:238
  298.0 1.7 copy.55
  299.7 1.6 fusion.2
  301.3 0.8 copy.53
  302.1 1.9 fusion.6
  304.1 0.3 fusion.30
  304.7 0.8 copy.54
  (57 shorter events, 2.4 us)
Async XLA Ops:
  7.2 75.8 %copy-start = (bf16[192,576]{1,0:T(8,128)(2,1)S(1)}, bf16[192,576]{1,0:T(8,128)(2,1)}, u32[]{:S(2)}) copy-start(bf16[192,576]{1,0:T(8,128)(2,1)} %param.15) | copy-start | bytes 663556
  7.2 290.8 %all-reduce.2.cloned.1.call-start = ((), (), s32[]{:S(2)}) async-start(), calls=%async_computation | async-start | bytes 319488 | tf_op jit(solution)/shard_map/psum | solution.py:238
  8.5 64.9 %collective-permute-start.4 = (bf16[1,4,6,12,192]{4,3,2,1,0:T(8,128)(2,1)S(1)}, bf16[1,4,6,12,192]{4,3,2,1,0:T(8,128)(2,1)S(1)}, u32[]{:S(2)}, u32[]{:S(2)}) collective-permute-start(bf16[1,4,6,12,192]{4,3,2,1,0:T(8,128)(2,1)S(1)} %fusion.7), channel_id=1, source_target_pairs={{0,480},{32,0},{64,32},{96,64},{128,96},{160,128},{192,160},{224,1... | collective-permute-start | bytes 331784 | tf_op jit(solution)/shard_map/ppermute | solution.py:20
  23.7 49.9 %collective-permute-start = (bf16[1,4,6,12,192]{4,3,2,1,0:T(8,128)(2,1)S(1)}, bf16[1,4,6,12,192]{4,3,2,1,0:T(8,128)(2,1)S(1)}, u32[]{:S(2)}, u32[]{:S(2)}) collective-permute-start(bf16[1,4,6,12,192]{4,3,2,1,0:T(8,128)(2,1)S(1)} %fusion.23), channel_id=1, source_target_pairs={{0,480},{32,0},{64,32},{96,64},{128,96},{160,128},{192,160},{224,1... | collective-permute-start | bytes 331784 | tf_op jit(solution)/shard_map/ppermute | solution.py:20
  57.8 10.3 %copy-start.13 = (s32[2]{0:T(128)S(1)}, s32[2]{0:T(128)}, u32[]{:S(2)}) copy-start(s32[2]{0:T(128)} %param.18) | copy-start | bytes 28
  73.5 4.3 %collective-permute-start.5 = (bf16[1,4,6,24,192]{4,3,2,1,0:T(8,128)(2,1)S(1)}, bf16[1,4,6,24,192]{4,3,2,1,0:T(8,128)(2,1)S(1)}, u32[]{:S(2)}, u32[]{:S(2)}) collective-permute-start(bf16[1,4,6,24,192]{4,3,2,1,0:T(8,128)(2,1)S(1)} %pad_maximum_fusion.4), channel_id=1, source_target_pairs={{0,30},{2,0},{4,2},{6,4},{8,6},{10,8},{12,10},{14,12},{16,14},{18,... | collective-permute-start | bytes 663560 | tf_op jit(solution)/shard_map/ppermute | solution.py:20
  73.7 7.3 %collective-permute-start.1 = (bf16[1,4,6,24,192]{4,3,2,1,0:T(8,128)(2,1)S(1)}, bf16[1,4,6,24,192]{4,3,2,1,0:T(8,128)(2,1)S(1)}, u32[]{:S(2)}, u32[]{:S(2)}) collective-permute-start(bf16[1,4,6,24,192]{4,3,2,1,0:T(8,128)(2,1)S(1)} %pad_maximum_fusion.2), channel_id=1, source_target_pairs={{0,30},{2,0},{4,2},{6,4},{8,6},{10,8},{12,10},{14,12},{16,14},{18,... | collective-permute-start | bytes 663560 | tf_op jit(solution)/shard_map/ppermute | solution.py:20
  86.9 1.7 copy-start.1
  86.9 1.7 copy-start.7
  88.7 3.8 %copy-start.4 = (bf16[2,6,32,144]{3,2,1,0:T(8,128)(2,1)}, bf16[2,6,32,144]{3,2,1,0:T(8,128)(2,1)S(1)}, u32[]{:S(2)}) copy-start(bf16[2,6,32,144]{3,2,1,0:T(8,128)(2,1)S(1)} %convolution_convert_fusion.4) | copy-start | bytes 331780
  90.3 2.2 copy-start.2
  92.5 0.9 copy-start.6
  93.6 7.8 %copy-start.5 = (bf16[2,6,32,144]{3,2,1,0:T(8,128)(2,1)S(1)}, bf16[2,6,32,144]{3,2,1,0:T(8,128)(2,1)}, u32[]{:S(2)}) copy-start(bf16[2,6,32,144]{3,2,1,0:T(8,128)(2,1)} %copy-done.4) | copy-start | bytes 331780
  97.8 44.2 %collective-permute-start.6 = (bf16[1,4,6,12,576]{4,3,2,1,0:T(8,128)(2,1)S(1)}, bf16[1,4,6,12,576]{4,3,2,1,0:T(8,128)(2,1)}, u32[]{:S(2)}, u32[]{:S(2)}) collective-permute-start(bf16[1,4,6,12,576]{4,3,2,1,0:T(8,128)(2,1)S(1)} %convert_element_type.73), channel_id=1, source_target_pairs={{0,32},{32,64},{64,96},{96,128},{128,160},{160,192},{192,224},{224... | collective-permute-start | bytes 995336 | tf_op jit(solution)/shard_map/ppermute | solution.py:20
  102.1 37.5 %copy-start.8 = (bf16[1,4,6,12,192]{4,3,2,1,0:T(8,128)(2,1)}, bf16[1,4,6,12,192]{4,3,2,1,0:T(8,128)(2,1)S(1)}, u32[]{:S(2)}) copy-start(bf16[1,4,6,12,192]{4,3,2,1,0:T(8,128)(2,1)S(1)} %reshape_transpose_reshape_reshape.4) | copy-start | bytes 331780
  102.1 37.5 %collective-permute-start.2 = (bf16[1,4,6,12,192]{4,3,2,1,0:T(8,128)(2,1)S(1)}, bf16[1,4,6,12,192]{4,3,2,1,0:T(8,128)(2,1)S(1)}, u32[]{:S(2)}, u32[]{:S(2)}) collective-permute-start(bf16[1,4,6,12,192]{4,3,2,1,0:T(8,128)(2,1)S(1)} %reshape_transpose_reshape_reshape.4), channel_id=1, source_target_pairs={{0,32},{32,64},{64,96},{96,128},{128,160},{160,192},{192,224},{224... | collective-permute-start | bytes 331784 | tf_op jit(solution)/shard_map/ppermute | solution.py:20
  139.6 4.5 %copy-start.9 = (bf16[1,4,6,12,192]{4,3,2,1,0:T(8,128)(2,1)}, bf16[1,4,6,12,192]{4,3,2,1,0:T(8,128)(2,1)S(1)}, u32[]{:S(2)}) copy-start(bf16[1,4,6,12,192]{4,3,2,1,0:T(8,128)(2,1)S(1)} %collective-permute-done.2) | copy-start | bytes 331780
  140.4 159.3 %collective-permute-start.3 = (bf16[1,4,6,24,192]{4,3,2,1,0:T(8,128)(2,1)}, bf16[1,4,6,24,192]{4,3,2,1,0:T(8,128)(2,1)}, u32[]{:S(2)}, u32[]{:S(2)}) collective-permute-start(bf16[1,4,6,24,192]{4,3,2,1,0:T(8,128)(2,1)} %pad_maximum_fusion.3), channel_id=1, source_target_pairs={{0,2},{2,4},{4,6},{6,8},{8,10},{10,12},{12,14},{14,16},{16,18},{18... | collective-permute-start | bytes 663560 | tf_op jit(solution)/shard_map/ppermute | solution.py:20
  144.1 155.6 %copy-start.11 = (bf16[192,192]{1,0:T(8,128)(2,1)S(1)}, bf16[192,192]{1,0:T(8,128)(2,1)}, u32[]{:S(2)}) copy-start(bf16[192,192]{1,0:T(8,128)(2,1)} %param.16) | copy-start | bytes 221188
  144.1 158.0 %collective-permute-start.7 = (bf16[1,4,6,24,576]{4,3,2,1,0:T(8,128)(2,1)}, bf16[1,4,6,24,576]{4,3,2,1,0:T(8,128)(2,1)}, u32[]{:S(2)}, u32[]{:S(2)}) collective-permute-start(bf16[1,4,6,24,576]{4,3,2,1,0:T(8,128)(2,1)} %pad_maximum_fusion), channel_id=1, source_target_pairs={{0,2},{2,4},{4,6},{6,8},{8,10},{10,12},{12,14},{14,16},{16,18},{18... | collective-permute-start | bytes 1990664 | tf_op jit(solution)/shard_map/ppermute | solution.py:20
  299.7 4.3 %copy-start.3 = (bf16[1,4,6,12,192]{4,1,3,2,0:T(4,128)(2,1)S(1)}, bf16[1,4,6,12,192]{4,1,3,2,0:T(4,128)(2,1)}, u32[]{:S(2)}) copy-start(bf16[1,4,6,12,192]{4,1,3,2,0:T(4,128)(2,1)} %param.11) | copy-start | bytes 331780
  299.7 4.3 %copy-start.12 = (f32[192]{0:T(256)S(1)}, f32[192]{0:T(256)}, u32[]{:S(2)}) copy-start(f32[192]{0:T(256)} %param.14) | copy-start | bytes 2308
  301.3 3.1 copy-start.10
Sparse Core Ops, SparseCore 0:
  146.6 151.3 all-reduce.1
where the time goes:
time: 314 us; the launch traced here: 312 us
  waiting for transfers between devices  156 us (50%)
  local copies, waits for them, and re-layouts  81.3 us (26%)
  matrix products  22.8 us (7%)
  starting transfers between devices  22.1 us (7%)
  between operations  21 us (7%)
  other arithmetic  9.54 us (3%)
    psum x1, waiting for transfers between devices, local(): bias_grad = lax.psum(compress_bias(bias_parts), ('lon', 'dp'))  149 us
    another operation x2, local copies, waits for them, and re-layouts, local(): bias_full = bias_full.reshape(-1, HEADS, WT, WT)  30.9 us
    another operation x3, local copies, waits for them, and re-layouts  24.1 us
    ppermute x8, starting transfers between devices, from_behind(): return lax.ppermute(x, axis, [(i, (i + by) % peers) for i in range(peers)])  22.1 us
    another operation x1, local copies, waits for them, and re-layouts, compress_bias(): unpacked = score_grad.reshape(leading + (WZ, WL, WC, WZ, WL, WC))  10.1 us
    dot_general x1, matrix products, expand_bias(): jnp.einsum('...pd,qd->...pq', combos, offset_table(WC), precision=lax.Pre...  8.87 us
    ppermute x8, waiting for transfers between devices, from_behind(): return lax.ppermute(x, axis, [(i, (i + by) % peers) for i in range(peers)])  6.64 us
  transfers between devices with their start and end apart: 9, of which 3 were waited for; matrix products, arithmetic and copies ran while one was open for 30% of the time, Pallas kernels for 0%

commit v1 on v0

v1 whole, which is shorter than its diff:
```python
import functools

import jax
import jax.numpy as jnp
from jax import lax
from jax.experimental import pallas as pl
from jax.experimental.pallas import tpu as pltpu
from jax.sharding import PartitionSpec as P

C = 192
HEADS = 6
HEAD = 32
LEVELS = 4
WL = 6
WC = 12
HALF = 6
POS = 3312
CHUNK = 138
SPAN = 23
GROUPS = 12
ROWS = 192
LANES = 384
CELLS = 288
PITCH = 16
WIDE = 3584
FOLD = 1664

norm_eps = 1e-05
mask_fill = -1e30
scale = HEAD**-0.5
vmem_bytes = 40 * 1024 * 1024

f32 = jnp.float32
bf16 = jnp.bfloat16


def iota(shape, dim):
    return lax.broadcasted_iota(jnp.int32, shape, dim)


def mm(a, b):
    return lax.dot_general(a, b, (((1,), (0,)), ((), ())), preferred_element_type=f32)


def mm_t(a, b):
    return lax.dot_general(a, b, (((1,), (1,)), ((), ())), preferred_element_type=f32)


def parts(index, size):
    return lax.div(index, jnp.int32(size)), lax.rem(index, jnp.int32(size))


def picks(index, count, dim):
    shape = (index.shape[0], count) if dim == 0 else (count, index.shape[1])
    return jnp.where(iota(shape, 1 - dim) == index, 1.0, 0.0).astype(bf16)


def line(size, dim):
    return iota((size, 1) if dim == 0 else (1, size), dim)


def query_cells(a, dim):
    column, group = parts(line(ROWS, dim), PITCH)
    level, row = parts(group, WL)
    return jnp.where(group < GROUPS, (row * WC + column) * LEVELS + 2 * a + level, -1)


def key_cells(a, dim):
    group, column = parts(line(LANES, dim), 32)
    level, row = parts(group, WL)
    return jnp.where(column < WC, (row * WC + column) * LEVELS + 2 * a + level, -1)


def spread_matrix(level, dim):
    group, place = parts(line(LANES, dim), 32)
    group = group - level * WL
    entry = jnp.where(
        (group >= 0) & (group < WL) & (place < SPAN), group * SPAN + place, -1
    )
    return picks(entry, LANES, dim)


def chunk_place(group, level):
    start = (((group // WL) * 2 + level) * WL + group % WL) * CHUNK
    return start // 128 * 128, start % 128


def table_kernel(bias_ref, table_ref, wide, pieces):
    wide[...] = jnp.zeros(wide.shape, f32)
    for a in range(2):
        for h in range(HEADS):
            wide[a * 8 + h : a * 8 + h + 1, 0:POS] = bias_ref[a * HEADS + h]
    total = jnp.zeros((ROWS, LANES), f32)
    for level in range(2):
        for group in range(GROUPS):
            tile, shift = chunk_place(group, level)
            piece = wide[:, tile : tile + LANES]
            if shift:
                piece = pltpu.roll(piece, LANES - shift, 1)
            pieces[group * PITCH : (group + 1) * PITCH, :] = piece
        spread = spread_matrix(level, 1)
        rest = pieces[...]
        for _ in range(3):
            part = rest.astype(bf16)
            total = total + mm(part, spread)
            rest = rest - part.astype(f32)
    pieces[...] = total
    table_ref[...] = jnp.zeros(table_ref.shape, f32)
    for group in range(GROUPS):
        for place in range(16):
            row = group * PITCH + place
            table_ref[place, group : group + 1, :] = pieces[row : row + 1, :]


def main_kernel(
    meta_ref,
    own_ref,
    east_ref,
    south_ref,
    diag_ref,
    gain_ref,
    w_qkv_ref,
    w_qkv_t_ref,
    w_proj_ref,
    table_ref,
    own_out,
    east_out,
    bias_out,
    framed,
    mask,
    queries,
    ups,
    queries_t,
    ups_t,
    keys_t,
    values_t,
    attended_t,
    grad_query_t,
    grad_key_t,
    grad_value_t,
    table_grad,
    wide,
    folds,
):
    shift = meta_ref[0]
    edge = meta_ref[1]

    half = HALF * LEVELS
    for r in range(WL):
        place = r + shift
        inside = place < WL
        near = jnp.minimum(place, WL - 1)
        far = jnp.maximum(place - WL, 0)
        left = jnp.where(inside, own_ref[near].astype(f32), south_ref[far].astype(f32))
        right = jnp.where(inside, east_ref[near].astype(f32), diag_ref[far].astype(f32))
        framed[2 * r * half : (2 * r + 1) * half, :] = left.reshape(half, 2 * C)
        framed[(2 * r + 1) * half : (2 * r + 2) * half, :] = right.reshape(half, 2 * C)

    cells = framed[:, 0:C]
    cotangent = framed[:, C : 2 * C].astype(bf16)
    centered = cells - jnp.mean(cells, axis=-1, keepdims=True)
    inverse = lax.rsqrt(jnp.mean(centered * centered, axis=-1, keepdims=True) + norm_eps)
    hidden = (centered * inverse * gain_ref[...]).astype(bf16)

    w_proj = w_proj_ref[...]
    for a in range(2):
        to_queries = picks(query_cells(a, 0), CELLS, 0)
        turned = mm(to_queries, hidden).astype(bf16)
        turned_cot = mm(to_queries, cotangent).astype(bf16)
        spaced = mm(picks(key_cells(a, 0), CELLS, 0), hidden).astype(bf16)
        queries[a] = mm(turned, w_qkv_ref[:, 0:C]).astype(bf16)
        queries_t[a] = mm_t(w_qkv_t_ref[0:C, :], turned).astype(bf16)
        keys_t[a] = mm_t(w_qkv_t_ref[C : 2 * C, :], spaced).astype(bf16)
        values_t[a] = mm_t(w_qkv_t_ref[2 * C : 3 * C, :], spaced).astype(bf16)
        ups[a] = mm_t(turned_cot, w_proj).astype(bf16)
        ups_t[a] = mm_t(w_proj, turned_cot).astype(bf16)

    query_row = parts(parts(line(ROWS, 0), PITCH)[1], WL)[1]
    key_group, key_column = parts(line(LANES, 1), 32)
    key_row = parts(key_group, WL)[1]
    query_id = jnp.where(query_row >= edge, 1, 0)
    key_id = jnp.where(key_column < WC, jnp.where(key_row >= edge, 1, 0), 2)
    mask[...] = jnp.where(query_id == key_id, 0.0, mask_fill)
    table_grad[...] = jnp.zeros(table_grad.shape, f32)

    def one_head(h, carry):
        features = pl.ds(pl.multiple_of(h * HEAD, HEAD), HEAD)
        chosen = iota((1, C), 1) // HEAD == h
        for a in range(2):
            query = jnp.where(chosen, queries[a], jnp.zeros((), bf16))
            up = jnp.where(chosen, ups[a], jnp.zeros((), bf16))
            scores = mm(query, keys_t[a]) * scale
            table = table_ref[a * 8 + h]
            bias = jnp.concatenate(
                [
                    pltpu.roll(table, (c - WC + 1) % LANES, 1) if c != WC - 1 else table
                    for c in range(WC)
                ],
                axis=0,
            )
            scores = scores + bias + mask[...]
            exponent = jnp.exp(scores - jnp.max(scores, axis=-1, keepdims=True))
            weights = exponent * (1.0 / jnp.sum(exponent, axis=-1, keepdims=True))
            weights_low = weights.astype(bf16)
            grad_weights = mm(up, values_t[a])
            row_dot = jnp.sum(weights * grad_weights, axis=-1, keepdims=True)
            grad_scores = weights * (grad_weights - row_dot)
            grad_low = grad_scores.astype(bf16)
            attended_t[a, features, :] = mm_t(values_t[a, features, :], weights_low).astype(bf16)
            grad_value_t[a, features, :] = mm(ups_t[a, features, :], weights_low).astype(bf16)
            grad_query_t[a, features, :] = (
                mm_t(keys_t[a, features, :], grad_low) * scale
            ).astype(bf16)
            grad_key_t[a, features, :] = (
                mm(queries_t[a, features, :], grad_low) * scale
            ).astype(bf16)
            folded = grad_scores[(WC - 1) * PITCH : WC * PITCH]
            for c in range(WC - 1):
                folded = folded + pltpu.roll(
                    grad_scores[c * PITCH : (c + 1) * PITCH], WC - 1 - c, 1
                )
            table_grad[a * 8 + h] = folded
        return carry

    lax.fori_loop(0, HEADS, one_head, 0)

    group, place = parts(line(ROWS, 0), PITCH)
    by_group = mm(
        picks(place * PITCH + group, 256, 0),
        table_grad[...].reshape(256, LANES).astype(bf16),
    ).astype(bf16)
    wide[...] = jnp.zeros(wide.shape, f32)
    for level in range(2):
        packed = mm(by_group, spread_matrix(level, 0))
        for group in range(GROUPS):
            tile, turn = chunk_place(group, level)
            piece = packed[group * PITCH : (group + 1) * PITCH]
            if turn:
                piece = pltpu.roll(piece, turn, 1)
            wide[:, tile : tile + LANES] += piece
    for side in range(2):
        for a in range(2):
            start = (2 * side + a) * HEADS
            folds[start : start + HEADS, :] = wide[
                a * 8 : a * 8 + HEADS, side * FOLD : (side + 1) * FOLD
            ]
    bias_out[...] = folds[...].astype(bf16)

    attended = jnp.zeros((CELLS, C), f32)
    coeffs = [jnp.zeros((CELLS, C), f32) for _ in range(3)]
    for a in range(2):
        from_queries = picks(query_cells(a, 1), CELLS, 1)
        from_keys = picks(key_cells(a, 1), CELLS, 1)
        attended = attended + mm_t(from_queries, attended_t[a])
        coeffs[0] = coeffs[0] + mm_t(from_queries, grad_query_t[a])
        coeffs[1] = coeffs[1] + mm_t(from_keys, grad_key_t[a])
        coeffs[2] = coeffs[2] + mm_t(from_keys, grad_value_t[a])
    framed[:, 0:C] = attended
    framed[:, C : 2 * C] = sum(
        mm(coeffs[part].astype(bf16), w_qkv_t_ref[part * C : (part + 1) * C, :])
        for part in range(3)
    )
    for r in range(WL):
        left = framed[2 * r * half : (2 * r + 1) * half, :]
        right = framed[(2 * r + 1) * half : (2 * r + 2) * half, :]
        own_out[r] = left.reshape(HALF, LEVELS, 2 * C).astype(bf16)
        east_out[r] = right.reshape(HALF, LEVELS, 2 * C).astype(bf16)


def home_kernel(
    meta_ref,
    own_ref,
    west_ref,
    north_ref,
    corner_ref,
    output_first_ref,
    output_second_ref,
    cotangent_second_ref,
    gain_ref,
    w_proj_ref,
    input_first_out,
    grad_second_out,
    placed,
):
    shift = meta_ref[0]
    half = HALF * LEVELS
    for r in range(WL):
        place = r - shift
        inside = place >= 0
        near = jnp.maximum(place, 0)
        far = jnp.minimum(place + WL, WL - 1)
        left = jnp.where(inside, west_ref[near].astype(f32), corner_ref[far].astype(f32))
        right = jnp.where(inside, own_ref[near].astype(f32), north_ref[far].astype(f32))
        placed[2 * r * half : (2 * r + 1) * half, :] = left.reshape(half, 2 * C)
        placed[(2 * r + 1) * half : (2 * r + 2) * half, :] = right.reshape(half, 2 * C)
    shape = (WL, WC, LEVELS, C)
    mixed = mm(placed[:, 0:C].astype(bf16), w_proj_ref[...])
    first = output_first_ref[...].astype(f32).reshape(CELLS, C)
    input_first_out[...] = (first - mixed).reshape(shape).astype(bf16)

    cells = output_second_ref[...].astype(f32).reshape(CELLS, C)
    centered = cells - jnp.mean(cells, axis=-1, keepdims=True)
    inverse = lax.rsqrt(jnp.mean(centered * centered, axis=-1, keepdims=True) + norm_eps)
    normed = centered * inverse
    scaled = placed[:, C : 2 * C] * gain_ref[...]
    backward = inverse * (
        scaled
        - jnp.mean(scaled, axis=-1, keepdims=True)
        - normed * jnp.mean(scaled * normed, axis=-1, keepdims=True)
    )
    second = cotangent_second_ref[...].astype(f32).reshape(CELLS, C)
    grad_second_out[...] = (second + backward).reshape(shape).astype(bf16)


def table_home_kernel(mine_ref, other_ref, table_out):
    total = mine_ref[...].astype(f32) + other_ref[...].astype(f32)
    rows = 2 * HEADS
    for row in range(rows):
        table_out[row, :, 0:FOLD] = total[row : row + 1]
        table_out[row, :, FOLD:POS] = total[rows + row : rows + row + 1, 0 : POS - FOLD]


def vmem(count):
    return [pl.BlockSpec(memory_space=pltpu.VMEM)] * count


def smem():
    return [pl.BlockSpec(memory_space=pltpu.SMEM)]


params = pltpu.CompilerParams(vmem_limit_bytes=vmem_bytes)


def cost(flops, moved):
    return pl.CostEstimate(flops=flops, bytes_accessed=moved, transcendentals=0)


def shifted(x, lat_step, lon_step):
    lats, lons = lax.axis_size("lat"), lax.axis_size("lon")
    if not lat_step:
        return lax.ppermute(x, "lon", [(i, (i + lon_step) % lons) for i in range(lons)])
    if not lon_step:
        return lax.ppermute(x, "lat", [(i, (i + lat_step) % lats) for i in range(lats)])
    pairs = [
        (j * lats + i, (j + lon_step) % lons * lats + (i + lat_step) % lats)
        for j in range(lons)
        for i in range(lats)
    ]
    return lax.ppermute(x, ("lon", "lat"), pairs)


def partner(x, axis, stride):
    return lax.ppermute(x, axis, [(i, i ^ stride) for i in range(lax.axis_size(axis))])


def by_cell(x):
    return x[0].transpose(1, 2, 0, 3)


def local(
    output_first,
    output_second,
    cotangent_first,
    cotangent_second,
    norm_gain,
    w_qkv,
    w_proj,
    earth_bias,
    shifts,
    region,
):
    second_cells = by_cell(output_second)
    pair = jnp.concatenate((second_cells, by_cell(cotangent_first)), axis=-1)
    left, right = pair[:, 0:HALF], pair[:, HALF:WC]
    east = shifted(left, 0, -1)
    diag = shifted(left, -1, -1)
    south = shifted(right, -1, 0)

    first_row = lax.axis_index("lat") * WL
    meta = jnp.stack((shifts[0], lax.axis_size("lat") * WL - shifts[0] - first_row))
    gain = norm_gain.reshape(1, C)
    w_qkv_t = w_qkv.T

    table = pl.pallas_call(
        table_kernel,
        out_shape=jax.ShapeDtypeStruct((16, 16, LANES), f32),
        in_specs=vmem(1),
        out_specs=vmem(1)[0],
        scratch_shapes=[pltpu.VMEM((16, WIDE), f32), pltpu.VMEM((ROWS, LANES), f32)],
        compiler_params=params,
        cost_estimate=cost(400_000_000, 1_000_000),
        name="bias_table",
    )(earth_bias.reshape(2 * HEADS, 1, POS))

    piece = functools.partial(jax.ShapeDtypeStruct, dtype=bf16)
    half_block = (WL, HALF, LEVELS, 2 * C)
    own, to_east, bias_part = pl.pallas_call(
        main_kernel,
        out_shape=(piece(half_block), piece(half_block), piece((4 * HEADS, FOLD))),
        in_specs=smem() + vmem(9),
        out_specs=tuple(vmem(3)),
        scratch_shapes=[
            pltpu.VMEM((CELLS, 2 * C), f32),
            pltpu.VMEM((ROWS, LANES), f32),
            pltpu.VMEM((2, ROWS, C), bf16),
            pltpu.VMEM((2, ROWS, C), bf16),
            pltpu.VMEM((2, C, ROWS), bf16),
            pltpu.VMEM((2, C, ROWS), bf16),
            pltpu.VMEM((2, C, LANES), bf16),
            pltpu.VMEM((2, C, LANES), bf16),
            pltpu.VMEM((2, C, ROWS), bf16),
            pltpu.VMEM((2, C, ROWS), bf16),
            pltpu.VMEM((2, C, LANES), bf16),
            pltpu.VMEM((2, C, LANES), bf16),
            pltpu.VMEM((16, 16, LANES), f32),
            pltpu.VMEM((16, WIDE), f32),
            pltpu.VMEM((4 * HEADS, FOLD), f32),
        ],
        compiler_params=params,
        cost_estimate=cost(4_000_000_000, 2_000_000),
        name="window_attention",
    )(meta, right, east, south, diag, gain, w_qkv, w_qkv_t, w_proj, table)

    west = shifted(to_east, 0, 1)
    corner = shifted(to_east, 1, 1)
    north = shifted(own, 1, 0)

    steps = [("lon", 1 << bit) for bit in range((lax.axis_size("lon") - 1).bit_length())]
    steps += [("dp", 1 << bit) for bit in range((lax.axis_size("dp") - 1).bit_length())]
    for axis, stride in steps[:-1]:
        other = partner(bias_part, axis, stride)
        bias_part = (bias_part.astype(f32) + other.astype(f32)).astype(bf16)
    bias_grad = pl.pallas_call(
        table_home_kernel,
        out_shape=jax.ShapeDtypeStruct((2 * HEADS, 1, POS), f32),
        in_specs=vmem(2),
        out_specs=vmem(1)[0],
        compiler_params=params,
        cost_estimate=cost(100_000, 400_000),
        name="table_home",
    )(bias_part, partner(bias_part, *steps[-1]))

    block = jax.ShapeDtypeStruct((WL, WC, LEVELS, C), bf16)
    input_first, grad_second = pl.pallas_call(
        home_kernel,
        out_shape=(block, block),
        in_specs=smem() + vmem(9),
        out_specs=tuple(vmem(2)),
        scratch_shapes=[pltpu.VMEM((CELLS, 2 * C), f32)],
        compiler_params=params,
        cost_estimate=cost(200_000_000, 2_000_000),
        name="home",
    )(
        meta,
        own,
        west,
        north,
        corner,
        by_cell(output_first),
        second_cells,
        by_cell(cotangent_second),
        gain,
        w_proj,
    )
    return (
        input_first.transpose(2, 0, 1, 3)[None],
        grad_second.transpose(2, 0, 1, 3)[None],
        bias_grad.reshape(2, 1, HEADS, POS),
    )


def solution(mesh):
    block = P("dp", None, "lat", "lon", None)
    table = P(None, "lat", None, None)
    return jax.shard_map(
        local,
        mesh=mesh,
        in_specs=(block, block, block, block, P(), P(), P(), table, P(), P()),
        out_specs=(block, block, table),
        check_vma=False,
    )
```

time: 314 us -> 80 us (0.25)
  the two profiles are of different devices: /device:TPU:8 before, /device:TPU:1 now
where the time goes in v1:
time: 80 us; the launch traced here: 79.6 us
  starting transfers between devices  43.2 us (54%)
  waiting for transfers between devices  16.9 us (21%)
  Pallas kernels  14.9 us (19%)
  local copies, waits for them, and re-layouts  2.25 us (3%)
  other arithmetic  1.43 us (2%)
  between operations  0.86 us (1%)
    ppermute x5, waiting for transfers between devices, partner(): lax.ppermute(x, axis, [(i, i ^ stride) for i in range(lax.axis_size(axis))])  16 us
    ppermute x2, starting transfers between devices, shifted(): lax.ppermute(x, 'lon', [(i, (i + lon_step) % lons) for i in range(lons)])  14.3 us
    ppermute x5, starting transfers between devices, partner(): lax.ppermute(x, axis, [(i, i ^ stride) for i in range(lax.axis_size(axis))])  13.9 us
    ppermute x2, starting transfers between devices, shifted(): return lax.ppermute(x, ('lon', 'lat'), pairs)  11.9 us
    pallas_call x1, Pallas kernels, local(): pl.pallas_call(main_kernel, out_shape=(piece(half_block), piece(half_bloc...  11.2 us
    ppermute x2, starting transfers between devices, shifted(): lax.ppermute(x, 'lat', [(i, (i + lat_step) % lats) for i in range(lats)])  3.05 us
    unnamed x17, local copies, waits for them, and re-layouts  2.25 us
    pallas_call x1, Pallas kernels, local(): pl.pallas_call(home_kernel, out_shape=(block, block), in_specs=smem() + v...  2.13 us
  transfers between devices with their start and end apart: 11, of which 5 were waited for; matrix products, arithmetic and copies ran while one was open for 0% of the time, Pallas kernels for 4%

profile of v1, /device:TPU:1, one launch (start us, length us, event | category | flops | bytes accessed | tf_op | source)
XLA Modules:
  0.0 79.6 jit_solution(5609757010628383299)
XLA Ops:
  0.6 0.0 copy-start.1
  0.6 1.2 %pad_maximum_fusion = (bf16[6,6,4,384]{3,2,1,0:T(4,128)(2,1)S(1)}, bf16[6,6,4,384]{3,2,1,0:T(4,128)(2,1)S(1)}) fusion(bf16[6,12,4,192]{3,2,1,0:T(4,128)(2,1)} %bitcast.34, bf16[6,12,4,192]{3,2,1,0:T(4,128)(2,1)} %bitcast.25), kind=kLoop, calls=%fused_computation.7 | loop fusion | flops 442368 | bytes 442368 | tf_op jit(solution)/shard_map/concatenate | solution.py:373
  1.9 12.4 %collective-permute-start = (bf16[6,6,4,384]{3,2,1,0:T(4,128)(2,1)S(1)}, bf16[6,6,4,384]{3,2,1,0:T(4,128)(2,1)S(1)}, u32[]{:S(2)}, u32[]{:S(2)}) collective-permute-start(bf16[6,6,4,384]{3,2,1,0:T(4,128)(2,1)S(1)} %get-tuple-element.13), channel_id=1, source_target_pairs={{0,480},{32,0},{64,32},{96,64},{128,96},{160,128},{192,160},{224,1... | collective-permute-start | bytes 331784 | tf_op jit(solution)/shard_map/ppermute | solution.py:341
  14.3 3.0 %collective-permute-start.2 = (bf16[6,6,4,384]{3,2,1,0:T(4,128)(2,1)S(1)}, bf16[6,6,4,384]{3,2,1,0:T(4,128)(2,1)S(1)}, u32[]{:S(2)}, u32[]{:S(2)}) collective-permute-start(bf16[6,6,4,384]{3,2,1,0:T(4,128)(2,1)S(1)} %get-tuple-element.13), channel_id=1, source_target_pairs={{0,510},{2,480},{4,482},{6,484},{8,486},{10,488},{12,490},{14,492}... | collective-permute-start | bytes 331784 | tf_op jit(solution)/shard_map/ppermute | solution.py:349
  17.3 2.5 %collective-permute-start.1 = (bf16[6,6,4,384]{3,2,1,0:T(4,128)(2,1)S(1)}, bf16[6,6,4,384]{3,2,1,0:T(4,128)(2,1)S(1)}, u32[]{:S(2)}, u32[]{:S(2)}) collective-permute-start(bf16[6,6,4,384]{3,2,1,0:T(4,128)(2,1)S(1)} %get-tuple-element.14.own_ref), channel_id=1, source_target_pairs={{0,30},{2,0},{4,2},{6,4},{8,6},{10,8},{12,10},{14,12},{16,14},{18,... | collective-permute-start | bytes 331784 | tf_op jit(solution)/shard_map/ppermute | solution.py:343
  19.8 0.0 copy-done.1
  19.8 0.0 copy-start.6
  19.8 0.2 copy.12
  20.0 0.7 copy-done.6
  20.7 0.0 copy-start.4
  20.7 0.9 %bias_table.1.table_ref = f32[16,16,384]{2,1,0:T(8,128)S(1)} custom-call(f32[12,1,3312]{2,1,0:T(1,128)S(1)} %bitcast.32), custom_call_target="tpu_custom_call" | custom-call | flops 400000000 | bytes 1000000 | tf_op jit(solution)/shard_map/bias_table/pallas_call | solution.py:384
  21.6 0.0 copy-start.7
  21.6 0.6 copy-done.7
  22.3 0.1 pad_add_fusion.meta_ref
  22.4 0.0 collective-permute-done.east_ref
  22.4 0.0 collective-permute-done.2.diag_ref
  22.4 0.0 collective-permute-done.1.south_ref
  22.4 0.0 copy-start.5
  22.4 0.0 copy-done.4
  22.5 0.7 copy-done.5
  23.1 11.2 %window_attention.1 = (bf16[6,6,4,384]{3,2,1,0:T(4,128)(2,1)S(1)}, bf16[6,6,4,384]{3,2,1,0:T(4,128)(2,1)S(1)}, bf16[24,1664]{1,0:T(8,128)(2,1)S(1)}) custom-call(s32[2]{0:T(128)S(1)} %pad_add_fusion.meta_ref, bf16[6,6,4,384]{3,2,1,0:T(4,128)(2,1)S(1)} %get-tuple-element.14.own_ref, bf16[6,6,4,384]{3,2,1,0:T(4,128)(2,1)S(1)} %collective-permute-done.east_ref, ...), custom_call_target="tpu_custom_call" | custom-call | flops 4000000000 | bytes 2000000 | tf_op jit(solution)/shard_map/window_attention/pallas_call | solution.py:397
  34.3 3.1 %collective-permute-start.6 = (bf16[24,1664]{1,0:T(8,128)(2,1)S(1)}, bf16[24,1664]{1,0:T(8,128)(2,1)S(1)}, u32[]{:S(2)}, u32[]{:S(2)}) collective-permute-start(bf16[24,1664]{1,0:T(8,128)(2,1)S(1)} %get-tuple-element.12), channel_id=1, source_target_pairs={{0,32},{32,0},{64,96},{96,64},{128,160},{160,128},{192,224},{224,1... | collective-permute-start | bytes 239624 | tf_op jit(solution)/shard_map/ppermute | solution.py:353
  37.5 2.1 %collective-permute-done.6 = bf16[24,1664]{1,0:T(8,128)(2,1)S(1)} collective-permute-done((bf16[24,1664]{1,0:T(8,128)(2,1)S(1)}, bf16[24,1664]{1,0:T(8,128)(2,1)S(1)}, u32[]{:S(2)}, u32[]{:S(2)}) %collective-permute-start.6) | collective-permute-done | bytes 79904 | tf_op jit(solution)/shard_map/ppermute | solution.py:353
  39.5 1.9 %collective-permute-start.7 = (bf16[24,1664]{1,0:T(8,128)(2,1)S(1)}, bf16[24,1664]{1,0:T(8,128)(2,1)S(1)}, u32[]{:S(2)}, u32[]{:S(2)}) collective-permute-start(bf16[24,1664]{1,0:T(8,128)(2,1)S(1)} %add_convert_fusion.3), channel_id=1, source_target_pairs={{0,64},{32,96},{64,0},{96,32},{128,192},{160,224},{192,128},{224,1... | collective-permute-start | bytes 239624 | tf_op jit(solution)/shard_map/ppermute | solution.py:353
  41.5 4.1 %collective-permute-done.7 = bf16[24,1664]{1,0:T(8,128)(2,1)S(1)} collective-permute-done((bf16[24,1664]{1,0:T(8,128)(2,1)S(1)}, bf16[24,1664]{1,0:T(8,128)(2,1)S(1)}, u32[]{:S(2)}, u32[]{:S(2)}) %collective-permute-start.7) | collective-permute-done | bytes 79904 | tf_op jit(solution)/shard_map/ppermute | solution.py:353
  45.6 2.2 %collective-permute-start.8 = (bf16[24,1664]{1,0:T(8,128)(2,1)S(1)}, bf16[24,1664]{1,0:T(8,128)(2,1)S(1)}, u32[]{:S(2)}, u32[]{:S(2)}) collective-permute-start(bf16[24,1664]{1,0:T(8,128)(2,1)S(1)} %add_convert_fusion.2), channel_id=1, source_target_pairs={{0,128},{32,160},{64,192},{96,224},{128,0},{160,32},{192,64},{224,... | collective-permute-start | bytes 239624 | tf_op jit(solution)/shard_map/ppermute | solution.py:353
  47.8 7.0 %collective-permute-done.8 = bf16[24,1664]{1,0:T(8,128)(2,1)S(1)} collective-permute-done((bf16[24,1664]{1,0:T(8,128)(2,1)S(1)}, bf16[24,1664]{1,0:T(8,128)(2,1)S(1)}, u32[]{:S(2)}, u32[]{:S(2)}) %collective-permute-start.8) | collective-permute-done | bytes 79904 | tf_op jit(solution)/shard_map/ppermute | solution.py:353
  54.8 0.0 copy-start.2
  54.8 0.0 copy-start.3
  54.8 0.0 copy-start
  54.8 2.2 %collective-permute-start.9 = (bf16[24,1664]{1,0:T(8,128)(2,1)S(1)}, bf16[24,1664]{1,0:T(8,128)(2,1)S(1)}, u32[]{:S(2)}, u32[]{:S(2)}) collective-permute-start(bf16[24,1664]{1,0:T(8,128)(2,1)S(1)} %add_convert_fusion.1), channel_id=1, source_target_pairs={{0,256},{32,288},{64,320},{96,352},{128,384},{160,416},{192,448},{... | collective-permute-start | bytes 239624 | tf_op jit(solution)/shard_map/ppermute | solution.py:353
  57.1 8.9 %collective-permute-start.5 = (bf16[6,6,4,384]{3,2,1,0:T(4,128)(2,1)S(1)}, bf16[6,6,4,384]{3,2,1,0:T(4,128)(2,1)S(1)}, u32[]{:S(2)}, u32[]{:S(2)}) collective-permute-start(bf16[6,6,4,384]{3,2,1,0:T(4,128)(2,1)S(1)} %get-tuple-element.9), channel_id=1, source_target_pairs={{0,34},{2,36},{4,38},{6,40},{8,42},{10,44},{12,46},{14,48},{16,50}... | collective-permute-start | bytes 331784 | tf_op jit(solution)/shard_map/ppermute | solution.py:349
  65.9 1.9 %collective-permute-start.3 = (bf16[6,6,4,384]{3,2,1,0:T(4,128)(2,1)S(1)}, bf16[6,6,4,384]{3,2,1,0:T(4,128)(2,1)S(1)}, u32[]{:S(2)}, u32[]{:S(2)}) collective-permute-start(bf16[6,6,4,384]{3,2,1,0:T(4,128)(2,1)S(1)} %get-tuple-element.9), channel_id=1, source_target_pairs={{0,32},{32,64},{64,96},{96,128},{128,160},{160,192},{192,224},{224... | collective-permute-start | bytes 331784 | tf_op jit(solution)/shard_map/ppermute | solution.py:341
  67.8 0.6 collective-permute-start.4
  68.4 0.0 collective-permute-done.9
  68.5 4.5 %collective-permute-start.10 = (bf16[24,1664]{1,0:T(8,128)(2,1)S(1)}, bf16[24,1664]{1,0:T(8,128)(2,1)S(1)}, u32[]{:S(2)}, u32[]{:S(2)}) collective-permute-start(bf16[24,1664]{1,0:T(8,128)(2,1)S(1)} %add_convert_fusion.mine_ref), channel_id=1, source_target_pairs={{0,1},{1,0},{2,3},{3,2},{4,5},{5,4},{6,7},{7,6},{8,9},{9,8},{10,11... | collective-permute-start | bytes 239624 | tf_op jit(solution)/shard_map/ppermute | solution.py:353
  73.0 0.0 collective-permute-done.4.north_ref
  73.0 0.0 collective-permute-done.5.corner_ref
  73.0 0.9 %collective-permute-done.3.west_ref = bf16[6,6,4,384]{3,2,1,0:T(4,128)(2,1)S(1)} collective-permute-done((bf16[6,6,4,384]{3,2,1,0:T(4,128)(2,1)S(1)}, bf16[6,6,4,384]{3,2,1,0:T(4,128)(2,1)S(1)}, u32[]{:S(2)}, u32[]{:S(2)}) %collective-permute-start.3) | collective-permute-done | bytes 110624 | tf_op jit(solution)/shard_map/ppermute | solution.py:341
  73.9 0.0 copy-done.2
  73.9 0.0 copy-done.3
  73.9 0.0 copy-done
  73.9 2.1 %home.1 = (bf16[6,12,4,192]{3,2,1,0:T(4,128)(2,1)}, bf16[6,12,4,192]{3,2,1,0:T(4,128)(2,1)}) custom-call(s32[2]{0:T(128)S(1)} %pad_add_fusion.meta_ref, bf16[6,6,4,384]{3,2,1,0:T(4,128)(2,1)S(1)} %get-tuple-element.8.own_ref, bf16[6,6,4,384]{3,2,1,0:T(4,128)(2,1)S(1)} %collective-permute-done.3.west_ref, ...), custom_call_target="tpu_custom_call" | custom-call | flops 200000000 | bytes 2000000 | tf_op jit(solution)/shard_map/home/pallas_call | solution.py:444
  76.0 2.8 %collective-permute-done.10.other_ref = bf16[24,1664]{1,0:T(8,128)(2,1)S(1)} collective-permute-done((bf16[24,1664]{1,0:T(8,128)(2,1)S(1)}, bf16[24,1664]{1,0:T(8,128)(2,1)S(1)}, u32[]{:S(2)}, u32[]{:S(2)}) %collective-permute-start.10) | collective-permute-done | bytes 79904 | tf_op jit(solution)/shard_map/ppermute | solution.py:353
  78.9 0.7 table_home.1
  (4 shorter events, 0.1 us)
Async XLA Ops:
  0.6 19.2 %copy-start.1 = (bf16[192,576]{1,0:T(8,128)(2,1)S(1)}, bf16[192,576]{1,0:T(8,128)(2,1)}, u32[]{:S(2)}) copy-start(bf16[192,576]{1,0:T(8,128)(2,1)} %w_qkv_ref.1) | copy-start | bytes 663556
  1.9 20.6 %collective-permute-start = (bf16[6,6,4,384]{3,2,1,0:T(4,128)(2,1)S(1)}, bf16[6,6,4,384]{3,2,1,0:T(4,128)(2,1)S(1)}, u32[]{:S(2)}, u32[]{:S(2)}) collective-permute-start(bf16[6,6,4,384]{3,2,1,0:T(4,128)(2,1)S(1)} %get-tuple-element.13), channel_id=1, source_target_pairs={{0,480},{32,0},{64,32},{96,64},{128,96},{160,128},{192,160},{224,1... | collective-permute-start | bytes 331784 | tf_op jit(solution)/shard_map/ppermute | solution.py:341
  14.3 8.1 %collective-permute-start.2 = (bf16[6,6,4,384]{3,2,1,0:T(4,128)(2,1)S(1)}, bf16[6,6,4,384]{3,2,1,0:T(4,128)(2,1)S(1)}, u32[]{:S(2)}, u32[]{:S(2)}) collective-permute-start(bf16[6,6,4,384]{3,2,1,0:T(4,128)(2,1)S(1)} %get-tuple-element.13), channel_id=1, source_target_pairs={{0,510},{2,480},{4,482},{6,484},{8,486},{10,488},{12,490},{14,492}... | collective-permute-start | bytes 331784 | tf_op jit(solution)/shard_map/ppermute | solution.py:349
  17.3 5.1 %collective-permute-start.1 = (bf16[6,6,4,384]{3,2,1,0:T(4,128)(2,1)S(1)}, bf16[6,6,4,384]{3,2,1,0:T(4,128)(2,1)S(1)}, u32[]{:S(2)}, u32[]{:S(2)}) collective-permute-start(bf16[6,6,4,384]{3,2,1,0:T(4,128)(2,1)S(1)} %get-tuple-element.14.own_ref), channel_id=1, source_target_pairs={{0,30},{2,0},{4,2},{6,4},{8,6},{10,8},{12,10},{14,12},{16,14},{18,... | collective-permute-start | bytes 331784 | tf_op jit(solution)/shard_map/ppermute | solution.py:343
  19.8 0.9 %copy-start.6 = (f32[2,1,6,3312]{3,1,2,0:T(1,128)S(1)}, f32[2,1,6,3312]{3,1,2,0:T(1,128)}, u32[]{:S(2)}) copy-start(f32[2,1,6,3312]{3,1,2,0:T(1,128)} %param.17) | copy-start | bytes 476932
  20.7 1.7 %copy-start.4 = (bf16[192,192]{1,0:T(8,128)(2,1)S(1)}, bf16[192,192]{1,0:T(8,128)(2,1)}, u32[]{:S(2)}) copy-start(bf16[192,192]{1,0:T(8,128)(2,1)} %w_proj_ref.3) | copy-start | bytes 221188
  21.6 0.7 copy-start.7
  22.4 0.7 copy-start.5
  34.3 5.2 %collective-permute-start.6 = (bf16[24,1664]{1,0:T(8,128)(2,1)S(1)}, bf16[24,1664]{1,0:T(8,128)(2,1)S(1)}, u32[]{:S(2)}, u32[]{:S(2)}) collective-permute-start(bf16[24,1664]{1,0:T(8,128)(2,1)S(1)} %get-tuple-element.12), channel_id=1, source_target_pairs={{0,32},{32,0},{64,96},{96,64},{128,160},{160,128},{192,224},{224,1... | collective-permute-start | bytes 239624 | tf_op jit(solution)/shard_map/ppermute | solution.py:353
  39.5 6.1 %collective-permute-start.7 = (bf16[24,1664]{1,0:T(8,128)(2,1)S(1)}, bf16[24,1664]{1,0:T(8,128)(2,1)S(1)}, u32[]{:S(2)}, u32[]{:S(2)}) collective-permute-start(bf16[24,1664]{1,0:T(8,128)(2,1)S(1)} %add_convert_fusion.3), channel_id=1, source_target_pairs={{0,64},{32,96},{64,0},{96,32},{128,192},{160,224},{192,128},{224,1... | collective-permute-start | bytes 239624 | tf_op jit(solution)/shard_map/ppermute | solution.py:353
  45.6 9.1 %collective-permute-start.8 = (bf16[24,1664]{1,0:T(8,128)(2,1)S(1)}, bf16[24,1664]{1,0:T(8,128)(2,1)S(1)}, u32[]{:S(2)}, u32[]{:S(2)}) collective-permute-start(bf16[24,1664]{1,0:T(8,128)(2,1)S(1)} %add_convert_fusion.2), channel_id=1, source_target_pairs={{0,128},{32,160},{64,192},{96,224},{128,0},{160,32},{192,64},{224,... | collective-permute-start | bytes 239624 | tf_op jit(solution)/shard_map/ppermute | solution.py:353
  54.8 19.1 %copy-start.2 = (bf16[1,4,6,12,192]{4,1,3,2,0:T(4,128)(2,1)S(1)}, bf16[1,4,6,12,192]{4,1,3,2,0:T(4,128)(2,1)}, u32[]{:S(2)}) copy-start(bf16[1,4,6,12,192]{4,1,3,2,0:T(4,128)(2,1)} %param.10) | copy-start | bytes 331780
  54.8 19.1 %copy-start.3 = (bf16[1,4,6,12,192]{4,1,3,2,0:T(4,128)(2,1)S(1)}, bf16[1,4,6,12,192]{4,1,3,2,0:T(4,128)(2,1)}, u32[]{:S(2)}) copy-start(bf16[1,4,6,12,192]{4,1,3,2,0:T(4,128)(2,1)} %param.13) | copy-start | bytes 331780
  54.8 19.1 %copy-start = (bf16[1,4,6,12,192]{4,1,3,2,0:T(4,128)(2,1)S(1)}, bf16[1,4,6,12,192]{4,1,3,2,0:T(4,128)(2,1)}, u32[]{:S(2)}) copy-start(bf16[1,4,6,12,192]{4,1,3,2,0:T(4,128)(2,1)} %param.11) | copy-start | bytes 331780
  54.8 13.6 %collective-permute-start.9 = (bf16[24,1664]{1,0:T(8,128)(2,1)S(1)}, bf16[24,1664]{1,0:T(8,128)(2,1)S(1)}, u32[]{:S(2)}, u32[]{:S(2)}) collective-permute-start(bf16[24,1664]{1,0:T(8,128)(2,1)S(1)} %add_convert_fusion.1), channel_id=1, source_target_pairs={{0,256},{32,288},{64,320},{96,352},{128,384},{160,416},{192,448},{... | collective-permute-start | bytes 239624 | tf_op jit(solution)/shard_map/ppermute | solution.py:353
  57.1 15.9 %collective-permute-start.5 = (bf16[6,6,4,384]{3,2,1,0:T(4,128)(2,1)S(1)}, bf16[6,6,4,384]{3,2,1,0:T(4,128)(2,1)S(1)}, u32[]{:S(2)}, u32[]{:S(2)}) collective-permute-start(bf16[6,6,4,384]{3,2,1,0:T(4,128)(2,1)S(1)} %get-tuple-element.9), channel_id=1, source_target_pairs={{0,34},{2,36},{4,38},{6,40},{8,42},{10,44},{12,46},{14,48},{16,50}... | collective-permute-start | bytes 331784 | tf_op jit(solution)/shard_map/ppermute | solution.py:349
  65.9 8.0 %collective-permute-start.3 = (bf16[6,6,4,384]{3,2,1,0:T(4,128)(2,1)S(1)}, bf16[6,6,4,384]{3,2,1,0:T(4,128)(2,1)S(1)}, u32[]{:S(2)}, u32[]{:S(2)}) collective-permute-start(bf16[6,6,4,384]{3,2,1,0:T(4,128)(2,1)S(1)} %get-tuple-element.9), channel_id=1, source_target_pairs={{0,32},{32,64},{64,96},{96,128},{128,160},{160,192},{192,224},{224... | collective-permute-start | bytes 331784 | tf_op jit(solution)/shard_map/ppermute | solution.py:341
  67.8 5.1 %collective-permute-start.4 = (bf16[6,6,4,384]{3,2,1,0:T(4,128)(2,1)S(1)}, bf16[6,6,4,384]{3,2,1,0:T(4,128)(2,1)S(1)}, u32[]{:S(2)}, u32[]{:S(2)}) collective-permute-start(bf16[6,6,4,384]{3,2,1,0:T(4,128)(2,1)S(1)} %get-tuple-element.8.own_ref), channel_id=1, source_target_pairs={{0,2},{2,4},{4,6},{6,8},{8,10},{10,12},{12,14},{14,16},{16,18},{18... | collective-permute-start | bytes 331784 | tf_op jit(solution)/shard_map/ppermute | solution.py:343
  68.5 10.4 %collective-permute-start.10 = (bf16[24,1664]{1,0:T(8,128)(2,1)S(1)}, bf16[24,1664]{1,0:T(8,128)(2,1)S(1)}, u32[]{:S(2)}, u32[]{:S(2)}) collective-permute-start(bf16[24,1664]{1,0:T(8,128)(2,1)S(1)} %add_convert_fusion.mine_ref), channel_id=1, source_target_pairs={{0,1},{1,0},{2,3},{3,2},{4,5},{5,4},{6,7},{7,6},{8,9},{9,8},{10,11... | collective-permute-start | bytes 239624 | tf_op jit(solution)/shard_map/ppermute | solution.py:353

commit v2 on v1

--- a/solution.py
+++ b/solution.py
@@ -24,11 +24,15 @@
 PITCH = 16
 WIDE = 3584
 FOLD = 1664
+TILES = 78
+CHUNKS = 16
+DEEP = 5
+SAMPLES = 2
 
 norm_eps = 1e-05
 mask_fill = -1e30
 scale = HEAD**-0.5
-vmem_bytes = 40 * 1024 * 1024
+vmem_bytes = 20 * 1024 * 1024
 
 f32 = jnp.float32
 bf16 = jnp.bfloat16
@@ -85,7 +89,8 @@
     return start // 128 * 128, start % 128
 
 
-def table_kernel(bias_ref, table_ref, wide, pieces):
+def table_kernel(bias_ref, gain_ref, table_ref, gain_out, wide, pieces):
+    gain_out[...] = gain_ref[...]
     wide[...] = jnp.zeros(wide.shape, f32)
     for a in range(2):
         for h in range(HEADS):
@@ -112,49 +117,73 @@
             table_ref[place, group : group + 1, :] = pieces[row : row + 1, :]
 
 
-def main_kernel(
+def frame_kernel(meta_ref, own_ref, other_ref, near_out, send_out):
+    for r in range(WL):
+        place = r + meta_ref[0]
+
+        @pl.when(place < WL)
+        def _():
+            near_out[r] = own_ref[place, HALF:WC]
+            send_out[r] = own_ref[place, 0:HALF]
+
+        @pl.when(place >= WL)
+        def _():
+            near_out[r] = other_ref[place - WL, HALF:WC]
+            send_out[r] = other_ref[place - WL, 0:HALF]
+
+
+def unframe_kernel(meta_ref, own_ref, other_ref, near_out, send_out):
+    for r in range(WL):
+        place = r - meta_ref[0]
+
+        @pl.when(place >= 0)
+        def _():
+            near_out[r] = own_ref[place, 0:HALF]
+            send_out[r] = own_ref[place, HALF:WC]
+
+        @pl.when(place < 0)
+        def _():
+            near_out[r] = other_ref[place + WL - 1, 0:HALF]
+            send_out[r] = other_ref[place + WL - 1, HALF:WC]
+
+
+def join_halves(left_ref, right_ref, joined):
+    half = HALF * LEVELS
+    for r in range(WL):
+        start = 2 * r * half
+        joined[start : start + half, :] = left_ref[r].astype(f32).reshape(half, 2 * C)
+        joined[start + half : start + 2 * half, :] = (
+            right_ref[r].astype(f32).reshape(half, 2 * C)
+        )
+
+
+def scores_kernel(
     meta_ref,
-    own_ref,
+    near_ref,
     east_ref,
-    south_ref,
-    diag_ref,
     gain_ref,
     w_qkv_ref,
     w_qkv_t_ref,
     w_proj_ref,
     table_ref,
-    own_out,
-    east_out,
+    weights_out,
+    grads_out,
+    queries_t,
+    ups_t,
+    keys_t,
+    values_t,
     bias_out,
     framed,
     mask,
     queries,
     ups,
-    queries_t,
-    ups_t,
-    keys_t,
-    values_t,
-    attended_t,
-    grad_query_t,
-    grad_key_t,
-    grad_value_t,
     table_grad,
     wide,
     folds,
+    packed_table,
 ):
-    shift = meta_ref[0]
     edge = meta_ref[1]
-
-    half = HALF * LEVELS
-    for r in range(WL):
-        place = r + shift
-        inside = place < WL
-        near = jnp.minimum(place, WL - 1)
-        far = jnp.maximum(place - WL, 0)
-        left = jnp.where(inside, own_ref[near].astype(f32), south_ref[far].astype(f32))
-        right = jnp.where(inside, east_ref[near].astype(f32), diag_ref[far].astype(f32))
-        framed[2 * r * half : (2 * r + 1) * half, :] = left.reshape(half, 2 * C)
-        framed[(2 * r + 1) * half : (2 * r + 2) * half, :] = right.reshape(half, 2 * C)
+    join_halves(near_ref, east_ref, framed)
 
     cells = framed[:, 0:C]
     cotangent = framed[:, C : 2 * C].astype(bf16)
@@ -184,7 +213,6 @@
     table_grad[...] = jnp.zeros(table_grad.shape, f32)
 
     def one_head(h, carry):
-        features = pl.ds(pl.multiple_of(h * HEAD, HEAD), HEAD)
         chosen = iota((1, C), 1) // HEAD == h
         for a in range(2):
             query = jnp.where(chosen, queries[a], jnp.zeros((), bf16))
@@ -205,15 +233,8 @@
             grad_weights = mm(up, values_t[a])
             row_dot = jnp.sum(weights * grad_weights, axis=-1, keepdims=True)
             grad_scores = weights * (grad_weights - row_dot)
-            grad_low = grad_scores.astype(bf16)
-            attended_t[a, features, :] = mm_t(values_t[a, features, :], weights_low).astype(bf16)
-            grad_value_t[a, features, :] = mm(ups_t[a, features, :], weights_low).astype(bf16)
-            grad_query_t[a, features, :] = (
-                mm_t(keys_t[a, features, :], grad_low) * scale
-            ).astype(bf16)
-            grad_key_t[a, features, :] = (
-                mm(queries_t[a, features, :], grad_low) * scale
-            ).astype(bf16)
+            weights_out[a, h] = weights_low
+            grads_out[a, h] = grad_scores.astype(bf16)
             folded = grad_scores[(WC - 1) * PITCH : WC * PITCH]
             for c in range(WC - 1):
                 folded = folded + pltpu.roll(
@@ -238,13 +259,48 @@
             if turn:
                 piece = pltpu.roll(piece, turn, 1)
             wide[:, tile : tile + LANES] += piece
+    packed_table[...] = jnp.zeros(packed_table.shape, f32)
     for side in range(2):
         for a in range(2):
             start = (2 * side + a) * HEADS
             folds[start : start + HEADS, :] = wide[
                 a * 8 : a * 8 + HEADS, side * FOLD : (side + 1) * FOLD
             ]
-    bias_out[...] = folds[...].astype(bf16)
+    for tile in range(TILES):
+        chunk, slot, fold_rows, fold_lanes = tile_place(tile)
+        packed_table[chunk, slot] = folds[fold_rows, fold_lanes]
+    bias_out[...] = packed_table[...].astype(bf16)
+
+
+def coeffs_kernel(
+    weights_ref,
+    grads_ref,
+    queries_t,
+    ups_t,
+    keys_t,
+    values_t,
+    w_qkv_t_ref,
+    own_out,
+    south_out,
+    attended_t,
+    grad_query_t,
+    grad_key_t,
+    grad_value_t,
+    joined,
+):
+    for h in range(HEADS):
+        features = slice(h * HEAD, (h + 1) * HEAD)
+        for a in range(2):
+            weights_low = weights_ref[a, h]
+            grad_low = grads_ref[a, h]
+            attended_t[a, features, :] = mm_t(values_t[a, features, :], weights_low).astype(bf16)
+            grad_value_t[a, features, :] = mm(ups_t[a, features, :], weights_low).astype(bf16)
+            grad_query_t[a, features, :] = (
+                mm_t(keys_t[a, features, :], grad_low) * scale
+            ).astype(bf16)
+            grad_key_t[a, features, :] = (
+                mm(queries_t[a, features, :], grad_low) * scale
+            ).astype(bf16)
 
     attended = jnp.zeros((CELLS, C), f32)
     coeffs = [jnp.zeros((CELLS, C), f32) for _ in range(3)]
@@ -255,24 +311,23 @@
         coeffs[0] = coeffs[0] + mm_t(from_queries, grad_query_t[a])
         coeffs[1] = coeffs[1] + mm_t(from_keys, grad_key_t[a])
         coeffs[2] = coeffs[2] + mm_t(from_keys, grad_value_t[a])
-    framed[:, 0:C] = attended
-    framed[:, C : 2 * C] = sum(
+    joined[:, 0:C] = attended
+    joined[:, C : 2 * C] = sum(
         mm(coeffs[part].astype(bf16), w_qkv_t_ref[part * C : (part + 1) * C, :])
         for part in range(3)
     )
+    row_cells = WC * LEVELS
     for r in range(WL):
-        left = framed[2 * r * half : (2 * r + 1) * half, :]
-        right = framed[(2 * r + 1) * half : (2 * r + 2) * half, :]
-        own_out[r] = left.reshape(HALF, LEVELS, 2 * C).astype(bf16)
-        east_out[r] = right.reshape(HALF, LEVELS, 2 * C).astype(bf16)
+        row = joined[r * row_cells : (r + 1) * row_cells, :]
+        row = row.reshape(WC, LEVELS, 2 * C).astype(bf16)
+        own_out[r] = row
+        if r:
+            south_out[r - 1] = row
 
 
 def home_kernel(
-    meta_ref,
-    own_ref,
     west_ref,
-    north_ref,
-    corner_ref,
+    near_ref,
     output_first_ref,
     output_second_ref,
     cotangent_second_ref,
@@ -282,17 +337,7 @@
     grad_second_out,
     placed,
 ):
-    shift = meta_ref[0]
-    half = HALF * LEVELS
-    for r in range(WL):
-        place = r - shift
-        inside = place >= 0
-        near = jnp.maximum(place, 0)
-        far = jnp.minimum(place + WL, WL - 1)
-        left = jnp.where(inside, west_ref[near].astype(f32), corner_ref[far].astype(f32))
-        right = jnp.where(inside, own_ref[near].astype(f32), north_ref[far].astype(f32))
-        placed[2 * r * half : (2 * r + 1) * half, :] = left.reshape(half, 2 * C)
-        placed[(2 * r + 1) * half : (2 * r + 2) * half, :] = right.reshape(half, 2 * C)
+    join_halves(west_ref, near_ref, placed)
     shape = (WL, WC, LEVELS, C)
     mixed = mm(placed[:, 0:C].astype(bf16), w_proj_ref[...])
     first = output_first_ref[...].astype(f32).reshape(CELLS, C)
@@ -312,12 +357,34 @@
     grad_second_out[...] = (second + backward).reshape(shape).astype(bf16)
 
 
-def table_home_kernel(mine_ref, other_ref, table_out):
-    total = mine_ref[...].astype(f32) + other_ref[...].astype(f32)
+def tile_place(tile):
+    chunk, slot = divmod(tile, DEEP)
+    block, column = divmod(tile, FOLD // 128)
+    return (
+        chunk,
+        slot,
+        slice(block * 4, block * 4 + 4),
+        slice(column * 128, column * 128 + 128),
+    )
+
+
+def table_sum_kernel(parts_ref, after_ref, sums_out):
+    total = jnp.sum(parts_ref[...].astype(f32), axis=0).astype(bf16)
+    for peer in range(sums_out.shape[0]):
+        sums_out[peer] = total
+
+
+def table_home_kernel(sums_ref, table_out, folds):
+    for tile in range(TILES):
+        chunk, slot, fold_rows, fold_lanes = tile_place(tile)
+        samples = [
+            sums_ref[chunk * SAMPLES + part, slot].astype(f32) for part in range(SAMPLES)
+        ]
+        folds[fold_rows, fold_lanes] = sum(samples)
     rows = 2 * HEADS
     for row in range(rows):
-        table_out[row, :, 0:FOLD] = total[row : row + 1]
-        table_out[row, :, FOLD:POS] = total[rows + row : rows + row + 1, 0 : POS - FOLD]
+        table_out[row, :, 0:FOLD] = folds[row : row + 1]
+        table_out[row, :, FOLD:POS] = folds[rows + row : rows + row + 1, 0 : POS - FOLD]
 
 
 def vmem(count):
@@ -335,22 +402,13 @@
     return pl.CostEstimate(flops=flops, bytes_accessed=moved, transcendentals=0)
 
 
-def shifted(x, lat_step, lon_step):
-    lats, lons = lax.axis_size("lat"), lax.axis_size("lon")
-    if not lat_step:
-        return lax.ppermute(x, "lon", [(i, (i + lon_step) % lons) for i in range(lons)])
-    if not lon_step:
-        return lax.ppermute(x, "lat", [(i, (i + lat_step) % lats) for i in range(lats)])
-    pairs = [
-        (j * lats + i, (j + lon_step) % lons * lats + (i + lat_step) % lats)
-        for j in range(lons)
-        for i in range(lats)
-    ]
-    return lax.ppermute(x, ("lon", "lat"), pairs)
-
-
-def partner(x, axis, stride):
-    return lax.ppermute(x, axis, [(i, i ^ stride) for i in range(lax.axis_size(axis))])
+def shifted(x, axis, step):
+    size = lax.axis_size(axis)
+    return lax.ppermute(x, axis, [(i, (i + step) % size) for i in range(size)])
+
+
+def every_peer(x, axes):
+    return lax.all_to_all(x, axes, 0, 0, tiled=True)
 
 
 def by_cell(x):
@@ -371,91 +429,133 @@
 ):
     second_cells = by_cell(output_second)
     pair = jnp.concatenate((second_cells, by_cell(cotangent_first)), axis=-1)
-    left, right = pair[:, 0:HALF], pair[:, HALF:WC]
-    east = shifted(left, 0, -1)
-    diag = shifted(left, -1, -1)
-    south = shifted(right, -1, 0)
+    south = shifted(pair[0 : WL - 1], "lat", -1)
 
     first_row = lax.axis_index("lat") * WL
     meta = jnp.stack((shifts[0], lax.axis_size("lat") * WL - shifts[0] - first_row))
-    gain = norm_gain.reshape(1, C)
     w_qkv_t = w_qkv.T
 
-    table = pl.pallas_call(
+    table, gain = pl.pallas_call(
         table_kernel,
-        out_shape=jax.ShapeDtypeStruct((16, 16, LANES), f32),
-        in_specs=vmem(1),
-        out_specs=vmem(1)[0],
+        out_shape=(
+            jax.ShapeDtypeStruct((16, 16, LANES), f32),
+            jax.ShapeDtypeStruct((1, C), f32),
+        ),
+        in_specs=vmem(2),
+        out_specs=tuple(vmem(2)),
         scratch_shapes=[pltpu.VMEM((16, WIDE), f32), pltpu.VMEM((ROWS, LANES), f32)],
         compiler_params=params,
         cost_estimate=cost(400_000_000, 1_000_000),
         name="bias_table",
-    )(earth_bias.reshape(2 * HEADS, 1, POS))
+    )(earth_bias.reshape(2 * HEADS, 1, POS), norm_gain.reshape(1, C))
 
     piece = functools.partial(jax.ShapeDtypeStruct, dtype=bf16)
     half_block = (WL, HALF, LEVELS, 2 * C)
-    own, to_east, bias_part = pl.pallas_call(
-        main_kernel,
-        out_shape=(piece(half_block), piece(half_block), piece((4 * HEADS, FOLD))),
-        in_specs=smem() + vmem(9),
-        out_specs=tuple(vmem(3)),
+    near, to_west = pl.pallas_call(
+        frame_kernel,
+        out_shape=(piece(half_block), piece(half_block)),
+        in_specs=smem() + vmem(2),
+        out_specs=tuple(vmem(2)),
+        compiler_params=params,
+        cost_estimate=cost(0, 500_000),
+        name="frame_rows",
+    )(meta, pair, south)
+    east = shifted(to_west, "lon", -1)
+
+    table_chunks = (CHUNKS, DEEP, 4, 128)
+    *attention, bias_part = pl.pallas_call(
+        scores_kernel,
+        out_shape=(
+            piece((2, HEADS, ROWS, LANES)),
+            piece((2, HEADS, ROWS, LANES)),
+            piece((2, C, ROWS)),
+            piece((2, C, ROWS)),
+            piece((2, C, LANES)),
+            piece((2, C, LANES)),
+            piece(table_chunks),
+        ),
+        in_specs=smem() + vmem(7),
+        out_specs=tuple(vmem(7)),
         scratch_shapes=[
             pltpu.VMEM((CELLS, 2 * C), f32),
             pltpu.VMEM((ROWS, LANES), f32),
             pltpu.VMEM((2, ROWS, C), bf16),
             pltpu.VMEM((2, ROWS, C), bf16),
+            pltpu.VMEM((16, 16, LANES), f32),
+            pltpu.VMEM((16, WIDE), f32),
+            pltpu.VMEM((4 * HEADS, FOLD), f32),
+            pltpu.VMEM(table_chunks, f32),
+        ],
+        compiler_params=params,
+        cost_estimate=cost(4_000_000_000, 2_000_000),
+        name="window_scores",
+    )(meta, near, east, gain, w_qkv, w_qkv_t, w_proj, table)
+
+    own, to_south = pl.pallas_call(
+        coeffs_kernel,
+        out_shape=(
+            piece((WL, WC, LEVELS, 2 * C)),
+            piece((WL - 1, WC, LEVELS, 2 * C)),
+        ),
+        in_specs=vmem(7),
+        out_specs=tuple(vmem(2)),
+        scratch_shapes=[
             pltpu.VMEM((2, C, ROWS), bf16),
             pltpu.VMEM((2, C, ROWS), bf16),
             pltpu.VMEM((2, C, LANES), bf16),
             pltpu.VMEM((2, C, LANES), bf16),
-            pltpu.VMEM((2, C, ROWS), bf16),
-            pltpu.VMEM((2, C, ROWS), bf16),
-            pltpu.VMEM((2, C, LANES), bf16),
-            pltpu.VMEM((2, C, LANES), bf16),
-            pltpu.VMEM((16, 16, LANES), f32),
-            pltpu.VMEM((16, WIDE), f32),
-            pltpu.VMEM((4 * HEADS, FOLD), f32),
+            pltpu.VMEM((CELLS, 2 * C), f32),
         ],
         compiler_params=params,
         cost_estimate=cost(4_000_000_000, 2_000_000),
-        name="window_attention",
-    )(meta, right, east, south, diag, gain, w_qkv, w_qkv_t, w_proj, table)
-
-    west = shifted(to_east, 0, 1)
-    corner = shifted(to_east, 1, 1)
-    north = shifted(own, 1, 0)
-
-    steps = [("lon", 1 << bit) for bit in range((lax.axis_size("lon") - 1).bit_length())]
-    steps += [("dp", 1 << bit) for bit in range((lax.axis_size("dp") - 1).bit_length())]
-    for axis, stride in steps[:-1]:
-        other = partner(bias_part, axis, stride)
-        bias_part = (bias_part.astype(f32) + other.astype(f32)).astype(bf16)
+        name="window_coeffs",
+    )(*attention, w_qkv_t)
+    north = shifted(to_south, "lat", 1)
+
+    sums = pl.pallas_call(
+        table_sum_kernel,
+        out_shape=piece((CHUNKS * SAMPLES, DEEP, 4, 128)),
+        in_specs=vmem(1) + [pl.BlockSpec(memory_space=pl.ANY)],
+        out_specs=vmem(1)[0],
+        compiler_params=params,
+        cost_estimate=cost(100_000, 400_000),
+        name="table_sum",
+    )(every_peer(bias_part, "lon"), north)
     bias_grad = pl.pallas_call(
         table_home_kernel,
         out_shape=jax.ShapeDtypeStruct((2 * HEADS, 1, POS), f32),
-        in_specs=vmem(2),
+        in_specs=vmem(1),
         out_specs=vmem(1)[0],
+        scratch_shapes=[pltpu.VMEM((4 * HEADS, FOLD), f32)],
         compiler_params=params,
         cost_estimate=cost(100_000, 400_000),
         name="table_home",
-    )(bias_part, partner(bias_part, *steps[-1]))
+    )(every_peer(sums, ("lon", "dp")))
+
+    near, to_east = pl.pallas_call(
+        unframe_kernel,
+        out_shape=(piece(half_block), piece(half_block)),
+        in_specs=smem() + vmem(2),
+        out_specs=tuple(vmem(2)),
+        compiler_params=params,
+        cost_estimate=cost(0, 500_000),
+        name="home_rows",
+    )(meta, own, north)
+    west = shifted(to_east, "lon", 1)
 
     block = jax.ShapeDtypeStruct((WL, WC, LEVELS, C), bf16)
     input_first, grad_second = pl.pallas_call(
         home_kernel,
         out_shape=(block, block),
-        in_specs=smem() + vmem(9),
+        in_specs=vmem(7),
         out_specs=tuple(vmem(2)),
         scratch_shapes=[pltpu.VMEM((CELLS, 2 * C), f32)],
         compiler_params=params,
         cost_estimate=cost(200_000_000, 2_000_000),
         name="home",
     )(
-        meta,
-        own,
         west,
-        north,
-        corner,
+        near,
         by_cell(output_first),
         second_cells,
         by_cell(cotangent_second),

time: 80 us -> 67.5 us (0.84)
  the two profiles are of different devices: /device:TPU:1 before, /device:TPU:25 now
where the time goes in v2:
time: 67.5 us; the launch traced here: 67.1 us
  starting transfers between devices  21.7 us (32%)
  Pallas kernels  16.8 us (25%)
  blocking collectives  13.1 us (19%)
  waiting for transfers between devices  9.88 us (15%)
  other arithmetic  3.06 us (5%)
  between operations  1.46 us (2%)
  local copies, waits for them, and re-layouts  1.13 us (2%)
    ppermute x4, starting transfers between devices, shifted(): return lax.ppermute(x, axis, [(i, (i + step) % size) for i in range(size)])  16.2 us
    all_to_all x1, blocking collectives, every_peer(): return lax.all_to_all(x, axes, 0, 0, tiled=True)  13.1 us
    ppermute x4, waiting for transfers between devices, shifted(): return lax.ppermute(x, axis, [(i, (i + step) % size) for i in range(size)])  9.88 us
    pallas_call x1, Pallas kernels, local(): pl.pallas_call(scores_kernel, out_shape=(piece((2, HEADS, ROWS, LANES)),...  8.52 us
    all_to_all x1, starting transfers between devices, every_peer(): return lax.all_to_all(x, axes, 0, 0, tiled=True)  5.54 us
    pallas_call x1, Pallas kernels, local(): pl.pallas_call(coeffs_kernel, out_shape=(piece((WL, WC, LEVELS, 2 * C)),...  3.02 us
    concatenate x2, other arithmetic, local(): pair = jnp.concatenate((second_cells, by_cell(cotangent_first)), axis=-1)  2.34 us
    pallas_call x1, Pallas kernels, local(): pl.pallas_call(home_kernel, out_shape=(block, block), in_specs=vmem(7), o...  1.58 us
  transfers between devices with their start and end apart: 5, of which 2 were waited for; matrix products, arithmetic and copies ran while one was open for 4% of the time, Pallas kernels for 5%

profile of v2, /device:TPU:25, one launch (start us, length us, event | category | flops | bytes accessed | tf_op | source)
XLA Modules:
  0.0 67.1 jit_solution(5921318852435926126)
XLA Ops:
  0.6 0.0 copy-start.1
  0.6 0.0 copy-start.5
  0.7 0.0 copy-start.6
  0.7 0.0 copy-start.4
  0.7 1.2 %fusion = bf16[5,12,4,384]{3,2,1,0:T(4,128)(2,1)S(1)} fusion(bf16[6,12,4,192]{3,2,1,0:T(4,128)(2,1)} %bitcast.25, bf16[6,12,4,192]{3,2,1,0:T(4,128)(2,1)} %bitcast.34), kind=kLoop, calls=%fused_computation.3 | loop fusion | flops 368640 | bytes 405504 | tf_op jit(solution)/shard_map/concatenate | solution.py:431
  1.9 0.7 %collective-permute-start = (bf16[5,12,4,384]{3,2,1,0:T(4,128)(2,1)S(1)}, bf16[5,12,4,384]{3,2,1,0:T(4,128)(2,1)S(1)}, u32[]{:S(2)}, u32[]{:S(2)}) collective-permute-start(bf16[5,12,4,384]{3,2,1,0:T(4,128)(2,1)S(1)} %fusion), channel_id=1, source_target_pairs={{0,30},{2,0},{4,2},{6,4},{8,6},{10,8},{12,10},{14,12},{16,14},{18,... | collective-permute-start | bytes 552968 | tf_op jit(solution)/shard_map/ppermute | solution.py:407
  3.2 0.7 %pad_add_fusion.meta_ref = s32[2]{0:T(128)S(1)} fusion(s32[1]{0:T(128)} %bitcast.1, s32[1]{0:T(128)} %bitcast.40), kind=kLoop, calls=%fused_computation.4 | loop fusion | flops 2 | bytes 16 | tf_op jit(solution)/shard_map/stack | solution.py:435
  3.9 1.2 %pad_maximum_fusion.own_ref = bf16[6,12,4,384]{3,2,1,0:T(4,128)(2,1)S(1)} fusion(bf16[6,12,4,192]{3,2,1,0:T(4,128)(2,1)} %bitcast.35, bf16[6,12,4,192]{3,2,1,0:T(4,128)(2,1)} %bitcast.26), kind=kLoop, calls=%fused_computation.1 | loop fusion | flops 442368 | bytes 442368 | tf_op jit(solution)/shard_map/concatenate | solution.py:431
  5.1 3.1 %collective-permute-done.other_ref = bf16[5,12,4,384]{3,2,1,0:T(4,128)(2,1)S(1)} collective-permute-done((bf16[5,12,4,384]{3,2,1,0:T(4,128)(2,1)S(1)}, bf16[5,12,4,384]{3,2,1,0:T(4,128)(2,1)S(1)}, u32[]{:S(2)}, u32[]{:S(2)}) %collective-permute-start) | collective-permute-done | bytes 184352 | tf_op jit(solution)/shard_map/ppermute | solution.py:407
  8.2 0.6 frame_rows.1
  8.8 11.6 %collective-permute-start.1 = (bf16[6,6,4,384]{3,2,1,0:T(4,128)(2,1)S(1)}, bf16[6,6,4,384]{3,2,1,0:T(4,128)(2,1)S(1)}, u32[]{:S(2)}, u32[]{:S(2)}) collective-permute-start(bf16[6,6,4,384]{3,2,1,0:T(4,128)(2,1)S(1)} %get-tuple-element.21), channel_id=1, source_target_pairs={{0,480},{32,0},{64,32},{96,64},{128,96},{160,128},{192,160},{224,1... | collective-permute-start | bytes 331784 | tf_op jit(solution)/shard_map/ppermute | solution.py:407
  20.4 1.1 %copy.12 = bf16[192,576]{0,1:T(8,128)(2,1)S(1)} copy(bf16[192,576]{1,0:T(8,128)(2,1)} %w_qkv_ref.1) | data formatting | bytes 442368 | tf_op args[5]
  21.5 0.0 copy-done.5
  21.5 0.0 copy-done.6
  21.5 0.9 %bias_table.1 = (f32[16,16,384]{2,1,0:T(8,128)S(1)}, f32[1,192]{1,0:T(1,128)S(1)}) custom-call(f32[12,1,3312]{2,1,0:T(1,128)S(1)} %bitcast.32, f32[1,192]{1,0:T(1,128)S(1)} %bitcast.33), custom_call_target="tpu_custom_call" | custom-call | flops 400000000 | bytes 1000000 | tf_op jit(solution)/shard_map/bias_table/pallas_call | solution.py:438
  22.4 0.0 collective-permute-done.1.east_ref
  22.4 0.0 copy-done.1
  22.4 0.0 copy-done.4
  22.5 8.5 %window_scores.1 = (bf16[2,6,192,384]{3,2,1,0:T(8,128)(2,1)S(1)}, bf16[2,6,192,384]{3,2,1,0:T(8,128)(2,1)S(1)}, bf16[2,192,192]{2,1,0:T(8,128)(2,1)S(1)}, bf16[2...) custom-call(s32[2]{0:T(128)S(1)} %pad_add_fusion.meta_ref, ...), custom_call_target="tpu_custom_call" | custom-call | flops 4000000000 | bytes 2000000 | tf_op jit(solution)/shard_map/window_scores/pallas_call | solution.py:466
  31.0 0.0 copy-start
  31.0 0.0 copy-start.2
  31.0 0.0 copy-start.3
  31.0 3.0 %window_coeffs.1 = (bf16[6,12,4,384]{3,2,1,0:T(4,128)(2,1)S(1)}, bf16[5,12,4,384]{3,2,1,0:T(4,128)(2,1)S(1)}) custom-call(bf16[2,6,192,384]{3,2,1,0:T(8,128)(2,1)S(1)} %get-tuple-element.24.weights_ref, bf16[2,6,192,384]{3,2,1,0:T(8,128)(2,1)S(1)} %get-tuple-element.25.grads_ref, bf16[2,192,192]{2,1,0:T(8,128)(2,1)S(1)} %get-tuple-element.26.queries_t, ...), custom_call_target="tpu_custom_call" | custom-call | flops 4000000000 | bytes 2000000 | tf_op jit(solution)/shard_map/window_coeffs/pallas_call | solution.py:494
  34.0 0.8 %collective-permute-start.2 = (bf16[5,12,4,384]{3,2,1,0:T(4,128)(2,1)S(1)}, bf16[5,12,4,384]{3,2,1,0:T(4,128)(2,1)S(1)}, u32[]{:S(2)}, u32[]{:S(2)}) collective-permute-start(bf16[5,12,4,384]{3,2,1,0:T(4,128)(2,1)S(1)} %get-tuple-element.31), channel_id=1, source_target_pairs={{0,2},{2,4},{4,6},{6,8},{8,10},{10,12},{12,14},{14,16},{16,18},{18... | collective-permute-start | bytes 552968 | tf_op jit(solution)/shard_map/ppermute | solution.py:407
  34.8 13.1 %all_to_all.10.parts_ref = bf16[16,5,4,128]{3,2,1,0:T(4,128)(2,1)S(1)} all-to-all(bf16[16,5,4,128]{3,2,1,0:T(4,128)(2,1)S(1)} %get-tuple-element.36), channel_id=1, replica_groups=mesh['lon'=16,'lat'=16,'dp'=2] {'lon'}, dimensions={0} | all-to-all | bytes 163840 | tf_op jit(solution)/shard_map/all_to_all | solution.py:411
  47.9 0.0 collective-permute-done.2.other_ref.after_ref
  47.9 0.7 %table_sum.1 = bf16[32,5,4,128]{3,2,1,0:T(4,128)(2,1)} custom-call(bf16[16,5,4,128]{3,2,1,0:T(4,128)(2,1)S(1)} %all_to_all.10.parts_ref, bf16[5,12,4,384]{3,2,1,0:T(4,128)(2,1)S(1)} %collective-permute-done.2.other_ref.after_ref), custom_call_target="tpu_custom_call" | custom-call | flops 100000 | bytes 400000 | tf_op jit(solution)/shard_map/table_sum/pallas_call | solution.py:515
  48.6 5.5 %all-to-all-start.1 = ((bf16[32,5,4,128]{3,2,1,0:T(4,128)(2,1)}), bf16[32,5,4,128]{3,2,1,0:T(4,128)(2,1)S(1)}, u32[]{:S(2)}, u32[]{:S(2)}) async-start(bf16[32,5,4,128]{3,2,1,0:T(4,128)(2,1)} %table_sum.1), calls=%async_computation.1 | async-start | bytes 327680 | tf_op jit(solution)/shard_map/all_to_all | solution.py:411
  54.2 0.6 home_rows.1
  54.8 3.1 %collective-permute-start.3 = (bf16[6,6,4,384]{3,2,1,0:T(4,128)(2,1)S(1)}, bf16[6,6,4,384]{3,2,1,0:T(4,128)(2,1)S(1)}, u32[]{:S(2)}, u32[]{:S(2)}) collective-permute-start(bf16[6,6,4,384]{3,2,1,0:T(4,128)(2,1)S(1)} %get-tuple-element.32), channel_id=1, source_target_pairs={{0,32},{32,64},{64,96},{96,128},{128,160},{160,192},{192,224},{224... | collective-permute-start | bytes 331784 | tf_op jit(solution)/shard_map/ppermute | solution.py:407
  58.0 6.8 %collective-permute-done.3.west_ref = bf16[6,6,4,384]{3,2,1,0:T(4,128)(2,1)S(1)} collective-permute-done((bf16[6,6,4,384]{3,2,1,0:T(4,128)(2,1)S(1)}, bf16[6,6,4,384]{3,2,1,0:T(4,128)(2,1)S(1)}, u32[]{:S(2)}, u32[]{:S(2)}) %collective-permute-start.3) | collective-permute-done | bytes 110624 | tf_op jit(solution)/shard_map/ppermute | solution.py:407
  64.8 0.0 copy-done
  64.8 0.0 copy-done.2
  64.8 0.0 copy-done.3
  64.8 1.6 %home.1 = (bf16[6,12,4,192]{3,2,1,0:T(4,128)(2,1)}, bf16[6,12,4,192]{3,2,1,0:T(4,128)(2,1)}) custom-call(bf16[6,6,4,384]{3,2,1,0:T(4,128)(2,1)S(1)} %collective-permute-done.3.west_ref, bf16[6,6,4,384]{3,2,1,0:T(4,128)(2,1)S(1)} %get-tuple-element.33.near_ref, bf16[6,12,4,192]{3,2,1,0:T(4,128)(2,1)S(1)} %bitcast.30, bf16[6,12,4,192]{3,2,1,0:T(4,128)(2,1)S(1)} %bitcast.27, ...), custom_call_target="tpu_custom_call" | custom-call | flops 200000000 | bytes 2000000 | tf_op jit(solution)/shard_map/home/pallas_call | solution.py:547
  66.4 0.0 all-to-all-done.1.sums_ref
  66.4 0.7 %table_home.1 = f32[12,1,3312]{2,1,0:T(1,128)} custom-call(bf16[32,5,4,128]{3,2,1,0:T(4,128)(2,1)S(1)} %all-to-all-done.1.sums_ref), custom_call_target="tpu_custom_call" | custom-call | flops 100000 | bytes 400000 | tf_op jit(solution)/shard_map/table_home/pallas_call | solution.py:524
Async XLA Ops:
  0.6 21.8 %copy-start.1 = (bf16[192,576]{1,0:T(8,128)(2,1)S(1)}, bf16[192,576]{1,0:T(8,128)(2,1)}, u32[]{:S(2)}) copy-start(bf16[192,576]{1,0:T(8,128)(2,1)} %w_qkv_ref.1) | copy-start | bytes 663556
  0.6 20.9 %copy-start.5 = (f32[2,1,6,3312]{3,1,2,0:T(1,128)S(1)}, f32[2,1,6,3312]{3,1,2,0:T(1,128)}, u32[]{:S(2)}) copy-start(f32[2,1,6,3312]{3,1,2,0:T(1,128)} %param.17) | copy-start | bytes 476932
  0.7 20.9 %copy-start.6 = (f32[192]{0:T(256)S(1)}, f32[192]{0:T(256)}, u32[]{:S(2)}) copy-start(f32[192]{0:T(256)} %param.14) | copy-start | bytes 2308
  0.7 21.8 %copy-start.4 = (bf16[192,192]{1,0:T(8,128)(2,1)S(1)}, bf16[192,192]{1,0:T(8,128)(2,1)}, u32[]{:S(2)}) copy-start(bf16[192,192]{1,0:T(8,128)(2,1)} %w_proj_ref.3) | copy-start | bytes 221188
  1.9 6.3 %collective-permute-start = (bf16[5,12,4,384]{3,2,1,0:T(4,128)(2,1)S(1)}, bf16[5,12,4,384]{3,2,1,0:T(4,128)(2,1)S(1)}, u32[]{:S(2)}, u32[]{:S(2)}) collective-permute-start(bf16[5,12,4,384]{3,2,1,0:T(4,128)(2,1)S(1)} %fusion), channel_id=1, source_target_pairs={{0,30},{2,0},{4,2},{6,4},{8,6},{10,8},{12,10},{14,12},{16,14},{18,... | collective-permute-start | bytes 552968 | tf_op jit(solution)/shard_map/ppermute | solution.py:407
  8.8 13.6 %collective-permute-start.1 = (bf16[6,6,4,384]{3,2,1,0:T(4,128)(2,1)S(1)}, bf16[6,6,4,384]{3,2,1,0:T(4,128)(2,1)S(1)}, u32[]{:S(2)}, u32[]{:S(2)}) collective-permute-start(bf16[6,6,4,384]{3,2,1,0:T(4,128)(2,1)S(1)} %get-tuple-element.21), channel_id=1, source_target_pairs={{0,480},{32,0},{64,32},{96,64},{128,96},{160,128},{192,160},{224,1... | collective-permute-start | bytes 331784 | tf_op jit(solution)/shard_map/ppermute | solution.py:407
  31.0 33.8 %copy-start = (bf16[1,4,6,12,192]{4,1,3,2,0:T(4,128)(2,1)S(1)}, bf16[1,4,6,12,192]{4,1,3,2,0:T(4,128)(2,1)}, u32[]{:S(2)}) copy-start(bf16[1,4,6,12,192]{4,1,3,2,0:T(4,128)(2,1)} %param.11) | copy-start | bytes 331780
  31.0 33.8 %copy-start.2 = (bf16[1,4,6,12,192]{4,1,3,2,0:T(4,128)(2,1)S(1)}, bf16[1,4,6,12,192]{4,1,3,2,0:T(4,128)(2,1)}, u32[]{:S(2)}) copy-start(bf16[1,4,6,12,192]{4,1,3,2,0:T(4,128)(2,1)} %param.10) | copy-start | bytes 331780
  31.0 33.8 %copy-start.3 = (bf16[1,4,6,12,192]{4,1,3,2,0:T(4,128)(2,1)S(1)}, bf16[1,4,6,12,192]{4,1,3,2,0:T(4,128)(2,1)}, u32[]{:S(2)}) copy-start(bf16[1,4,6,12,192]{4,1,3,2,0:T(4,128)(2,1)} %param.13) | copy-start | bytes 331780
  34.0 13.9 %collective-permute-start.2 = (bf16[5,12,4,384]{3,2,1,0:T(4,128)(2,1)S(1)}, bf16[5,12,4,384]{3,2,1,0:T(4,128)(2,1)S(1)}, u32[]{:S(2)}, u32[]{:S(2)}) collective-permute-start(bf16[5,12,4,384]{3,2,1,0:T(4,128)(2,1)S(1)} %get-tuple-element.31), channel_id=1, source_target_pairs={{0,2},{2,4},{4,6},{6,8},{8,10},{10,12},{12,14},{14,16},{16,18},{18... | collective-permute-start | bytes 552968 | tf_op jit(solution)/shard_map/ppermute | solution.py:407
  48.6 17.7 %all-to-all-start.1 = ((bf16[32,5,4,128]{3,2,1,0:T(4,128)(2,1)}), bf16[32,5,4,128]{3,2,1,0:T(4,128)(2,1)S(1)}, u32[]{:S(2)}, u32[]{:S(2)}) async-start(bf16[32,5,4,128]{3,2,1,0:T(4,128)(2,1)} %table_sum.1), calls=%async_computation.1 | async-start | bytes 327680 | tf_op jit(solution)/shard_map/all_to_all | solution.py:411
  54.8 9.9 %collective-permute-start.3 = (bf16[6,6,4,384]{3,2,1,0:T(4,128)(2,1)S(1)}, bf16[6,6,4,384]{3,2,1,0:T(4,128)(2,1)S(1)}, u32[]{:S(2)}, u32[]{:S(2)}) collective-permute-start(bf16[6,6,4,384]{3,2,1,0:T(4,128)(2,1)S(1)} %get-tuple-element.32), channel_id=1, source_target_pairs={{0,32},{32,64},{64,96},{96,128},{128,160},{160,192},{192,224},{224... | collective-permute-start | bytes 331784 | tf_op jit(solution)/shard_map/ppermute | solution.py:407

commit v3 on v1

v3 whole, which is shorter than its diff:
```python
import functools

import jax
import jax.numpy as jnp
from jax import lax
from jax.experimental import pallas as pl
from jax.experimental.pallas import tpu as pltpu
from jax.sharding import PartitionSpec as P

C = 192
HEADS = 6
HEAD = 32
LEVELS = 4
WL = 6
WC = 12
HALF = 6
POS = 3312
CHUNK = 138
SPAN = 23
GROUPS = 12
ROWS = 144
LANES = 256
REACH = 384
CELLS = 288
PITCH = 16
WIDE = 3584
FOLD = 1664
TILES = 156
CHUNKS = 32
DEEP = 5

norm_eps = 1e-05
mask_fill = -1e30
scale = HEAD**-0.5
vmem_bytes = 20 * 1024 * 1024

f32 = jnp.float32
bf16 = jnp.bfloat16


def iota(shape, dim):
    return lax.broadcasted_iota(jnp.int32, shape, dim)


def mm(a, b):
    return lax.dot_general(a, b, (((1,), (0,)), ((), ())), preferred_element_type=f32)


def mm_t(a, b):
    return lax.dot_general(a, b, (((1,), (1,)), ((), ())), preferred_element_type=f32)


def parts(index, size):
    return lax.div(index, jnp.int32(size)), lax.rem(index, jnp.int32(size))


def picks(index, count, dim):
    shape = (index.shape[0], count) if dim == 0 else (count, index.shape[1])
    return jnp.where(iota(shape, 1 - dim) == index, 1.0, 0.0).astype(bf16)


def line(size, dim):
    return iota((size, 1) if dim == 0 else (1, size), dim)


def query_cells(a, dim):
    column, group = parts(line(ROWS, dim), GROUPS)
    level, row = parts(group, WL)
    return (row * WC + column) * LEVELS + 2 * a + level


def key_cells(a, dim):
    group, column = parts(line(LANES, dim), PITCH)
    level, row = parts(group, WL)
    return jnp.where(
        (group < GROUPS) & (column < WC), (row * WC + column) * LEVELS + 2 * a + level, -1
    )


def spread_entries(level, part, dim):
    group, place = parts(line(LANES, dim), PITCH)
    group = group - level * WL - part
    count = SPAN - PITCH if part else PITCH
    return jnp.where(
        (group >= 0) & (group < WL) & (place < count),
        group * SPAN + place + part * PITCH,
        -1,
    )


def chunk_place(group, level):
    start = (((group // WL) * 2 + level) * WL + group % WL) * CHUNK
    return start // 128 * 128, start % 128


def table_kernel(
    shifts_ref, bias_ref, gain_ref, expanded_out, gain_out, wide, pieces, tables, mask
):
    gain_out[...] = gain_ref[...]
    wide[...] = jnp.zeros(wide.shape, f32)
    for a in range(2):
        for h in range(HEADS):
            wide[a * 8 + h : a * 8 + h + 1, 0:POS] = bias_ref[a * HEADS + h]
    totals = [jnp.zeros((GROUPS * PITCH, LANES), f32) for _ in range(2)]
    for level in range(2):
        for group in range(GROUPS):
            tile, shift = chunk_place(group, level)
            piece = wide[:, tile : tile + REACH]
            if shift:
                piece = pltpu.roll(piece, REACH - shift, 1)
            pieces[group * PITCH : (group + 1) * PITCH, :] = piece[:, 0:LANES]
        spreads = [picks(spread_entries(level, part, 1), LANES, 1) for part in range(2)]
        rest = pieces[...]
        for _ in range(3):
            top = rest.astype(bf16)
            for part in range(2):
                totals[part] = totals[part] + mm(top, spreads[part])
            rest = rest - top.astype(f32)
    for part in range(2):
        pieces[...] = totals[part]
        for group in range(GROUPS):
            for a in range(2):
                for h in range(HEADS):
                    row = group * PITCH + a * 8 + h
                    tables[part, a * HEADS + h, group : group + 1, :] = pieces[row : row + 1, :]

    first_row = lax.axis_index("lat") * WL
    edge = lax.axis_size("lat") * WL - shifts_ref[0] - first_row
    query_row = parts(line(GROUPS, 0), WL)[1]
    key_group, key_column = parts(line(LANES, 1), PITCH)
    key_row = parts(key_group, WL)[1]
    query_id = jnp.where(query_row >= edge, 1, 0)
    valid = (key_group < GROUPS) & (key_column < WC)
    key_id = jnp.where(valid, jnp.where(key_row >= edge, 1, 0), 2)
    mask[...] = jnp.where(query_id == key_id, 0.0, mask_fill)

    def expand(index, carry):
        first, second = tables[0, index], tables[1, index]
        for c in range(WC):
            shift = (c - WC + 1) % LANES
            low = pltpu.roll(first, shift, 1) if shift else first
            high = pltpu.roll(second, shift, 1) if shift else second
            bias = jnp.where(key_column + (WC - 1 - c) < PITCH, low, high)
            expanded_out[index, c * GROUPS : (c + 1) * GROUPS, :] = bias + mask[...]
        return carry

    lax.fori_loop(0, 2 * HEADS, expand, 0)


def unframe_kernel(shifts_ref, own_ref, other_ref, near_out, send_out):
    for r in range(WL):
        place = r - shifts_ref[0]

        @pl.when(place >= 0)
        def _():
            near_out[r] = own_ref[place, 0:HALF]
            send_out[r] = own_ref[place, HALF:WC]

        @pl.when(place < 0)
        def _():
            near_out[r] = other_ref[place + WL - 1, 0:HALF]
            send_out[r] = other_ref[place + WL - 1, HALF:WC]


def join_halves(left_ref, right_ref, joined):
    half = HALF * LEVELS
    for r in range(WL):
        start = 2 * r * half
        joined[start : start + half, :] = left_ref[r].astype(f32).reshape(half, 2 * C)
        joined[start + half : start + 2 * half, :] = (
            right_ref[r].astype(f32).reshape(half, 2 * C)
        )


def attention_kernel(
    shifts_ref,
    own_ref,
    east_ref,
    south_ref,
    diag_ref,
    gain_ref,
    w_qkv_ref,
    w_qkv_t_ref,
    w_proj_ref,
    bias_ref,
    own_out,
    south_out,
    bias_out,
    framed,
    queries,
    ups,
    queries_t,
    ups_t,
    keys_t,
    values_t,
    attended_t,
    grad_query_t,
    grad_key_t,
    grad_value_t,
    table_grad,
    wide,
    folds,
    packed_table,
):
    half = HALF * LEVELS
    for r in range(WL):
        place = r + shifts_ref[0]
        left = slice(2 * r * half, (2 * r + 1) * half)
        right = slice((2 * r + 1) * half, (2 * r + 2) * half)

        @pl.when(place < WL)
        def _():
            framed[left, :] = own_ref[place].astype(f32).reshape(half, 2 * C)
            framed[right, :] = east_ref[place].astype(f32).reshape(half, 2 * C)

        @pl.when(place >= WL)
        def _():
            framed[left, :] = south_ref[place - WL].astype(f32).reshape(half, 2 * C)
            framed[right, :] = diag_ref[place - WL].astype(f32).reshape(half, 2 * C)

    cells = framed[:, 0:C]
    cotangent = framed[:, C : 2 * C].astype(bf16)
    centered = cells - jnp.mean(cells, axis=-1, keepdims=True)
    inverse = lax.rsqrt(jnp.mean(centered * centered, axis=-1, keepdims=True) + norm_eps)
    hidden = (centered * inverse * gain_ref[...]).astype(bf16)

    w_proj = w_proj_ref[...]
    for a in range(2):
        to_queries = picks(query_cells(a, 0), CELLS, 0)
        turned = mm(to_queries, hidden).astype(bf16)
        turned_cot = mm(to_queries, cotangent).astype(bf16)
        spaced = mm(picks(key_cells(a, 0), CELLS, 0), hidden).astype(bf16)
        queries[a] = mm(turned, w_qkv_ref[:, 0:C]).astype(bf16)
        queries_t[a] = mm_t(w_qkv_t_ref[0:C, :], turned).astype(bf16)
        keys_t[a] = mm_t(w_qkv_t_ref[C : 2 * C, :], spaced).astype(bf16)
        values_t[a] = mm_t(w_qkv_t_ref[2 * C : 3 * C, :], spaced).astype(bf16)
        ups[a] = mm_t(turned_cot, w_proj).astype(bf16)
        ups_t[a] = mm_t(w_proj, turned_cot).astype(bf16)

    table_grad[...] = jnp.zeros(table_grad.shape, f32)
    key_column = parts(line(LANES, 1), PITCH)[1]

    def one_head(h, carry):
        features = pl.ds(pl.multiple_of(h * HEAD, HEAD), HEAD)
        chosen = parts(line(C, 1), HEAD)[0] == h
        for a in range(2):
            query = jnp.where(chosen, queries[a], jnp.zeros((), bf16))
            up = jnp.where(chosen, ups[a], jnp.zeros((), bf16))
            scores = mm(query, keys_t[a]) * scale + bias_ref[a * HEADS + h]
            exponent = jnp.exp(scores - jnp.max(scores, axis=-1, keepdims=True))
            weights = exponent * (1.0 / jnp.sum(exponent, axis=-1, keepdims=True))
            weights_low = weights.astype(bf16)
            grad_weights = mm(up, values_t[a])
            row_dot = jnp.sum(weights * grad_weights, axis=-1, keepdims=True)
            grad_scores = weights * (grad_weights - row_dot)
            grad_low = grad_scores.astype(bf16)
            attended_t[a, features, :] = mm_t(values_t[a, features, :], weights_low).astype(bf16)
            grad_value_t[a, features, :] = mm(ups_t[a, features, :], weights_low).astype(bf16)
            grad_query_t[a, features, :] = (
                mm_t(keys_t[a, features, :], grad_low) * scale
            ).astype(bf16)
            grad_key_t[a, features, :] = (
                mm(queries_t[a, features, :], grad_low) * scale
            ).astype(bf16)
            low = jnp.zeros((GROUPS, LANES), f32)
            high = jnp.zeros((GROUPS, LANES), f32)
            for c in range(WC):
                shift = WC - 1 - c
                turned_grad = grad_scores[c * GROUPS : (c + 1) * GROUPS]
                if shift:
                    turned_grad = pltpu.roll(turned_grad, shift, 1)
                kept = key_column >= shift
                low = low + jnp.where(kept, turned_grad, 0.0)
                high = high + jnp.where(kept, 0.0, turned_grad)
            table_grad[0, a * 8 + h, 0:GROUPS] = low
            table_grad[1, a * 8 + h, 0:GROUPS] = high
        return carry

    lax.fori_loop(0, HEADS, one_head, 0)

    group, place = parts(line(GROUPS * PITCH, 0), PITCH)
    to_groups = picks(place * PITCH + group, 256, 0)
    by_group = [
        mm(to_groups, table_grad[part].reshape(256, LANES).astype(bf16)).astype(bf16)
        for part in range(2)
    ]
    wide[...] = jnp.zeros(wide.shape, f32)
    for level in range(2):
        packed = sum(
            mm(by_group[part], picks(spread_entries(level, part, 0), REACH, 0))
            for part in range(2)
        )
        for group in range(GROUPS):
            tile, turn = chunk_place(group, level)
            piece = packed[group * PITCH : (group + 1) * PITCH]
            if turn:
                piece = pltpu.roll(piece, turn, 1)
            wide[:, tile : tile + REACH] += piece
    packed_table[...] = jnp.zeros(packed_table.shape, f32)
    for side in range(2):
        for a in range(2):
            start = (2 * side + a) * HEADS
            folds[start : start + HEADS, :] = wide[
                a * 8 : a * 8 + HEADS, side * FOLD : (side + 1) * FOLD
            ]
    for tile in range(TILES):
        chunk, slot, fold_rows, fold_lanes = tile_place(tile)
        packed_table[chunk, slot] = folds[fold_rows, fold_lanes]
    bias_out[...] = packed_table[...].astype(bf16)

    attended = jnp.zeros((CELLS, C), f32)
    coeffs = [jnp.zeros((CELLS, C), f32) for _ in range(3)]
    for a in range(2):
        from_queries = picks(query_cells(a, 1), CELLS, 1)
        from_keys = picks(key_cells(a, 1), CELLS, 1)
        attended = attended + mm_t(from_queries, attended_t[a])
        coeffs[0] = coeffs[0] + mm_t(from_queries, grad_query_t[a])
        coeffs[1] = coeffs[1] + mm_t(from_keys, grad_key_t[a])
        coeffs[2] = coeffs[2] + mm_t(from_keys, grad_value_t[a])
    framed[:, 0:C] = attended
    framed[:, C : 2 * C] = sum(
        mm(coeffs[part].astype(bf16), w_qkv_t_ref[part * C : (part + 1) * C, :])
        for part in range(3)
    )
    row_cells = WC * LEVELS
    for r in range(WL):
        row = framed[r * row_cells : (r + 1) * row_cells, :]
        row = row.reshape(WC, LEVELS, 2 * C).astype(bf16)
        own_out[r] = row
        if r:
            south_out[r - 1] = row


def home_kernel(
    west_ref,
    near_ref,
    output_first_ref,
    output_second_ref,
    cotangent_second_ref,
    gain_ref,
    w_proj_ref,
    input_first_out,
    grad_second_out,
    placed,
):
    join_halves(west_ref, near_ref, placed)
    shape = (WL, WC, LEVELS, C)
    mixed = mm(placed[:, 0:C].astype(bf16), w_proj_ref[...])
    first = output_first_ref[...].astype(f32).reshape(CELLS, C)
    input_first_out[...] = (first - mixed).reshape(shape).astype(bf16)

    cells = output_second_ref[...].astype(f32).reshape(CELLS, C)
    centered = cells - jnp.mean(cells, axis=-1, keepdims=True)
    inverse = lax.rsqrt(jnp.mean(centered * centered, axis=-1, keepdims=True) + norm_eps)
    normed = centered * inverse
    scaled = placed[:, C : 2 * C] * gain_ref[...]
    backward = inverse * (
        scaled
        - jnp.mean(scaled, axis=-1, keepdims=True)
        - normed * jnp.mean(scaled * normed, axis=-1, keepdims=True)
    )
    second = cotangent_second_ref[...].astype(f32).reshape(CELLS, C)
    grad_second_out[...] = (second + backward).reshape(shape).astype(bf16)


def tile_place(tile):
    chunk, slot = divmod(tile, DEEP)
    block, column = divmod(tile, FOLD // 128)
    return (
        chunk,
        slot,
        slice(block * 2, block * 2 + 2),
        slice(column * 128, column * 128 + 128),
    )


def table_sum_kernel(parts_ref, after_ref, sums_out):
    total = jnp.sum(parts_ref[...].astype(f32), axis=0).astype(bf16)
    for peer in range(CHUNKS):
        sums_out[peer] = total


def table_home_kernel(sums_ref, table_out, folds):
    for tile in range(TILES):
        chunk, slot, fold_rows, fold_lanes = tile_place(tile)
        folds[fold_rows, fold_lanes] = sums_ref[chunk, slot].astype(f32)
    rows = 2 * HEADS
    for row in range(rows):
        table_out[row, :, 0:FOLD] = folds[row : row + 1]
        table_out[row, :, FOLD:POS] = folds[rows + row : rows + row + 1, 0 : POS - FOLD]


def vmem(count):
    return [pl.BlockSpec(memory_space=pltpu.VMEM)] * count


def smem():
    return [pl.BlockSpec(memory_space=pltpu.SMEM)]


params = pltpu.CompilerParams(vmem_limit_bytes=vmem_bytes)


def cost(flops, moved):
    return pl.CostEstimate(flops=flops, bytes_accessed=moved, transcendentals=0)


def shifted(x, axis, step):
    size = lax.axis_size(axis)
    return lax.ppermute(x, axis, [(i, (i + step) % size) for i in range(size)])


def from_diagonal(x):
    lons, lats = lax.axis_size("lon"), lax.axis_size("lat")
    pairs = [
        (i * lats + j, (i - 1) % lons * lats + (j - 1) % lats)
        for i in range(lons)
        for j in range(lats)
    ]
    return lax.ppermute(x, ("lon", "lat"), pairs)


def every_peer(x):
    return lax.all_to_all(x, ("lon", "dp"), 0, 0, tiled=True)


def by_cell(x):
    return x[0].transpose(1, 2, 0, 3)


def local(
    output_first,
    output_second,
    cotangent_first,
    cotangent_second,
    norm_gain,
    w_qkv,
    w_proj,
    earth_bias,
    shifts,
    region,
):
    second_cells = by_cell(output_second)
    pair = jnp.concatenate((second_cells, by_cell(cotangent_first)), axis=-1)
    left, right = pair[:, 0:HALF], pair[:, HALF:WC]
    east = shifted(left, "lon", -1)
    diag = from_diagonal(left)
    south = shifted(right, "lat", -1)

    w_qkv_t = w_qkv.T

    bias, gain = pl.pallas_call(
        table_kernel,
        out_shape=(
            jax.ShapeDtypeStruct((2 * HEADS, ROWS, LANES), f32),
            jax.ShapeDtypeStruct((1, C), f32),
        ),
        in_specs=smem() + vmem(2),
        out_specs=tuple(vmem(2)),
        scratch_shapes=[
            pltpu.VMEM((16, WIDE), f32),
            pltpu.VMEM((GROUPS * PITCH, LANES), f32),
            pltpu.VMEM((2, 2 * HEADS, GROUPS, LANES), f32),
            pltpu.VMEM((GROUPS, LANES), f32),
        ],
        compiler_params=params,
        cost_estimate=cost(400_000_000, 2_000_000),
        name="bias_table",
    )(shifts, earth_bias.reshape(2 * HEADS, 1, POS), norm_gain.reshape(1, C))

    piece = functools.partial(jax.ShapeDtypeStruct, dtype=bf16)
    table_chunks = (CHUNKS, DEEP, 2, 128)
    own, to_south, bias_part = pl.pallas_call(
        attention_kernel,
        out_shape=(
            piece((WL, WC, LEVELS, 2 * C)),
            piece((WL - 1, WC, LEVELS, 2 * C)),
            piece(table_chunks),
        ),
        in_specs=smem() + vmem(9),
        out_specs=tuple(vmem(3)),
        scratch_shapes=[
            pltpu.VMEM((CELLS, 2 * C), f32),
            pltpu.VMEM((2, ROWS, C), bf16),
            pltpu.VMEM((2, ROWS, C), bf16),
            pltpu.VMEM((2, C, ROWS), bf16),
            pltpu.VMEM((2, C, ROWS), bf16),
            pltpu.VMEM((2, C, LANES), bf16),
            pltpu.VMEM((2, C, LANES), bf16),
            pltpu.VMEM((2, C, ROWS), bf16),
            pltpu.VMEM((2, C, ROWS), bf16),
            pltpu.VMEM((2, C, LANES), bf16),
            pltpu.VMEM((2, C, LANES), bf16),
            pltpu.VMEM((2, 16, 16, LANES), f32),
            pltpu.VMEM((16, WIDE), f32),
            pltpu.VMEM((4 * HEADS, FOLD), f32),
            pltpu.VMEM(table_chunks, f32),
        ],
        compiler_params=params,
        cost_estimate=cost(4_000_000_000, 2_000_000),
        name="window_attention",
    )(shifts, right, east, south, diag, gain, w_qkv, w_qkv_t, w_proj, bias)
    north = shifted(to_south, "lat", 1)

    half_block = (WL, HALF, LEVELS, 2 * C)
    near, to_east = pl.pallas_call(
        unframe_kernel,
        out_shape=(piece(half_block), piece(half_block)),
        in_specs=smem() + vmem(2),
        out_specs=tuple(vmem(2)),
        compiler_params=params,
        cost_estimate=cost(20_000_000_000, 500_000),
        name="home_rows",
    )(shifts, own, north)
    west = shifted(to_east, "lon", 1)

    sums = pl.pallas_call(
        table_sum_kernel,
        out_shape=piece(table_chunks),
        in_specs=vmem(1) + [pl.BlockSpec(memory_space=pl.ANY)],
        out_specs=vmem(1)[0],
        compiler_params=params,
        cost_estimate=cost(100_000, 400_000),
        name="table_sum",
    )(every_peer(bias_part), near)
    bias_grad = pl.pallas_call(
        table_home_kernel,
        out_shape=jax.ShapeDtypeStruct((2 * HEADS, 1, POS), f32),
        in_specs=vmem(1),
        out_specs=vmem(1)[0],
        scratch_shapes=[pltpu.VMEM((4 * HEADS, FOLD), f32)],
        compiler_params=params,
        cost_estimate=cost(100_000, 400_000),
        name="table_home",
    )(every_peer(sums))

    block = jax.ShapeDtypeStruct((WL, WC, LEVELS, C), bf16)
    input_first, grad_second = pl.pallas_call(
        home_kernel,
        out_shape=(block, block),
        in_specs=vmem(7),
        out_specs=tuple(vmem(2)),
        scratch_shapes=[pltpu.VMEM((CELLS, 2 * C), f32)],
        compiler_params=params,
        cost_estimate=cost(20_000_000_000, 2_000_000),
        name="home",
    )(
        west,
        near,
        by_cell(output_first),
        second_cells,
        by_cell(cotangent_second),
        gain,
        w_proj,
    )
    return (
        input_first.transpose(2, 0, 1, 3)[None],
        grad_second.transpose(2, 0, 1, 3)[None],
        bias_grad.reshape(2, 1, HEADS, POS),
    )


def solution(mesh):
    block = P("dp", None, "lat", "lon", None)
    table = P(None, "lat", None, None)
    return jax.shard_map(
        local,
        mesh=mesh,
        in_specs=(block, block, block, block, P(), P(), P(), table, P(), P()),
        out_specs=(block, block, table),
        check_vma=False,
    )
```

time: 80 us -> 66.8 us (0.83)
  the two profiles are of different devices: /device:TPU:1 before, /device:TPU:2 now
where the time goes in v3:
time: 66.8 us; the launch traced here: 66.4 us
  starting transfers between devices  31.5 us (47%)
  Pallas kernels  16.8 us (25%)
  waiting for transfers between devices  12.6 us (19%)
  local copies, waits for them, and re-layouts  3.37 us (5%)
  other arithmetic  1.23 us (2%)
  between operations  0.84 us (1%)
    ppermute x4, starting transfers between devices, shifted(): return lax.ppermute(x, axis, [(i, (i + step) % size) for i in range(size)])  15.4 us
    all_to_all x2, waiting for transfers between devices, every_peer(): return lax.all_to_all(x, ('lon', 'dp'), 0, 0, tiled=True)  12.5 us
    all_to_all x2, starting transfers between devices, every_peer(): return lax.all_to_all(x, ('lon', 'dp'), 0, 0, tiled=True)  11.6 us
    pallas_call x1, Pallas kernels, local(): pl.pallas_call(attention_kernel, out_shape=(piece((WL, WC, LEVELS, 2 * C)...  9.83 us
    ppermute x1, starting transfers between devices, from_diagonal(): return lax.ppermute(x, ('lon', 'lat'), pairs)  4.53 us
    unnamed x19, local copies, waits for them, and re-layouts  3.37 us
    pallas_call x1, Pallas kernels, local(): pl.pallas_call(table_kernel, out_shape=(jax.ShapeDtypeStruct((2 * HEADS,...  3.3 us
    pallas_call x1, Pallas kernels, local(): pl.pallas_call(home_kernel, out_shape=(block, block), in_specs=vmem(7), o...  1.58 us
  transfers between devices with their start and end apart: 7, of which 2 were waited for; matrix products, arithmetic and copies ran while one was open for 2% of the time, Pallas kernels for 9%

profile of v3, /device:TPU:2, one launch (start us, length us, event | category | flops | bytes accessed | tf_op | source)
XLA Modules:
  0.0 66.4 jit_solution(17183687528941748664)
XLA Ops:
  0.6 0.0 copy-start
  0.6 0.0 copy-start.5
  0.7 1.2 %pad_maximum_fusion = (bf16[6,6,4,384]{3,2,1,0:T(4,128)(2,1)S(1)}, bf16[6,6,4,384]{3,2,1,0:T(4,128)(2,1)S(1)}) fusion(bf16[6,12,4,192]{3,2,1,0:T(4,128)(2,1)} %bitcast.30, bf16[6,12,4,192]{3,2,1,0:T(4,128)(2,1)} %bitcast.23), kind=kLoop, calls=%fused_computation.3 | loop fusion | flops 442368 | bytes 442368 | tf_op jit(solution)/shard_map/concatenate | solution.py:444
  1.9 10.9 %collective-permute-start = (bf16[6,6,4,384]{3,2,1,0:T(4,128)(2,1)S(1)}, bf16[6,6,4,384]{3,2,1,0:T(4,128)(2,1)S(1)}, u32[]{:S(2)}, u32[]{:S(2)}) collective-permute-start(bf16[6,6,4,384]{3,2,1,0:T(4,128)(2,1)S(1)} %get-tuple-element.21), channel_id=1, source_target_pairs={{0,480},{32,0},{64,32},{96,64},{128,96},{160,128},{192,160},{224,1... | collective-permute-start | bytes 331784 | tf_op jit(solution)/shard_map/ppermute | solution.py:410
  12.8 4.5 %collective-permute-start.2 = (bf16[6,6,4,384]{3,2,1,0:T(4,128)(2,1)S(1)}, bf16[6,6,4,384]{3,2,1,0:T(4,128)(2,1)S(1)}, u32[]{:S(2)}, u32[]{:S(2)}) collective-permute-start(bf16[6,6,4,384]{3,2,1,0:T(4,128)(2,1)S(1)} %get-tuple-element.21), channel_id=1, source_target_pairs={{0,510},{2,480},{4,482},{6,484},{8,486},{10,488},{12,490},{14,492}... | collective-permute-start | bytes 331784 | tf_op jit(solution)/shard_map/ppermute | solution.py:420
  17.3 1.1 %collective-permute-start.1 = (bf16[6,6,4,384]{3,2,1,0:T(4,128)(2,1)S(1)}, bf16[6,6,4,384]{3,2,1,0:T(4,128)(2,1)S(1)}, u32[]{:S(2)}, u32[]{:S(2)}) collective-permute-start(bf16[6,6,4,384]{3,2,1,0:T(4,128)(2,1)S(1)} %get-tuple-element.22.own_ref), channel_id=1, source_target_pairs={{0,30},{2,0},{4,2},{6,4},{8,6},{10,8},{12,10},{14,12},{16,14},{18,... | collective-permute-start | bytes 331784 | tf_op jit(solution)/shard_map/ppermute | solution.py:410
  18.5 1.1 %copy.12 = bf16[192,576]{0,1:T(8,128)(2,1)S(1)} copy(bf16[192,576]{1,0:T(8,128)(2,1)} %w_qkv_ref.1) | data formatting | bytes 442368 | tf_op args[5]
  19.6 0.0 copy-start.2
  19.6 0.9 %copy-done.2 = f32[2,1,6,3312]{3,1,2,0:T(1,128)S(1)} copy-done((f32[2,1,6,3312]{3,1,2,0:T(1,128)S(1)}, f32[2,1,6,3312]{3,1,2,0:T(1,128)}, u32[]{:S(2)}) %copy-start.2) | copy-done | bytes 159000
  20.5 0.0 copy-start.6
  20.5 0.7 %copy-done.6 = f32[192]{0:T(256)S(1)} copy-done((f32[192]{0:T(256)S(1)}, f32[192]{0:T(256)}, u32[]{:S(2)}) %copy-start.6) | copy-done | bytes 792
  21.2 0.0 copy-start.7
  21.2 0.7 copy-done.7
  21.8 3.3 %bias_table.1 = (f32[12,144,256]{2,1,0:T(8,128)S(1)}, f32[1,192]{1,0:T(1,128)S(1)}) custom-call(s32[2]{0:T(128)S(1)} %copy-done.7, f32[12,1,3312]{2,1,0:T(1,128)S(1)} %bitcast.25, f32[1,192]{1,0:T(1,128)S(1)} %bitcast.28), custom_call_target="tpu_custom_call" | custom-call | flops 400000000 | bytes 2000000 | tf_op jit(solution)/shard_map/bias_table/pallas_call | solution.py:452
  25.1 0.0 collective-permute-done.east_ref
  25.2 0.0 collective-permute-done.2.diag_ref
  25.2 0.0 collective-permute-done.1.south_ref
  25.2 0.0 copy-done
  25.2 0.0 copy-done.5
  25.2 0.0 copy-start.8
  25.2 9.8 %window_attention.1 = (bf16[6,12,4,384]{3,2,1,0:T(4,128)(2,1)S(1)}, bf16[5,12,4,384]{3,2,1,0:T(4,128)(2,1)S(1)}, bf16[32,5,2,128]{3,2,1,0:T(2,128)(2,1)}) custom-call(s32[2]{0:T(128)S(1)} %copy-done.7, bf16[6,6,4,384]{3,2,1,0:T(4,128)(2,1)S(1)} %get-tuple-element.22.own_ref, bf16[6,6,4,384]{3,2,1,0:T(4,128)(2,1)S(1)} %collective-permute-done.east_ref, ...), custom_call_target="tpu_custom_call" | custom-call | flops 4000000000 | bytes 2000000 | tf_op jit(solution)/shard_map/window_attention/pallas_call | solution.py:473
  35.0 0.0 collective-permute-start.3
  35.0 6.6 %all-to-all-start = ((bf16[32,5,2,128]{3,2,1,0:T(2,128)(2,1)}), bf16[32,5,2,128]{3,2,1,0:T(2,128)(2,1)S(1)}, u32[]{:S(2)}, u32[]{:S(2)}) async-start(bf16[32,5,2,128]{3,2,1,0:T(2,128)(2,1)} %get-tuple-element.20), calls=%async_computation | async-start | bytes 163840 | tf_op jit(solution)/shard_map/all_to_all | solution.py:424
  41.6 0.0 collective-permute-done.3.other_ref
  41.6 0.0 copy-done.8
  41.6 0.0 copy-start.1
  41.6 0.0 copy-start.3
  41.7 0.0 copy-start.4
  41.7 0.6 home_rows.1
  42.3 3.4 %collective-permute-start.4 = (bf16[6,6,4,384]{3,2,1,0:T(4,128)(2,1)S(1)}, bf16[6,6,4,384]{3,2,1,0:T(4,128)(2,1)S(1)}, u32[]{:S(2)}, u32[]{:S(2)}) collective-permute-start(bf16[6,6,4,384]{3,2,1,0:T(4,128)(2,1)S(1)} %get-tuple-element.16), channel_id=1, source_target_pairs={{0,32},{32,64},{64,96},{96,128},{128,160},{160,192},{192,224},{224... | collective-permute-start | bytes 331784 | tf_op jit(solution)/shard_map/ppermute | solution.py:410
  45.7 5.0 %all-to-all-done.parts_ref = bf16[32,5,2,128]{3,2,1,0:T(2,128)(2,1)S(1)} async-done(((bf16[32,5,2,128]{3,2,1,0:T(2,128)(2,1)}), bf16[32,5,2,128]{3,2,1,0:T(2,128)(2,1)S(1)}, u32[]{:S(2)}, u32[]{:S(2)}) %all-to-all-start) | async-done | bytes 81952 | tf_op jit(solution)/shard_map/all_to_all | solution.py:424
  50.7 0.7 %table_sum.1 = bf16[32,5,2,128]{3,2,1,0:T(2,128)(2,1)} custom-call(bf16[32,5,2,128]{3,2,1,0:T(2,128)(2,1)S(1)} %all-to-all-done.parts_ref, bf16[6,6,4,384]{3,2,1,0:T(4,128)(2,1)S(1)} %get-tuple-element.17.near_ref.after_ref), custom_call_target="tpu_custom_call" | custom-call | flops 100000 | bytes 400000 | tf_op jit(solution)/shard_map/table_sum/pallas_call | solution.py:517
  51.5 5.0 %all-to-all-start.1 = ((bf16[32,5,2,128]{3,2,1,0:T(2,128)(2,1)}), bf16[32,5,2,128]{3,2,1,0:T(2,128)(2,1)S(1)}, u32[]{:S(2)}, u32[]{:S(2)}) async-start(bf16[32,5,2,128]{3,2,1,0:T(2,128)(2,1)} %table_sum.1), calls=%async_computation.1 | async-start | bytes 163840 | tf_op jit(solution)/shard_map/all_to_all | solution.py:424
  56.5 0.0 collective-permute-done.4.west_ref
  56.5 0.0 copy-done.1
  56.5 0.0 copy-done.3
  56.5 0.0 copy-done.4
  56.5 1.6 %home.1 = (bf16[6,12,4,192]{3,2,1,0:T(4,128)(2,1)}, bf16[6,12,4,192]{3,2,1,0:T(4,128)(2,1)}) custom-call(bf16[6,6,4,384]{3,2,1,0:T(4,128)(2,1)S(1)} %collective-permute-done.4.west_ref, bf16[6,6,4,384]{3,2,1,0:T(4,128)(2,1)S(1)} %get-tuple-element.17.near_ref.after_ref, bf16[6,12,4,192]{3,2,1,0:T(4,128)(2,1)S(1)} %bitcast.26, ...), custom_call_target="tpu_custom_call" | custom-call | flops 20000000000 | bytes 2000000 | tf_op jit(solution)/shard_map/home/pallas_call | solution.py:538
  58.1 7.5 %all-to-all-done.1.sums_ref = bf16[32,5,2,128]{3,2,1,0:T(2,128)(2,1)S(1)} async-done(((bf16[32,5,2,128]{3,2,1,0:T(2,128)(2,1)}), bf16[32,5,2,128]{3,2,1,0:T(2,128)(2,1)S(1)}, u32[]{:S(2)}, u32[]{:S(2)}) %all-to-all-start.1) | async-done | bytes 81952 | tf_op jit(solution)/shard_map/all_to_all | solution.py:424
  65.6 0.8 %table_home.1 = f32[12,1,3312]{2,1,0:T(1,128)} custom-call(bf16[32,5,2,128]{3,2,1,0:T(2,128)(2,1)S(1)} %all-to-all-done.1.sums_ref), custom_call_target="tpu_custom_call" | custom-call | flops 100000 | bytes 400000 | tf_op jit(solution)/shard_map/table_home/pallas_call | solution.py:526
Async XLA Ops:
  0.6 24.5 %copy-start = (bf16[192,576]{1,0:T(8,128)(2,1)S(1)}, bf16[192,576]{1,0:T(8,128)(2,1)}, u32[]{:S(2)}) copy-start(bf16[192,576]{1,0:T(8,128)(2,1)} %w_qkv_ref.1) | copy-start | bytes 663556
  0.6 24.5 %copy-start.5 = (bf16[192,192]{1,0:T(8,128)(2,1)S(1)}, bf16[192,192]{1,0:T(8,128)(2,1)}, u32[]{:S(2)}) copy-start(bf16[192,192]{1,0:T(8,128)(2,1)} %w_proj_ref.3) | copy-start | bytes 221188
  1.9 23.3 %collective-permute-start = (bf16[6,6,4,384]{3,2,1,0:T(4,128)(2,1)S(1)}, bf16[6,6,4,384]{3,2,1,0:T(4,128)(2,1)S(1)}, u32[]{:S(2)}, u32[]{:S(2)}) collective-permute-start(bf16[6,6,4,384]{3,2,1,0:T(4,128)(2,1)S(1)} %get-tuple-element.21), channel_id=1, source_target_pairs={{0,480},{32,0},{64,32},{96,64},{128,96},{160,128},{192,160},{224,1... | collective-permute-start | bytes 331784 | tf_op jit(solution)/shard_map/ppermute | solution.py:410
  12.8 12.3 %collective-permute-start.2 = (bf16[6,6,4,384]{3,2,1,0:T(4,128)(2,1)S(1)}, bf16[6,6,4,384]{3,2,1,0:T(4,128)(2,1)S(1)}, u32[]{:S(2)}, u32[]{:S(2)}) collective-permute-start(bf16[6,6,4,384]{3,2,1,0:T(4,128)(2,1)S(1)} %get-tuple-element.21), channel_id=1, source_target_pairs={{0,510},{2,480},{4,482},{6,484},{8,486},{10,488},{12,490},{14,492}... | collective-permute-start | bytes 331784 | tf_op jit(solution)/shard_map/ppermute | solution.py:420
  17.3 7.8 %collective-permute-start.1 = (bf16[6,6,4,384]{3,2,1,0:T(4,128)(2,1)S(1)}, bf16[6,6,4,384]{3,2,1,0:T(4,128)(2,1)S(1)}, u32[]{:S(2)}, u32[]{:S(2)}) collective-permute-start(bf16[6,6,4,384]{3,2,1,0:T(4,128)(2,1)S(1)} %get-tuple-element.22.own_ref), channel_id=1, source_target_pairs={{0,30},{2,0},{4,2},{6,4},{8,6},{10,8},{12,10},{14,12},{16,14},{18,... | collective-permute-start | bytes 331784 | tf_op jit(solution)/shard_map/ppermute | solution.py:410
  19.6 0.9 %copy-start.2 = (f32[2,1,6,3312]{3,1,2,0:T(1,128)S(1)}, f32[2,1,6,3312]{3,1,2,0:T(1,128)}, u32[]{:S(2)}) copy-start(f32[2,1,6,3312]{3,1,2,0:T(1,128)} %param.17) | copy-start | bytes 476932
  20.5 0.7 %copy-start.6 = (f32[192]{0:T(256)S(1)}, f32[192]{0:T(256)}, u32[]{:S(2)}) copy-start(f32[192]{0:T(256)} %param.14) | copy-start | bytes 2308
  21.2 0.7 copy-start.7
  25.2 16.4 %copy-start.8 = (s32[2]{0:T(128)S(1)}, s32[2]{0:T(128)}, u32[]{:S(2)}) copy-start(s32[2]{0:T(128)} %shifts_ref.5) | copy-start | bytes 28
  35.0 6.6 %collective-permute-start.3 = (bf16[5,12,4,384]{3,2,1,0:T(4,128)(2,1)S(1)}, bf16[5,12,4,384]{3,2,1,0:T(4,128)(2,1)S(1)}, u32[]{:S(2)}, u32[]{:S(2)}) collective-permute-start(bf16[5,12,4,384]{3,2,1,0:T(4,128)(2,1)S(1)} %get-tuple-element.15), channel_id=1, source_target_pairs={{0,2},{2,4},{4,6},{6,8},{8,10},{10,12},{12,14},{14,16},{16,18},{18... | collective-permute-start | bytes 552968 | tf_op jit(solution)/shard_map/ppermute | solution.py:410
  35.0 15.7 %all-to-all-start = ((bf16[32,5,2,128]{3,2,1,0:T(2,128)(2,1)}), bf16[32,5,2,128]{3,2,1,0:T(2,128)(2,1)S(1)}, u32[]{:S(2)}, u32[]{:S(2)}) async-start(bf16[32,5,2,128]{3,2,1,0:T(2,128)(2,1)} %get-tuple-element.20), calls=%async_computation | async-start | bytes 163840 | tf_op jit(solution)/shard_map/all_to_all | solution.py:424
  41.6 14.9 %copy-start.1 = (bf16[1,4,6,12,192]{4,1,3,2,0:T(4,128)(2,1)S(1)}, bf16[1,4,6,12,192]{4,1,3,2,0:T(4,128)(2,1)}, u32[]{:S(2)}) copy-start(bf16[1,4,6,12,192]{4,1,3,2,0:T(4,128)(2,1)} %param.11) | copy-start | bytes 331780
  41.6 14.9 %copy-start.3 = (bf16[1,4,6,12,192]{4,1,3,2,0:T(4,128)(2,1)S(1)}, bf16[1,4,6,12,192]{4,1,3,2,0:T(4,128)(2,1)}, u32[]{:S(2)}) copy-start(bf16[1,4,6,12,192]{4,1,3,2,0:T(4,128)(2,1)} %param.10) | copy-start | bytes 331780
  41.7 14.9 %copy-start.4 = (bf16[1,4,6,12,192]{4,1,3,2,0:T(4,128)(2,1)S(1)}, bf16[1,4,6,12,192]{4,1,3,2,0:T(4,128)(2,1)}, u32[]{:S(2)}) copy-start(bf16[1,4,6,12,192]{4,1,3,2,0:T(4,128)(2,1)} %param.13) | copy-start | bytes 331780
  42.3 14.2 %collective-permute-start.4 = (bf16[6,6,4,384]{3,2,1,0:T(4,128)(2,1)S(1)}, bf16[6,6,4,384]{3,2,1,0:T(4,128)(2,1)S(1)}, u32[]{:S(2)}, u32[]{:S(2)}) collective-permute-start(bf16[6,6,4,384]{3,2,1,0:T(4,128)(2,1)S(1)} %get-tuple-element.16), channel_id=1, source_target_pairs={{0,32},{32,64},{64,96},{96,128},{128,160},{160,192},{192,224},{224... | collective-permute-start | bytes 331784 | tf_op jit(solution)/shard_map/ppermute | solution.py:410
  51.5 14.1 %all-to-all-start.1 = ((bf16[32,5,2,128]{3,2,1,0:T(2,128)(2,1)}), bf16[32,5,2,128]{3,2,1,0:T(2,128)(2,1)S(1)}, u32[]{:S(2)}, u32[]{:S(2)}) async-start(bf16[32,5,2,128]{3,2,1,0:T(2,128)(2,1)} %table_sum.1), calls=%async_computation.1 | async-start | bytes 163840 | tf_op jit(solution)/shard_map/all_to_all | solution.py:424

commit v4 on v3

--- a/solution.py
+++ b/solution.py
@@ -24,7 +24,6 @@
 CELLS = 288
 PITCH = 16
 WIDE = 3584
-FOLD = 1664
 TILES = 156
 CHUNKS = 32
 DEEP = 5
@@ -193,13 +192,14 @@
     ups_t,
     keys_t,
     values_t,
+    weights_low,
+    grads_low,
     attended_t,
     grad_query_t,
     grad_key_t,
     grad_value_t,
     table_grad,
     wide,
-    folds,
     packed_table,
 ):
     half = HALF * LEVELS
@@ -241,7 +241,6 @@
     key_column = parts(line(LANES, 1), PITCH)[1]
 
     def one_head(h, carry):
-        features = pl.ds(pl.multiple_of(h * HEAD, HEAD), HEAD)
         chosen = parts(line(C, 1), HEAD)[0] == h
         for a in range(2):
             query = jnp.where(chosen, queries[a], jnp.zeros((), bf16))
@@ -249,19 +248,11 @@
             scores = mm(query, keys_t[a]) * scale + bias_ref[a * HEADS + h]
             exponent = jnp.exp(scores - jnp.max(scores, axis=-1, keepdims=True))
             weights = exponent * (1.0 / jnp.sum(exponent, axis=-1, keepdims=True))
-            weights_low = weights.astype(bf16)
             grad_weights = mm(up, values_t[a])
             row_dot = jnp.sum(weights * grad_weights, axis=-1, keepdims=True)
             grad_scores = weights * (grad_weights - row_dot)
-            grad_low = grad_scores.astype(bf16)
-            attended_t[a, features, :] = mm_t(values_t[a, features, :], weights_low).astype(bf16)
-            grad_value_t[a, features, :] = mm(ups_t[a, features, :], weights_low).astype(bf16)
-            grad_query_t[a, features, :] = (
-                mm_t(keys_t[a, features, :], grad_low) * scale
-            ).astype(bf16)
-            grad_key_t[a, features, :] = (
-                mm(queries_t[a, features, :], grad_low) * scale
-            ).astype(bf16)
+            weights_low[a, h] = weights.astype(bf16)
+            grads_low[a, h] = grad_scores.astype(bf16)
             low = jnp.zeros((GROUPS, LANES), f32)
             high = jnp.zeros((GROUPS, LANES), f32)
             for c in range(WC):
@@ -297,16 +288,24 @@
                 piece = pltpu.roll(piece, turn, 1)
             wide[:, tile : tile + REACH] += piece
     packed_table[...] = jnp.zeros(packed_table.shape, f32)
-    for side in range(2):
+    for tile in range(TILES):
+        chunk, slot, row, lanes = tile_place(tile)
+        row = row // HEADS * 8 + row % HEADS
+        packed_table[chunk, slot] = wide[row : row + 2, lanes]
+    bias_out[...] = packed_table[...].astype(bf16)
+
+    for h in range(HEADS):
+        features = slice(h * HEAD, (h + 1) * HEAD)
         for a in range(2):
-            start = (2 * side + a) * HEADS
-            folds[start : start + HEADS, :] = wide[
-                a * 8 : a * 8 + HEADS, side * FOLD : (side + 1) * FOLD
-            ]
-    for tile in range(TILES):
-        chunk, slot, fold_rows, fold_lanes = tile_place(tile)
-        packed_table[chunk, slot] = folds[fold_rows, fold_lanes]
-    bias_out[...] = packed_table[...].astype(bf16)
+            weight, grad = weights_low[a, h], grads_low[a, h]
+            attended_t[a, features, :] = mm_t(values_t[a, features, :], weight).astype(bf16)
+            grad_value_t[a, features, :] = mm(ups_t[a, features, :], weight).astype(bf16)
+            grad_query_t[a, features, :] = (
+                mm_t(keys_t[a, features, :], grad) * scale
+            ).astype(bf16)
+            grad_key_t[a, features, :] = (
+                mm(queries_t[a, features, :], grad) * scale
+            ).astype(bf16)
 
     attended = jnp.zeros((CELLS, C), f32)
     coeffs = [jnp.zeros((CELLS, C), f32) for _ in range(3)]
@@ -365,13 +364,8 @@
 
 def tile_place(tile):
     chunk, slot = divmod(tile, DEEP)
-    block, column = divmod(tile, FOLD // 128)
-    return (
-        chunk,
-        slot,
-        slice(block * 2, block * 2 + 2),
-        slice(column * 128, column * 128 + 128),
-    )
+    pair, column = divmod(tile, TILES // HEADS)
+    return chunk, slot, 2 * pair, slice(column * 128, column * 128 + 128)
 
 
 def table_sum_kernel(parts_ref, after_ref, sums_out):
@@ -380,14 +374,15 @@
         sums_out[peer] = total
 
 
-def table_home_kernel(sums_ref, table_out, folds):
+def table_home_kernel(sums_ref, table_out):
     for tile in range(TILES):
-        chunk, slot, fold_rows, fold_lanes = tile_place(tile)
-        folds[fold_rows, fold_lanes] = sums_ref[chunk, slot].astype(f32)
-    rows = 2 * HEADS
-    for row in range(rows):
-        table_out[row, :, 0:FOLD] = folds[row : row + 1]
-        table_out[row, :, FOLD:POS] = folds[rows + row : rows + row + 1, 0 : POS - FOLD]
+        chunk, slot, row, lanes = tile_place(tile)
+        sums = sums_ref[chunk, slot].astype(f32)
+        width = min(128, POS - lanes.start)
+        for place in range(2):
+            table_out[row + place, :, lanes.start : lanes.start + width] = sums[
+                place : place + 1, 0:width
+            ]
 
 
 def vmem(count):
@@ -487,13 +482,14 @@
             pltpu.VMEM((2, C, ROWS), bf16),
             pltpu.VMEM((2, C, LANES), bf16),
             pltpu.VMEM((2, C, LANES), bf16),
+            pltpu.VMEM((2, HEADS, ROWS, LANES), bf16),
+            pltpu.VMEM((2, HEADS, ROWS, LANES), bf16),
             pltpu.VMEM((2, C, ROWS), bf16),
             pltpu.VMEM((2, C, ROWS), bf16),
             pltpu.VMEM((2, C, LANES), bf16),
             pltpu.VMEM((2, C, LANES), bf16),
             pltpu.VMEM((2, 16, 16, LANES), f32),
             pltpu.VMEM((16, WIDE), f32),
-            pltpu.VMEM((4 * HEADS, FOLD), f32),
             pltpu.VMEM(table_chunks, f32),
         ],
         compiler_params=params,
@@ -528,7 +524,6 @@
         out_shape=jax.ShapeDtypeStruct((2 * HEADS, 1, POS), f32),
         in_specs=vmem(1),
         out_specs=vmem(1)[0],
-        scratch_shapes=[pltpu.VMEM((4 * HEADS, FOLD), f32)],
         compiler_params=params,
         cost_estimate=cost(100_000, 400_000),
         name="table_home",

time: 66.8 us -> 65 us (0.973)
  Pallas kernels: 16.8 us -> 15 us
    pallas_call x1, Pallas kernels: 9.83 us -> 8.04 us  [local(): pl.pallas_call(attention_kernel, out_shape=(piece((WL, WC, LEVELS, 2 * C)...]
  transfers between devices with their start and end apart: 7 -> 7, of which waited for: 2 -> 2; matrix products, arithmetic and copies ran while one was open for 2% -> 2% of each run, Pallas kernels for 9% -> 10%
where the time goes in v4:
time: 65 us; the launch traced here: 64.6 us
  starting transfers between devices  31.5 us (48%)
  Pallas kernels  15 us (23%)
  waiting for transfers between devices  12.6 us (19%)
  local copies, waits for them, and re-layouts  3.37 us (5%)
  other arithmetic  1.23 us (2%)
  between operations  0.84 us (1%)
    ppermute x4, starting transfers between devices, shifted(): return lax.ppermute(x, axis, [(i, (i + step) % size) for i in range(size)])  15.4 us
    all_to_all x2, waiting for transfers between devices, every_peer(): return lax.all_to_all(x, ('lon', 'dp'), 0, 0, tiled=True)  12.5 us
    all_to_all x2, starting transfers between devices, every_peer(): return lax.all_to_all(x, ('lon', 'dp'), 0, 0, tiled=True)  11.6 us
    pallas_call x1, Pallas kernels, local(): pl.pallas_call(attention_kernel, out_shape=(piece((WL, WC, LEVELS, 2 * C)...  8.04 us
    ppermute x1, starting transfers between devices, from_diagonal(): return lax.ppermute(x, ('lon', 'lat'), pairs)  4.53 us
    unnamed x19, local copies, waits for them, and re-layouts  3.37 us
    pallas_call x1, Pallas kernels, local(): pl.pallas_call(table_kernel, out_shape=(jax.ShapeDtypeStruct((2 * HEADS,...  3.3 us
    pallas_call x1, Pallas kernels, local(): pl.pallas_call(home_kernel, out_shape=(block, block), in_specs=vmem(7), o...  1.58 us
  transfers between devices with their start and end apart: 7, of which 2 were waited for; matrix products, arithmetic and copies ran while one was open for 2% of the time, Pallas kernels for 10%

profile of v4, /device:TPU:2, one launch (start us, length us, event | category | flops | bytes accessed | tf_op | source)
XLA Modules:
  0.0 64.6 jit_solution(966330037000464204)
XLA Ops:
  0.6 0.0 copy-start
  0.6 0.0 copy-start.5
  0.7 1.2 %pad_maximum_fusion = (bf16[6,6,4,384]{3,2,1,0:T(4,128)(2,1)S(1)}, bf16[6,6,4,384]{3,2,1,0:T(4,128)(2,1)S(1)}) fusion(bf16[6,12,4,192]{3,2,1,0:T(4,128)(2,1)} %bitcast.30, bf16[6,12,4,192]{3,2,1,0:T(4,128)(2,1)} %bitcast.23), kind=kLoop, calls=%fused_computation.3 | loop fusion | flops 442368 | bytes 442368 | tf_op jit(solution)/shard_map/concatenate | solution.py:439
  1.9 10.9 %collective-permute-start = (bf16[6,6,4,384]{3,2,1,0:T(4,128)(2,1)S(1)}, bf16[6,6,4,384]{3,2,1,0:T(4,128)(2,1)S(1)}, u32[]{:S(2)}, u32[]{:S(2)}) collective-permute-start(bf16[6,6,4,384]{3,2,1,0:T(4,128)(2,1)S(1)} %get-tuple-element.21), channel_id=1, source_target_pairs={{0,480},{32,0},{64,32},{96,64},{128,96},{160,128},{192,160},{224,1... | collective-permute-start | bytes 331784 | tf_op jit(solution)/shard_map/ppermute | solution.py:405
  12.8 4.5 %collective-permute-start.2 = (bf16[6,6,4,384]{3,2,1,0:T(4,128)(2,1)S(1)}, bf16[6,6,4,384]{3,2,1,0:T(4,128)(2,1)S(1)}, u32[]{:S(2)}, u32[]{:S(2)}) collective-permute-start(bf16[6,6,4,384]{3,2,1,0:T(4,128)(2,1)S(1)} %get-tuple-element.21), channel_id=1, source_target_pairs={{0,510},{2,480},{4,482},{6,484},{8,486},{10,488},{12,490},{14,492}... | collective-permute-start | bytes 331784 | tf_op jit(solution)/shard_map/ppermute | solution.py:415
  17.3 1.1 %collective-permute-start.1 = (bf16[6,6,4,384]{3,2,1,0:T(4,128)(2,1)S(1)}, bf16[6,6,4,384]{3,2,1,0:T(4,128)(2,1)S(1)}, u32[]{:S(2)}, u32[]{:S(2)}) collective-permute-start(bf16[6,6,4,384]{3,2,1,0:T(4,128)(2,1)S(1)} %get-tuple-element.22.own_ref), channel_id=1, source_target_pairs={{0,30},{2,0},{4,2},{6,4},{8,6},{10,8},{12,10},{14,12},{16,14},{18,... | collective-permute-start | bytes 331784 | tf_op jit(solution)/shard_map/ppermute | solution.py:405
  18.5 1.1 %copy.12 = bf16[192,576]{0,1:T(8,128)(2,1)S(1)} copy(bf16[192,576]{1,0:T(8,128)(2,1)} %w_qkv_ref.1) | data formatting | bytes 442368 | tf_op args[5]
  19.6 0.0 copy-start.2
  19.6 0.9 %copy-done.2 = f32[2,1,6,3312]{3,1,2,0:T(1,128)S(1)} copy-done((f32[2,1,6,3312]{3,1,2,0:T(1,128)S(1)}, f32[2,1,6,3312]{3,1,2,0:T(1,128)}, u32[]{:S(2)}) %copy-start.2) | copy-done | bytes 159000
  20.5 0.0 copy-start.6
  20.5 0.7 %copy-done.6 = f32[192]{0:T(256)S(1)} copy-done((f32[192]{0:T(256)S(1)}, f32[192]{0:T(256)}, u32[]{:S(2)}) %copy-start.6) | copy-done | bytes 792
  21.2 0.0 copy-start.7
  21.2 0.7 %copy-done.7 = s32[2]{0:T(128)S(1)} copy-done((s32[2]{0:T(128)S(1)}, s32[2]{0:T(128)}, u32[]{:S(2)}) %copy-start.7) | copy-done | bytes 32
  21.8 3.3 %bias_table.1 = (f32[12,144,256]{2,1,0:T(8,128)S(1)}, f32[1,192]{1,0:T(1,128)S(1)}) custom-call(s32[2]{0:T(128)S(1)} %copy-done.7, f32[12,1,3312]{2,1,0:T(1,128)S(1)} %bitcast.25, f32[1,192]{1,0:T(1,128)S(1)} %bitcast.28), custom_call_target="tpu_custom_call" | custom-call | flops 400000000 | bytes 2000000 | tf_op jit(solution)/shard_map/bias_table/pallas_call | solution.py:447
  25.1 0.0 collective-permute-done.east_ref
  25.2 0.0 collective-permute-done.2.diag_ref
  25.2 0.0 collective-permute-done.1.south_ref
  25.2 0.0 copy-done
  25.2 0.0 copy-done.5
  25.2 0.0 copy-start.8
  25.2 8.0 %window_attention.1 = (bf16[6,12,4,384]{3,2,1,0:T(4,128)(2,1)S(1)}, bf16[5,12,4,384]{3,2,1,0:T(4,128)(2,1)S(1)}, bf16[32,5,2,128]{3,2,1,0:T(2,128)(2,1)}) custom-call(s32[2]{0:T(128)S(1)} %copy-done.7, bf16[6,6,4,384]{3,2,1,0:T(4,128)(2,1)S(1)} %get-tuple-element.22.own_ref, bf16[6,6,4,384]{3,2,1,0:T(4,128)(2,1)S(1)} %collective-permute-done.east_ref, ...), custom_call_target="tpu_custom_call" | custom-call | flops 4000000000 | bytes 2000000 | tf_op jit(solution)/shard_map/window_attention/pallas_call | solution.py:468
  33.3 0.0 collective-permute-start.3
  33.3 6.6 %all-to-all-start = ((bf16[32,5,2,128]{3,2,1,0:T(2,128)(2,1)}), bf16[32,5,2,128]{3,2,1,0:T(2,128)(2,1)S(1)}, u32[]{:S(2)}, u32[]{:S(2)}) async-start(bf16[32,5,2,128]{3,2,1,0:T(2,128)(2,1)} %get-tuple-element.20), calls=%async_computation | async-start | bytes 163840 | tf_op jit(solution)/shard_map/all_to_all | solution.py:419
  39.8 0.0 collective-permute-done.3.other_ref
  39.8 0.0 copy-done.8
  39.8 0.0 copy-start.1
  39.9 0.0 copy-start.3
  39.9 0.0 copy-start.4
  39.9 0.6 home_rows.1
  40.5 3.4 %collective-permute-start.4 = (bf16[6,6,4,384]{3,2,1,0:T(4,128)(2,1)S(1)}, bf16[6,6,4,384]{3,2,1,0:T(4,128)(2,1)S(1)}, u32[]{:S(2)}, u32[]{:S(2)}) collective-permute-start(bf16[6,6,4,384]{3,2,1,0:T(4,128)(2,1)S(1)} %get-tuple-element.16), channel_id=1, source_target_pairs={{0,32},{32,64},{64,96},{96,128},{128,160},{160,192},{192,224},{224... | collective-permute-start | bytes 331784 | tf_op jit(solution)/shard_map/ppermute | solution.py:405
  43.9 5.0 %all-to-all-done.parts_ref = bf16[32,5,2,128]{3,2,1,0:T(2,128)(2,1)S(1)} async-done(((bf16[32,5,2,128]{3,2,1,0:T(2,128)(2,1)}), bf16[32,5,2,128]{3,2,1,0:T(2,128)(2,1)S(1)}, u32[]{:S(2)}, u32[]{:S(2)}) %all-to-all-start) | async-done | bytes 81952 | tf_op jit(solution)/shard_map/all_to_all | solution.py:419
  48.9 0.7 %table_sum.1 = bf16[32,5,2,128]{3,2,1,0:T(2,128)(2,1)} custom-call(bf16[32,5,2,128]{3,2,1,0:T(2,128)(2,1)S(1)} %all-to-all-done.parts_ref, bf16[6,6,4,384]{3,2,1,0:T(4,128)(2,1)S(1)} %get-tuple-element.17.near_ref.after_ref), custom_call_target="tpu_custom_call" | custom-call | flops 100000 | bytes 400000 | tf_op jit(solution)/shard_map/table_sum/pallas_call | solution.py:513
  49.7 5.0 %all-to-all-start.1 = ((bf16[32,5,2,128]{3,2,1,0:T(2,128)(2,1)}), bf16[32,5,2,128]{3,2,1,0:T(2,128)(2,1)S(1)}, u32[]{:S(2)}, u32[]{:S(2)}) async-start(bf16[32,5,2,128]{3,2,1,0:T(2,128)(2,1)} %table_sum.1), calls=%async_computation.1 | async-start | bytes 163840 | tf_op jit(solution)/shard_map/all_to_all | solution.py:419
  54.7 0.0 collective-permute-done.4.west_ref
  54.7 0.0 copy-done.1
  54.7 0.0 copy-done.3
  54.7 0.0 copy-done.4
  54.7 1.6 %home.1 = (bf16[6,12,4,192]{3,2,1,0:T(4,128)(2,1)}, bf16[6,12,4,192]{3,2,1,0:T(4,128)(2,1)}) custom-call(bf16[6,6,4,384]{3,2,1,0:T(4,128)(2,1)S(1)} %collective-permute-done.4.west_ref, bf16[6,6,4,384]{3,2,1,0:T(4,128)(2,1)S(1)} %get-tuple-element.17.near_ref.after_ref, bf16[6,12,4,192]{3,2,1,0:T(4,128)(2,1)S(1)} %bitcast.26, ...), custom_call_target="tpu_custom_call" | custom-call | flops 20000000000 | bytes 2000000 | tf_op jit(solution)/shard_map/home/pallas_call | solution.py:533
  56.3 7.5 %all-to-all-done.1.sums_ref = bf16[32,5,2,128]{3,2,1,0:T(2,128)(2,1)S(1)} async-done(((bf16[32,5,2,128]{3,2,1,0:T(2,128)(2,1)}), bf16[32,5,2,128]{3,2,1,0:T(2,128)(2,1)S(1)}, u32[]{:S(2)}, u32[]{:S(2)}) %all-to-all-start.1) | async-done | bytes 81952 | tf_op jit(solution)/shard_map/all_to_all | solution.py:419
  63.8 0.8 %table_home.1 = f32[12,1,3312]{2,1,0:T(1,128)} custom-call(bf16[32,5,2,128]{3,2,1,0:T(2,128)(2,1)S(1)} %all-to-all-done.1.sums_ref), custom_call_target="tpu_custom_call" | custom-call | flops 100000 | bytes 400000 | tf_op jit(solution)/shard_map/table_home/pallas_call | solution.py:522
Async XLA Ops:
  0.6 24.5 %copy-start = (bf16[192,576]{1,0:T(8,128)(2,1)S(1)}, bf16[192,576]{1,0:T(8,128)(2,1)}, u32[]{:S(2)}) copy-start(bf16[192,576]{1,0:T(8,128)(2,1)} %w_qkv_ref.1) | copy-start | bytes 663556
  0.6 24.5 %copy-start.5 = (bf16[192,192]{1,0:T(8,128)(2,1)S(1)}, bf16[192,192]{1,0:T(8,128)(2,1)}, u32[]{:S(2)}) copy-start(bf16[192,192]{1,0:T(8,128)(2,1)} %w_proj_ref.3) | copy-start | bytes 221188
  1.9 23.3 %collective-permute-start = (bf16[6,6,4,384]{3,2,1,0:T(4,128)(2,1)S(1)}, bf16[6,6,4,384]{3,2,1,0:T(4,128)(2,1)S(1)}, u32[]{:S(2)}, u32[]{:S(2)}) collective-permute-start(bf16[6,6,4,384]{3,2,1,0:T(4,128)(2,1)S(1)} %get-tuple-element.21), channel_id=1, source_target_pairs={{0,480},{32,0},{64,32},{96,64},{128,96},{160,128},{192,160},{224,1... | collective-permute-start | bytes 331784 | tf_op jit(solution)/shard_map/ppermute | solution.py:405
  12.8 12.3 %collective-permute-start.2 = (bf16[6,6,4,384]{3,2,1,0:T(4,128)(2,1)S(1)}, bf16[6,6,4,384]{3,2,1,0:T(4,128)(2,1)S(1)}, u32[]{:S(2)}, u32[]{:S(2)}) collective-permute-start(bf16[6,6,4,384]{3,2,1,0:T(4,128)(2,1)S(1)} %get-tuple-element.21), channel_id=1, source_target_pairs={{0,510},{2,480},{4,482},{6,484},{8,486},{10,488},{12,490},{14,492}... | collective-permute-start | bytes 331784 | tf_op jit(solution)/shard_map/ppermute | solution.py:415
  17.3 7.8 %collective-permute-start.1 = (bf16[6,6,4,384]{3,2,1,0:T(4,128)(2,1)S(1)}, bf16[6,6,4,384]{3,2,1,0:T(4,128)(2,1)S(1)}, u32[]{:S(2)}, u32[]{:S(2)}) collective-permute-start(bf16[6,6,4,384]{3,2,1,0:T(4,128)(2,1)S(1)} %get-tuple-element.22.own_ref), channel_id=1, source_target_pairs={{0,30},{2,0},{4,2},{6,4},{8,6},{10,8},{12,10},{14,12},{16,14},{18,... | collective-permute-start | bytes 331784 | tf_op jit(solution)/shard_map/ppermute | solution.py:405
  19.6 0.9 %copy-start.2 = (f32[2,1,6,3312]{3,1,2,0:T(1,128)S(1)}, f32[2,1,6,3312]{3,1,2,0:T(1,128)}, u32[]{:S(2)}) copy-start(f32[2,1,6,3312]{3,1,2,0:T(1,128)} %param.17) | copy-start | bytes 476932
  20.5 0.7 %copy-start.6 = (f32[192]{0:T(256)S(1)}, f32[192]{0:T(256)}, u32[]{:S(2)}) copy-start(f32[192]{0:T(256)} %param.14) | copy-start | bytes 2308
  21.2 0.7 %copy-start.7 = (s32[2]{0:T(128)S(1)}, s32[2]{0:T(128)}, u32[]{:S(2)}) copy-start(s32[2]{0:T(128)} %shifts_ref.5) | copy-start | bytes 28
  25.2 14.6 %copy-start.8 = (s32[2]{0:T(128)S(1)}, s32[2]{0:T(128)}, u32[]{:S(2)}) copy-start(s32[2]{0:T(128)} %shifts_ref.5) | copy-start | bytes 28
  33.3 6.6 %collective-permute-start.3 = (bf16[5,12,4,384]{3,2,1,0:T(4,128)(2,1)S(1)}, bf16[5,12,4,384]{3,2,1,0:T(4,128)(2,1)S(1)}, u32[]{:S(2)}, u32[]{:S(2)}) collective-permute-start(bf16[5,12,4,384]{3,2,1,0:T(4,128)(2,1)S(1)} %get-tuple-element.15), channel_id=1, source_target_pairs={{0,2},{2,4},{4,6},{6,8},{8,10},{10,12},{12,14},{14,16},{16,18},{18... | collective-permute-start | bytes 552968 | tf_op jit(solution)/shard_map/ppermute | solution.py:405
  33.3 15.7 %all-to-all-start = ((bf16[32,5,2,128]{3,2,1,0:T(2,128)(2,1)}), bf16[32,5,2,128]{3,2,1,0:T(2,128)(2,1)S(1)}, u32[]{:S(2)}, u32[]{:S(2)}) async-start(bf16[32,5,2,128]{3,2,1,0:T(2,128)(2,1)} %get-tuple-element.20), calls=%async_computation | async-start | bytes 163840 | tf_op jit(solution)/shard_map/all_to_all | solution.py:419
  39.8 14.9 %copy-start.1 = (bf16[1,4,6,12,192]{4,1,3,2,0:T(4,128)(2,1)S(1)}, bf16[1,4,6,12,192]{4,1,3,2,0:T(4,128)(2,1)}, u32[]{:S(2)}) copy-start(bf16[1,4,6,12,192]{4,1,3,2,0:T(4,128)(2,1)} %param.11) | copy-start | bytes 331780
  39.9 14.9 %copy-start.3 = (bf16[1,4,6,12,192]{4,1,3,2,0:T(4,128)(2,1)S(1)}, bf16[1,4,6,12,192]{4,1,3,2,0:T(4,128)(2,1)}, u32[]{:S(2)}) copy-start(bf16[1,4,6,12,192]{4,1,3,2,0:T(4,128)(2,1)} %param.10) | copy-start | bytes 331780
  39.9 14.9 %copy-start.4 = (bf16[1,4,6,12,192]{4,1,3,2,0:T(4,128)(2,1)S(1)}, bf16[1,4,6,12,192]{4,1,3,2,0:T(4,128)(2,1)}, u32[]{:S(2)}) copy-start(bf16[1,4,6,12,192]{4,1,3,2,0:T(4,128)(2,1)} %param.13) | copy-start | bytes 331780
  40.5 14.2 %collective-permute-start.4 = (bf16[6,6,4,384]{3,2,1,0:T(4,128)(2,1)S(1)}, bf16[6,6,4,384]{3,2,1,0:T(4,128)(2,1)S(1)}, u32[]{:S(2)}, u32[]{:S(2)}) collective-permute-start(bf16[6,6,4,384]{3,2,1,0:T(4,128)(2,1)S(1)} %get-tuple-element.16), channel_id=1, source_target_pairs={{0,32},{32,64},{64,96},{96,128},{128,160},{160,192},{192,224},{224... | collective-permute-start | bytes 331784 | tf_op jit(solution)/shard_map/ppermute | solution.py:405
  49.7 14.1 %all-to-all-start.1 = ((bf16[32,5,2,128]{3,2,1,0:T(2,128)(2,1)}), bf16[32,5,2,128]{3,2,1,0:T(2,128)(2,1)S(1)}, u32[]{:S(2)}, u32[]{:S(2)}) async-start(bf16[32,5,2,128]{3,2,1,0:T(2,128)(2,1)} %table_sum.1), calls=%async_computation.1 | async-start | bytes 163840 | tf_op jit(solution)/shard_map/all_to_all | solution.py:419

commit v5 on v4

--- a/solution.py
+++ b/solution.py
@@ -93,9 +93,23 @@
 
 
 def table_kernel(
-    shifts_ref, bias_ref, gain_ref, expanded_out, gain_out, wide, pieces, tables, mask
+    shifts_ref,
+    bias_ref,
+    gain_ref,
+    w_qkv_ref,
+    expanded_out,
+    gain_out,
+    w_qkv_t_out,
+    wide,
+    pieces,
+    tables,
+    mask,
 ):
     gain_out[...] = gain_ref[...]
+    same = picks(line(C, 0), C, 0)
+    for part in range(3):
+        block = w_qkv_ref[:, part * C : (part + 1) * C]
+        w_qkv_t_out[part * C : (part + 1) * C, :] = mm_t(same, block).astype(bf16)
     wide[...] = jnp.zeros(wide.shape, f32)
     for a in range(2):
         for h in range(HEADS):
@@ -137,9 +151,9 @@
         first, second = tables[0, index], tables[1, index]
         for c in range(WC):
             shift = (c - WC + 1) % LANES
-            low = pltpu.roll(first, shift, 1) if shift else first
-            high = pltpu.roll(second, shift, 1) if shift else second
-            bias = jnp.where(key_column + (WC - 1 - c) < PITCH, low, high)
+            bias = jnp.where(key_column >= WC - 1 - c, first, second)
+            if shift:
+                bias = pltpu.roll(bias, shift, 1)
             expanded_out[index, c * GROUPS : (c + 1) * GROUPS, :] = bias + mask[...]
         return carry
 
@@ -178,7 +192,6 @@
     south_ref,
     diag_ref,
     gain_ref,
-    w_qkv_ref,
     w_qkv_t_ref,
     w_proj_ref,
     bias_ref,
@@ -230,7 +243,7 @@
         turned = mm(to_queries, hidden).astype(bf16)
         turned_cot = mm(to_queries, cotangent).astype(bf16)
         spaced = mm(picks(key_cells(a, 0), CELLS, 0), hidden).astype(bf16)
-        queries[a] = mm(turned, w_qkv_ref[:, 0:C]).astype(bf16)
+        queries[a] = mm_t(turned, w_qkv_t_ref[0:C, :]).astype(bf16)
         queries_t[a] = mm_t(w_qkv_t_ref[0:C, :], turned).astype(bf16)
         keys_t[a] = mm_t(w_qkv_t_ref[C : 2 * C, :], spaced).astype(bf16)
         values_t[a] = mm_t(w_qkv_t_ref[2 * C : 3 * C, :], spaced).astype(bf16)
@@ -442,16 +455,16 @@
     diag = from_diagonal(left)
     south = shifted(right, "lat", -1)
 
-    w_qkv_t = w_qkv.T
-
-    bias, gain = pl.pallas_call(
+
+    bias, gain, w_qkv_t = pl.pallas_call(
         table_kernel,
         out_shape=(
             jax.ShapeDtypeStruct((2 * HEADS, ROWS, LANES), f32),
             jax.ShapeDtypeStruct((1, C), f32),
+            jax.ShapeDtypeStruct((3 * C, C), bf16),
         ),
-        in_specs=smem() + vmem(2),
-        out_specs=tuple(vmem(2)),
+        in_specs=smem() + vmem(3),
+        out_specs=tuple(vmem(3)),
         scratch_shapes=[
             pltpu.VMEM((16, WIDE), f32),
             pltpu.VMEM((GROUPS * PITCH, LANES), f32),
@@ -461,7 +474,7 @@
         compiler_params=params,
         cost_estimate=cost(400_000_000, 2_000_000),
         name="bias_table",
-    )(shifts, earth_bias.reshape(2 * HEADS, 1, POS), norm_gain.reshape(1, C))
+    )(shifts, earth_bias.reshape(2 * HEADS, 1, POS), norm_gain.reshape(1, C), w_qkv)
 
     piece = functools.partial(jax.ShapeDtypeStruct, dtype=bf16)
     table_chunks = (CHUNKS, DEEP, 2, 128)
@@ -472,7 +485,7 @@
             piece((WL - 1, WC, LEVELS, 2 * C)),
             piece(table_chunks),
         ),
-        in_specs=smem() + vmem(9),
+        in_specs=smem() + vmem(8),
         out_specs=tuple(vmem(3)),
         scratch_shapes=[
             pltpu.VMEM((CELLS, 2 * C), f32),
@@ -495,7 +508,7 @@
         compiler_params=params,
         cost_estimate=cost(4_000_000_000, 2_000_000),
         name="window_attention",
-    )(shifts, right, east, south, diag, gain, w_qkv, w_qkv_t, w_proj, bias)
+    )(shifts, right, east, south, diag, gain, w_qkv_t, w_proj, bias)
     north = shifted(to_south, "lat", 1)
 
     half_block = (WL, HALF, LEVELS, 2 * C)

time: 65 us -> 64.3 us (0.989)
    unnamed x19 -> x18, local copies, waits for them, and re-layouts: 3.37 us -> 3.22 us
  transfers between devices with their start and end apart: 7 -> 7, of which waited for: 2 -> 2; matrix products, arithmetic and copies ran while one was open for 2% -> 0% of each run, Pallas kernels for 10% -> 9%
where the time goes in v5:
time: 64.3 us; the launch traced here: 63.9 us
  starting transfers between devices  31.5 us (49%)
  Pallas kernels  14.6 us (23%)
  waiting for transfers between devices  12.6 us (20%)
  local copies, waits for them, and re-layouts  3.22 us (5%)
  other arithmetic  1.22 us (2%)
  between operations  0.81 us (1%)
    ppermute x4, starting transfers between devices, shifted(): return lax.ppermute(x, axis, [(i, (i + step) % size) for i in range(size)])  15.4 us
    all_to_all x2, waiting for transfers between devices, every_peer(): return lax.all_to_all(x, ('lon', 'dp'), 0, 0, tiled=True)  12.5 us
    all_to_all x2, starting transfers between devices, every_peer(): return lax.all_to_all(x, ('lon', 'dp'), 0, 0, tiled=True)  11.6 us
    pallas_call x1, Pallas kernels, local(): pl.pallas_call(attention_kernel, out_shape=(piece((WL, WC, LEVELS, 2 * C)...  8.08 us
    ppermute x1, starting transfers between devices, from_diagonal(): return lax.ppermute(x, ('lon', 'lat'), pairs)  4.53 us
    unnamed x18, local copies, waits for them, and re-layouts  3.22 us
    pallas_call x1, Pallas kernels, local(): pl.pallas_call(table_kernel, out_shape=(jax.ShapeDtypeStruct((2 * HEADS,...  2.78 us
    pallas_call x1, Pallas kernels, local(): pl.pallas_call(home_kernel, out_shape=(block, block), in_specs=vmem(7), o...  1.58 us
  transfers between devices with their start and end apart: 7, of which 2 were waited for; matrix products, arithmetic and copies ran while one was open for 0% of the time, Pallas kernels for 9%

profile of v5, /device:TPU:2, one launch (start us, length us, event | category | flops | bytes accessed | tf_op | source)
XLA Modules:
  0.0 63.9 jit_solution(11458470141795923435)
XLA Ops:
  0.6 0.0 copy-start.5
  0.6 1.2 %pad_maximum_fusion = (bf16[6,6,4,384]{3,2,1,0:T(4,128)(2,1)S(1)}, bf16[6,6,4,384]{3,2,1,0:T(4,128)(2,1)S(1)}) fusion(bf16[6,12,4,192]{3,2,1,0:T(4,128)(2,1)} %bitcast.28, bf16[6,12,4,192]{3,2,1,0:T(4,128)(2,1)} %bitcast.21), kind=kLoop, calls=%fused_computation.3 | loop fusion | flops 442368 | bytes 442368 | tf_op jit(solution)/shard_map/concatenate | solution.py:452
  1.9 10.9 %collective-permute-start = (bf16[6,6,4,384]{3,2,1,0:T(4,128)(2,1)S(1)}, bf16[6,6,4,384]{3,2,1,0:T(4,128)(2,1)S(1)}, u32[]{:S(2)}, u32[]{:S(2)}) collective-permute-start(bf16[6,6,4,384]{3,2,1,0:T(4,128)(2,1)S(1)} %get-tuple-element.23), channel_id=1, source_target_pairs={{0,480},{32,0},{64,32},{96,64},{128,96},{160,128},{192,160},{224,1... | collective-permute-start | bytes 331784 | tf_op jit(solution)/shard_map/ppermute | solution.py:418
  12.8 4.5 %collective-permute-start.2 = (bf16[6,6,4,384]{3,2,1,0:T(4,128)(2,1)S(1)}, bf16[6,6,4,384]{3,2,1,0:T(4,128)(2,1)S(1)}, u32[]{:S(2)}, u32[]{:S(2)}) collective-permute-start(bf16[6,6,4,384]{3,2,1,0:T(4,128)(2,1)S(1)} %get-tuple-element.23), channel_id=1, source_target_pairs={{0,510},{2,480},{4,482},{6,484},{8,486},{10,488},{12,490},{14,492}... | collective-permute-start | bytes 331784 | tf_op jit(solution)/shard_map/ppermute | solution.py:428
  17.3 1.1 %collective-permute-start.1 = (bf16[6,6,4,384]{3,2,1,0:T(4,128)(2,1)S(1)}, bf16[6,6,4,384]{3,2,1,0:T(4,128)(2,1)S(1)}, u32[]{:S(2)}, u32[]{:S(2)}) collective-permute-start(bf16[6,6,4,384]{3,2,1,0:T(4,128)(2,1)S(1)} %get-tuple-element.24.own_ref), channel_id=1, source_target_pairs={{0,30},{2,0},{4,2},{6,4},{8,6},{10,8},{12,10},{14,12},{16,14},{18,... | collective-permute-start | bytes 331784 | tf_op jit(solution)/shard_map/ppermute | solution.py:418
  18.5 0.0 copy-start.1
  18.5 0.9 %copy-done.1 = bf16[192,576]{1,0:T(8,128)(2,1)S(1)} copy-done((bf16[192,576]{1,0:T(8,128)(2,1)S(1)}, bf16[192,576]{1,0:T(8,128)(2,1)}, u32[]{:S(2)}) %copy-start.1) | copy-done | bytes 221208
  19.4 0.0 copy-start.2
  19.4 0.9 %copy-done.2 = f32[2,1,6,3312]{3,1,2,0:T(1,128)S(1)} copy-done((f32[2,1,6,3312]{3,1,2,0:T(1,128)S(1)}, f32[2,1,6,3312]{3,1,2,0:T(1,128)}, u32[]{:S(2)}) %copy-start.2) | copy-done | bytes 159000
  20.3 0.0 copy-start.6
  20.3 0.7 %copy-done.6 = f32[192]{0:T(256)S(1)} copy-done((f32[192]{0:T(256)S(1)}, f32[192]{0:T(256)}, u32[]{:S(2)}) %copy-start.6) | copy-done | bytes 792
  21.0 0.0 copy-start.7
  21.0 0.7 %copy-done.7 = s32[2]{0:T(128)S(1)} copy-done((s32[2]{0:T(128)S(1)}, s32[2]{0:T(128)}, u32[]{:S(2)}) %copy-start.7) | copy-done | bytes 32
  21.7 2.8 %bias_table.1 = (f32[12,144,256]{2,1,0:T(8,128)S(1)}, f32[1,192]{1,0:T(1,128)S(1)}, bf16[576,192]{1,0:T(8,128)(2,1)S(1)}) custom-call(s32[2]{0:T(128)S(1)} %copy-done.7, f32[12,1,3312]{2,1,0:T(1,128)S(1)} %bitcast.23, f32[1,192]{1,0:T(1,128)S(1)} %bitcast.26, bf16[192,576]{1,0:T(8,128)(2,1)S(1)} %copy-done.1), custom_call_target="tpu_custom_call" | custom-call | flops 400000000 | bytes 2000000 | tf_op jit(solution)/shard_map/bias_table/pallas_call | solution.py:459
  24.4 0.0 collective-permute-done.east_ref
  24.4 0.0 collective-permute-done.2.diag_ref
  24.5 0.0 collective-permute-done.1.south_ref
  24.5 0.0 copy-done.5
  24.5 0.0 copy-start.8
  24.5 8.1 %window_attention.1 = (bf16[6,12,4,384]{3,2,1,0:T(4,128)(2,1)S(1)}, bf16[5,12,4,384]{3,2,1,0:T(4,128)(2,1)S(1)}, bf16[32,5,2,128]{3,2,1,0:T(2,128)(2,1)}) custom-call(s32[2]{0:T(128)S(1)} %copy-done.7, bf16[6,6,4,384]{3,2,1,0:T(4,128)(2,1)S(1)} %get-tuple-element.24.own_ref, bf16[6,6,4,384]{3,2,1,0:T(4,128)(2,1)S(1)} %collective-permute-done.east_ref, ...), custom_call_target="tpu_custom_call" | custom-call | flops 4000000000 | bytes 2000000 | tf_op jit(solution)/shard_map/window_attention/pallas_call | solution.py:481
  32.6 0.0 collective-permute-start.3
  32.6 6.6 %all-to-all-start = ((bf16[32,5,2,128]{3,2,1,0:T(2,128)(2,1)}), bf16[32,5,2,128]{3,2,1,0:T(2,128)(2,1)S(1)}, u32[]{:S(2)}, u32[]{:S(2)}) async-start(bf16[32,5,2,128]{3,2,1,0:T(2,128)(2,1)} %get-tuple-element.22), calls=%async_computation | async-start | bytes 163840 | tf_op jit(solution)/shard_map/all_to_all | solution.py:432
  39.1 0.0 collective-permute-done.3.other_ref
  39.2 0.0 copy-done.8
  39.2 0.0 copy-start
  39.2 0.0 copy-start.3
  39.2 0.0 copy-start.4
  39.2 0.6 %home_rows.1 = (bf16[6,6,4,384]{3,2,1,0:T(4,128)(2,1)S(1)}, bf16[6,6,4,384]{3,2,1,0:T(4,128)(2,1)S(1)}) custom-call(s32[2]{0:T(128)S(1)} %copy-done.8, bf16[6,12,4,384]{3,2,1,0:T(4,128)(2,1)S(1)} %get-tuple-element.16.own_ref, bf16[5,12,4,384]{3,2,1,0:T(4,128)(2,1)S(1)} %collective-permute-done.3.other_ref), custom_call_target="tpu_custom_call" | custom-call | flops 20000000000 | bytes 500000 | tf_op jit(solution)/shard_map/home_rows/pallas_call | solution.py:515
  39.9 3.4 %collective-permute-start.4 = (bf16[6,6,4,384]{3,2,1,0:T(4,128)(2,1)S(1)}, bf16[6,6,4,384]{3,2,1,0:T(4,128)(2,1)S(1)}, u32[]{:S(2)}, u32[]{:S(2)}) collective-permute-start(bf16[6,6,4,384]{3,2,1,0:T(4,128)(2,1)S(1)} %get-tuple-element.18), channel_id=1, source_target_pairs={{0,32},{32,64},{64,96},{96,128},{128,160},{160,192},{192,224},{224... | collective-permute-start | bytes 331784 | tf_op jit(solution)/shard_map/ppermute | solution.py:418
  43.2 5.0 %all-to-all-done.parts_ref = bf16[32,5,2,128]{3,2,1,0:T(2,128)(2,1)S(1)} async-done(((bf16[32,5,2,128]{3,2,1,0:T(2,128)(2,1)}), bf16[32,5,2,128]{3,2,1,0:T(2,128)(2,1)S(1)}, u32[]{:S(2)}, u32[]{:S(2)}) %all-to-all-start) | async-done | bytes 81952 | tf_op jit(solution)/shard_map/all_to_all | solution.py:432
  48.3 0.7 %table_sum.1 = bf16[32,5,2,128]{3,2,1,0:T(2,128)(2,1)} custom-call(bf16[32,5,2,128]{3,2,1,0:T(2,128)(2,1)S(1)} %all-to-all-done.parts_ref, bf16[6,6,4,384]{3,2,1,0:T(4,128)(2,1)S(1)} %get-tuple-element.19.near_ref.after_ref), custom_call_target="tpu_custom_call" | custom-call | flops 100000 | bytes 400000 | tf_op jit(solution)/shard_map/table_sum/pallas_call | solution.py:526
  49.0 5.0 %all-to-all-start.1 = ((bf16[32,5,2,128]{3,2,1,0:T(2,128)(2,1)}), bf16[32,5,2,128]{3,2,1,0:T(2,128)(2,1)S(1)}, u32[]{:S(2)}, u32[]{:S(2)}) async-start(bf16[32,5,2,128]{3,2,1,0:T(2,128)(2,1)} %table_sum.1), calls=%async_computation.1 | async-start | bytes 163840 | tf_op jit(solution)/shard_map/all_to_all | solution.py:432
  54.0 0.0 collective-permute-done.4.west_ref
  54.0 0.0 copy-done
  54.0 0.0 copy-done.3
  54.0 0.0 copy-done.4
  54.1 1.6 %home.1 = (bf16[6,12,4,192]{3,2,1,0:T(4,128)(2,1)}, bf16[6,12,4,192]{3,2,1,0:T(4,128)(2,1)}) custom-call(bf16[6,6,4,384]{3,2,1,0:T(4,128)(2,1)S(1)} %collective-permute-done.4.west_ref, bf16[6,6,4,384]{3,2,1,0:T(4,128)(2,1)S(1)} %get-tuple-element.19.near_ref.after_ref, bf16[6,12,4,192]{3,2,1,0:T(4,128)(2,1)S(1)} %bitcast.24, ...), custom_call_target="tpu_custom_call" | custom-call | flops 20000000000 | bytes 2000000 | tf_op jit(solution)/shard_map/home/pallas_call | solution.py:546
  55.6 7.5 %all-to-all-done.1.sums_ref = bf16[32,5,2,128]{3,2,1,0:T(2,128)(2,1)S(1)} async-done(((bf16[32,5,2,128]{3,2,1,0:T(2,128)(2,1)}), bf16[32,5,2,128]{3,2,1,0:T(2,128)(2,1)S(1)}, u32[]{:S(2)}, u32[]{:S(2)}) %all-to-all-start.1) | async-done | bytes 81952 | tf_op jit(solution)/shard_map/all_to_all | solution.py:432
  63.1 0.8 %table_home.1 = f32[12,1,3312]{2,1,0:T(1,128)} custom-call(bf16[32,5,2,128]{3,2,1,0:T(2,128)(2,1)S(1)} %all-to-all-done.1.sums_ref), custom_call_target="tpu_custom_call" | custom-call | flops 100000 | bytes 400000 | tf_op jit(solution)/shard_map/table_home/pallas_call | solution.py:535
Async XLA Ops:
  0.6 23.8 %copy-start.5 = (bf16[192,192]{1,0:T(8,128)(2,1)S(1)}, bf16[192,192]{1,0:T(8,128)(2,1)}, u32[]{:S(2)}) copy-start(bf16[192,192]{1,0:T(8,128)(2,1)} %w_proj_ref.3) | copy-start | bytes 221188
  1.9 22.6 %collective-permute-start = (bf16[6,6,4,384]{3,2,1,0:T(4,128)(2,1)S(1)}, bf16[6,6,4,384]{3,2,1,0:T(4,128)(2,1)S(1)}, u32[]{:S(2)}, u32[]{:S(2)}) collective-permute-start(bf16[6,6,4,384]{3,2,1,0:T(4,128)(2,1)S(1)} %get-tuple-element.23), channel_id=1, source_target_pairs={{0,480},{32,0},{64,32},{96,64},{128,96},{160,128},{192,160},{224,1... | collective-permute-start | bytes 331784 | tf_op jit(solution)/shard_map/ppermute | solution.py:418
  12.8 11.7 %collective-permute-start.2 = (bf16[6,6,4,384]{3,2,1,0:T(4,128)(2,1)S(1)}, bf16[6,6,4,384]{3,2,1,0:T(4,128)(2,1)S(1)}, u32[]{:S(2)}, u32[]{:S(2)}) collective-permute-start(bf16[6,6,4,384]{3,2,1,0:T(4,128)(2,1)S(1)} %get-tuple-element.23), channel_id=1, source_target_pairs={{0,510},{2,480},{4,482},{6,484},{8,486},{10,488},{12,490},{14,492}... | collective-permute-start | bytes 331784 | tf_op jit(solution)/shard_map/ppermute | solution.py:428
  17.3 7.1 %collective-permute-start.1 = (bf16[6,6,4,384]{3,2,1,0:T(4,128)(2,1)S(1)}, bf16[6,6,4,384]{3,2,1,0:T(4,128)(2,1)S(1)}, u32[]{:S(2)}, u32[]{:S(2)}) collective-permute-start(bf16[6,6,4,384]{3,2,1,0:T(4,128)(2,1)S(1)} %get-tuple-element.24.own_ref), channel_id=1, source_target_pairs={{0,30},{2,0},{4,2},{6,4},{8,6},{10,8},{12,10},{14,12},{16,14},{18,... | collective-permute-start | bytes 331784 | tf_op jit(solution)/shard_map/ppermute | solution.py:418
  18.5 0.9 %copy-start.1 = (bf16[192,576]{1,0:T(8,128)(2,1)S(1)}, bf16[192,576]{1,0:T(8,128)(2,1)}, u32[]{:S(2)}) copy-start(bf16[192,576]{1,0:T(8,128)(2,1)} %w_qkv_ref.1) | copy-start | bytes 663556
  19.4 0.9 %copy-start.2 = (f32[2,1,6,3312]{3,1,2,0:T(1,128)S(1)}, f32[2,1,6,3312]{3,1,2,0:T(1,128)}, u32[]{:S(2)}) copy-start(f32[2,1,6,3312]{3,1,2,0:T(1,128)} %param.17) | copy-start | bytes 476932
  20.3 0.7 %copy-start.6 = (f32[192]{0:T(256)S(1)}, f32[192]{0:T(256)}, u32[]{:S(2)}) copy-start(f32[192]{0:T(256)} %param.14) | copy-start | bytes 2308
  21.0 0.7 %copy-start.7 = (s32[2]{0:T(128)S(1)}, s32[2]{0:T(128)}, u32[]{:S(2)}) copy-start(s32[2]{0:T(128)} %shifts_ref.5) | copy-start | bytes 28
  24.5 14.7 %copy-start.8 = (s32[2]{0:T(128)S(1)}, s32[2]{0:T(128)}, u32[]{:S(2)}) copy-start(s32[2]{0:T(128)} %shifts_ref.5) | copy-start | bytes 28
  32.6 6.6 %collective-permute-start.3 = (bf16[5,12,4,384]{3,2,1,0:T(4,128)(2,1)S(1)}, bf16[5,12,4,384]{3,2,1,0:T(4,128)(2,1)S(1)}, u32[]{:S(2)}, u32[]{:S(2)}) collective-permute-start(bf16[5,12,4,384]{3,2,1,0:T(4,128)(2,1)S(1)} %get-tuple-element.17), channel_id=1, source_target_pairs={{0,2},{2,4},{4,6},{6,8},{8,10},{10,12},{12,14},{14,16},{16,18},{18... | collective-permute-start | bytes 552968 | tf_op jit(solution)/shard_map/ppermute | solution.py:418
  32.6 15.7 %all-to-all-start = ((bf16[32,5,2,128]{3,2,1,0:T(2,128)(2,1)}), bf16[32,5,2,128]{3,2,1,0:T(2,128)(2,1)S(1)}, u32[]{:S(2)}, u32[]{:S(2)}) async-start(bf16[32,5,2,128]{3,2,1,0:T(2,128)(2,1)} %get-tuple-element.22), calls=%async_computation | async-start | bytes 163840 | tf_op jit(solution)/shard_map/all_to_all | solution.py:432
  39.2 14.9 %copy-start = (bf16[1,4,6,12,192]{4,1,3,2,0:T(4,128)(2,1)S(1)}, bf16[1,4,6,12,192]{4,1,3,2,0:T(4,128)(2,1)}, u32[]{:S(2)}) copy-start(bf16[1,4,6,12,192]{4,1,3,2,0:T(4,128)(2,1)} %param.11) | copy-start | bytes 331780
  39.2 14.9 %copy-start.3 = (bf16[1,4,6,12,192]{4,1,3,2,0:T(4,128)(2,1)S(1)}, bf16[1,4,6,12,192]{4,1,3,2,0:T(4,128)(2,1)}, u32[]{:S(2)}) copy-start(bf16[1,4,6,12,192]{4,1,3,2,0:T(4,128)(2,1)} %param.10) | copy-start | bytes 331780
  39.2 14.9 %copy-start.4 = (bf16[1,4,6,12,192]{4,1,3,2,0:T(4,128)(2,1)S(1)}, bf16[1,4,6,12,192]{4,1,3,2,0:T(4,128)(2,1)}, u32[]{:S(2)}) copy-start(bf16[1,4,6,12,192]{4,1,3,2,0:T(4,128)(2,1)} %param.13) | copy-start | bytes 331780
  39.9 14.2 %collective-permute-start.4 = (bf16[6,6,4,384]{3,2,1,0:T(4,128)(2,1)S(1)}, bf16[6,6,4,384]{3,2,1,0:T(4,128)(2,1)S(1)}, u32[]{:S(2)}, u32[]{:S(2)}) collective-permute-start(bf16[6,6,4,384]{3,2,1,0:T(4,128)(2,1)S(1)} %get-tuple-element.18), channel_id=1, source_target_pairs={{0,32},{32,64},{64,96},{96,128},{128,160},{160,192},{192,224},{224... | collective-permute-start | bytes 331784 | tf_op jit(solution)/shard_map/ppermute | solution.py:418
  49.0 14.1 %all-to-all-start.1 = ((bf16[32,5,2,128]{3,2,1,0:T(2,128)(2,1)}), bf16[32,5,2,128]{3,2,1,0:T(2,128)(2,1)S(1)}, u32[]{:S(2)}, u32[]{:S(2)}) async-start(bf16[32,5,2,128]{3,2,1,0:T(2,128)(2,1)} %table_sum.1), calls=%async_computation.1 | async-start | bytes 163840 | tf_op jit(solution)/shard_map/all_to_all | solution.py:432
